TPU v7x, 512 devices: a whole 4x8x8 slice. The times are simulated.
512 devices in a mesh: req: 32 (over y_hi, z), cfg: 2 (over core), sp: 8 (over y_lo, x).
Axes of the slice: x: 4, y: 8 (y_hi: 4, y_lo: 2; y = y_hi * 2 + y_lo), z: 8, core: 2. Of those that a mesh axis runs over, the one named last changes fastest.
Arguments:
- vis_qkv: bfloat16 [2, 24576, 3, 16, 128], P('cfg', ('req', 'sp')), parts along dimension 1, may hold values from -26 to 26
- text_kv: bfloat16 [2, 8192, 2, 16, 128], P('cfg', ('req', 'sp')), parts along dimension 1, may hold values from -6 to 6
- text_len: int32 [2, 32], P('cfg', 'req'), parts along dimension 1, may hold values from 1 to 256
- vis_hidden: bfloat16 [2, 24576, 3072], P('cfg', ('req', 'sp')), parts along dimension 1, may hold values from -3 to 3
- out_weight: bfloat16 [2048, 3072], P(None, ('cfg', 'sp')), may hold values from -0.125 to 0.125
- modulation: float32 [2, 96, 3072], P('cfg', 'req'), parts along dimension 1, may hold values from -4 to 4
- final_weight: bfloat16 [3072, 48], replicated, may hold values from -0.0546875 to 0.0546875
- latent: float32 [24576, 48], P(('req', 'sp'), 'cfg'), parts along dimension 0, may hold values from -5 to 5
- timestep: int32 [32], P('req'), parts along dimension 0, may hold values from 0 to 31
Outputs:
- velocity: float32 [24576, 48], P(('req', 'sp'), 'cfg'), parts along dimension 0
- latent_next: float32 [24576, 48], P(('req', 'sp'), 'cfg'), parts along dimension 0
- denoised: float32 [24576, 48], P(('req', 'sp'), 'cfg'), parts along dimension 0
There are 32 independent parts, one for each index of `req`. A program takes and returns all parts, laid end to end along the dimension named above; an argument that names none is the same for every part. Nothing has to cross between parts.
All inputs are finite; a program needn't handle non-finite values.
Results may differ from a plain program's by a relative error of at most 0.0038.
Values may be sent and summed in bfloat16 or wider, within the bound.
No kernel may reach another device: no remote copies, remote signals or barrier semaphores. Data moves between devices by JAX's collectives and lax.ppermute only.
A program may use at most 64 MiB of HBM per device.

v0:
```python
import math

import jax
import jax.numpy as jnp
from jax import lax
from jax.sharding import PartitionSpec as P

STEPS = 64


def partner(block, axis, bit):
    count = lax.axis_size(axis)
    route = []
    for low in range(count):
        high = low | 1 << bit
        if high != low and high < count:
            route += [(low, high), (high, low)]
    return lax.ppermute(block, axis, route)


def shards(
    vis_qkv, text_kv, text_len, vis_hidden, out_weight, modulation, final_weight, latent, timestep
):
    heads_vis, heads_text = (
        lax.all_to_all(vis_qkv, "sp", split_axis=3, concat_axis=1, tiled=True),
        lax.all_to_all(text_kv, "sp", split_axis=3, concat_axis=1, tiled=True),
    )
    queries = heads_vis[0, :, 0]
    key_rows = jnp.concatenate([heads_vis[0, :, 1], heads_text[0, :, 0]], axis=0)
    value_rows = jnp.concatenate([heads_vis[0, :, 2], heads_text[0, :, 1]], axis=0)
    total_vis = queries.shape[0]
    key_valid = jnp.arange(key_rows.shape[0], dtype=jnp.int32) < total_vis + text_len[0, 0]
    block_rows = total_vis
    while block_rows > 1024 and block_rows % 2 == 0:
        block_rows = block_rows // 2
    query_blocks = queries.reshape(
        total_vis // block_rows, block_rows, queries.shape[1], queries.shape[2]
    )
    inv_scale = 1.0 / math.sqrt(queries.shape[2])

    def attend(query_rows):
        scores = (
            jnp.einsum("qhd,khd->hqk", query_rows, key_rows, preferred_element_type=jnp.float32)
            * inv_scale
        )
        scores = jnp.where(key_valid[None, None, :], scores, -1e30)
        row_peak = jnp.max(scores, axis=2, keepdims=True)
        raised = jnp.exp(scores - row_peak)
        weights = (raised / jnp.sum(raised, axis=2, keepdims=True)).astype(jnp.bfloat16)
        return jnp.einsum(
            "hqk,khd->qhd", weights, value_rows, preferred_element_type=jnp.float32
        ).astype(jnp.bfloat16)

    attended = lax.map(attend, query_blocks).reshape(total_vis, queries.shape[1], queries.shape[2])
    returned = lax.all_to_all(attended[None], "sp", split_axis=1, concat_axis=2, tiled=True)
    own_rows = returned.reshape(returned.shape[1], returned.shape[2] * returned.shape[3])
    branch = lax.axis_index("cfg")
    projected = jnp.dot(
        own_rows,
        lax.all_gather(out_weight, ("cfg", "sp"), axis=1, tiled=True),
        preferred_element_type=jnp.float32,
    )
    mods = modulation[0]
    resid = vis_hidden[0].astype(jnp.float32) + mods[0] * projected
    center = jnp.mean(resid, axis=1, keepdims=True)
    spread = jnp.mean((resid - center) * (resid - center), axis=1, keepdims=True)
    normed = (resid - center) * lax.rsqrt(spread + 1e-06)
    modulated = (normed * (1.0 + mods[1]) + mods[2]).astype(jnp.bfloat16)
    own_pred = jnp.dot(modulated, final_weight, preferred_element_type=jnp.float32)
    half_width = latent.shape[1]
    kept_cols = lax.dynamic_slice_in_dim(own_pred, branch * half_width, half_width, 1)
    sent_cols = lax.dynamic_slice_in_dim(own_pred, (1 - branch) * half_width, half_width, 1)
    other_pred = partner(sent_cols, "cfg", 0)
    cond_pred = jnp.where(branch == 0, kept_cols, other_pred)
    uncond_pred = jnp.where(branch == 0, other_pred, kept_cols)
    velocity = uncond_pred + 4.5 * (cond_pred - uncond_pred)
    step_now = timestep[0].astype(jnp.float32)
    remain_now = 1.0 - step_now / STEPS
    remain_next = 1.0 - (step_now + 1.0) / STEPS
    sigma_now = remain_now * remain_now
    sigma_next = remain_next * remain_next
    latent_next = latent + (sigma_next - sigma_now) * velocity
    denoised = latent - sigma_now * velocity
    return (velocity, latent_next, denoised)


def solution(mesh):
    return jax.shard_map(
        shards,
        mesh=mesh,
        in_specs=(
            P("cfg", ("req", "sp"), None, None, None),
            P("cfg", ("req", "sp"), None, None, None),
            P("cfg", "req"),
            P("cfg", ("req", "sp"), None),
            P(None, ("cfg", "sp")),
            P("cfg", "req", None),
            P(),
            P(("req", "sp"), "cfg"),
            P("req"),
        ),
        out_specs=(P(("req", "sp"), "cfg"), P(("req", "sp"), "cfg"), P(("req", "sp"), "cfg")),
        check_vma=False,
    )
```

profile of v0, /device:TPU:1, one launch (start us, length us, event | category | flops | bytes accessed | tf_op | source)
XLA Modules:
  0.0 126.4 jit_solution(14541745614816064769)
XLA Ops:
  7.2 0.0 copy-start
  7.2 0.0 copy-start.1
  7.2 0.0 all-gather.2.cloned.1.call-start
  7.2 0.7 all-gather.2.cloned.1.call-update
  7.9 1.8 %copy.33 = bf16[1,32,2,16,128]{4,1,2,0,3:T(8,128)(2,1)} copy(bf16[1,32,2,16,128]{4,3,2,1,0:T(8,128)(2,1)} %param.10) | data formatting | bytes 524288 | tf_op args[1]
  9.7 5.9 %all-to-all-start.1 = ((bf16[1,32,2,16,128]{4,1,2,0,3:T(8,128)(2,1)}), bf16[1,32,2,16,128]{4,1,2,0,3:T(8,128)(2,1)S(1)}, u32[]{:S(2)}, u32[]{:S(2)}) async-start(bf16[1,32,2,16,128]{4,1,2,0,3:T(8,128)(2,1)} %copy.33), calls=%async_computation.1 | async-start | bytes 524288 | tf_op jit(solution)/shard_map/all_to_all | solution.py:26
  15.5 1.4 %copy.31 = bf16[1,96,3,16,128]{4,1,2,0,3:T(8,128)(2,1)} copy(bf16[1,96,3,16,128]{4,3,2,1,0:T(8,128)(2,1)S(1)} %copy-done.1) | data formatting | bytes 2359296 | tf_op args[0]
  16.9 4.7 %all-to-all-done.1 = bf16[1,32,2,16,128]{4,1,2,0,3:T(8,128)(2,1)S(1)} async-done(((bf16[1,32,2,16,128]{4,1,2,0,3:T(8,128)(2,1)}), bf16[1,32,2,16,128]{4,1,2,0,3:T(8,128)(2,1)S(1)}, u32[]{:S(2)}, u32[]{:S(2)}) %all-to-all-start.1) | async-done | bytes 262176 | tf_op jit(solution)/shard_map/all_to_all | solution.py:26
  21.6 3.6 %all-to-all-start = ((bf16[1,96,3,16,128]{4,1,2,0,3:T(8,128)(2,1)}), bf16[1,96,3,16,128]{4,1,2,0,3:T(8,128)(2,1)S(1)}, u32[]{:S(2)}, u32[]{:S(2)}) async-start(bf16[1,96,3,16,128]{4,1,2,0,3:T(8,128)(2,1)} %copy.31), calls=%async_computation | async-start | bytes 2359296 | tf_op jit(solution)/shard_map/all_to_all | solution.py:25
  25.9 14.1 %all-to-all-done = bf16[1,96,3,16,128]{4,1,2,0,3:T(8,128)(2,1)S(1)} async-done(((bf16[1,96,3,16,128]{4,1,2,0,3:T(8,128)(2,1)}), bf16[1,96,3,16,128]{4,1,2,0,3:T(8,128)(2,1)S(1)}, u32[]{:S(2)}, u32[]{:S(2)}) %all-to-all-start) | async-done | bytes 1179680 | tf_op jit(solution)/shard_map/all_to_all | solution.py:25
  40.0 0.1 copy.32
  40.1 0.1 slice_bitcast_fusion.2
  40.2 4.7 %fusion.26 = (f32[2,768]{1,0:T(2,128)S(1)}, f32[2,768,1024]{1,2,0:T(8,128)}) fusion(pred[1024]{0:T(1024)(128)(4,1)S(1)} %iota_compare_fusion, bf16[1,768,3,2,128]{4,1,3,2,0:T(8,128)(2,1)S(1)} %bitcast.60, bf16[256,2,128]{2,0,1:T(8,128)(2,1)S(1)} %get-tuple-element.26, bf16[768,2,128]{2,0,1:T(8,128)(2,1)S(1)} %get-tuple-element.24), kind=kOutput, calls=%fused_computation.42 | convolution fusion | flops 409994240 | bytes 7216128 | tf_op jit(solution)/shard_map/while/body/eval_jaxpr/sub | solution.py:48
  44.9 3.5 %fusion.11 = bf16[1,768,2,128]{1,3,2,0:T(8,128)(2,1)S(1)} fusion(f32[2,768,1024]{1,2,0:T(8,128)} %get-tuple-element.31, f32[2,768]{1,0:T(2,128)S(1)} %get-tuple-element.30, bf16[256,2,128]{2,0,1:T(8,128)(2,1)S(1)} %get-tuple-element.25, bf16[768,2,128]{2,0,1:T(8,128)(2,1)S(1)} %get-tuple-element.17), kind=kOutput, calls=%fused_computation.14 | convolution fusion | flops 407044096 | bytes 7215104 | tf_op jit(solution)/shard_map/while/body/eval_jaxpr/hqk,khd->qhd/dot_general | solution.py:50
  48.4 0.0 copy-start.5
  48.4 1.1 copy.37
  49.5 7.0 %all-to-all-start.2 = ((bf16[1,768,2,128]{3,2,0,1:T(2,128)(2,1)}), bf16[1,768,2,128]{3,2,0,1:T(2,128)(2,1)S(1)}, u32[]{:S(2)}, u32[]{:S(2)}) async-start(bf16[1,768,2,128]{3,2,0,1:T(2,128)(2,1)} %copy.37), calls=%async_computation.2 | async-start | bytes 786432 | tf_op jit(solution)/shard_map/all_to_all | solution.py:55
  56.6 0.0 copy-start.2
  56.6 9.4 %all-to-all-done.2 = bf16[1,768,2,128]{3,2,0,1:T(2,128)(2,1)S(1)} async-done(((bf16[1,768,2,128]{3,2,0,1:T(2,128)(2,1)}), bf16[1,768,2,128]{3,2,0,1:T(2,128)(2,1)S(1)}, u32[]{:S(2)}, u32[]{:S(2)}) %all-to-all-start.2) | async-done | bytes 393248 | tf_op jit(solution)/shard_map/all_to_all | solution.py:55
  66.0 0.1 copy.38
  66.0 0.4 copy.39
  66.4 0.3 reshape.58
  66.7 39.2 %all-gather.2.cloned.1.call-done = bf16[2048,3072]{0,1:T(8,128)(2,1)} async-done(((bf16[2048,192]{0,1:T(8,128)(2,1)}), bf16[2048,3072]{0,1:T(8,128)(2,1)}) %all-gather.2.cloned.1.call-update) | async-done | bytes 12582928 | tf_op jit(solution)/shard_map/all_gather | solution.py:60
  105.9 8.7 %fusion.27 = (f32[96]{0:T(128)S(1)}, f32[96,3072]{1,0:T(8,128)S(1)}) fusion(bf16[96,2048]{1,0:T(8,128)(2,1)S(1)} %reshape.58, bf16[2048,3072]{0,1:T(8,128)(2,1)} %all-gather.2.cloned.1.call-done, f32[3072]{0:T(1024)S(1)} %bitcast.64, bf16[1,96,3072]{2,1,0:T(8,128)(2,1)S(1)} %copy-done.2), kind=kOutput, calls=%fused_computation.43 | convolution fusion | flops 1209139072 | bytes 14758272 | tf_op jit(solution)/shard_map/dot_general | solution.py:58
  114.6 0.0 copy-start.3
  114.6 0.3 multiply_reduce_fusion
  114.9 0.0 copy-done
  114.9 0.4 fusion.14
  115.3 2.2 %collective-permute-start = (f32[96,24]{0,1:T(8,128)S(1)}, f32[96,24]{0,1:T(8,128)S(1)}, u32[]{:S(2)}, u32[]{:S(2)}) collective-permute-start(f32[96,24]{0,1:T(8,128)S(1)} %constant_dynamic-slice_fusion), channel_id=1, source_target_pairs={{0,8},{8,0},{1,9},{9,1},{2,10},{10,2},{3,11},{11,3},{4,12},{12,4},... | collective-permute-start | bytes 27656 | tf_op jit(solution)/shard_map/ppermute | solution.py:18
  118.1 0.2 collective-permute-done
  118.4 0.6 multiply_subtract_fusion
  119.0 0.6 multiply_add_fusion
  (13 shorter events, 0.1 us)
Async XLA Ops:
  7.2 107.7 %copy-start = (bf16[3072,48]{0,1:T(8,128)(2,1)S(1)}, bf16[3072,48]{0,1:T(8,128)(2,1)}, u32[]{:S(2)}) copy-start(bf16[3072,48]{0,1:T(8,128)(2,1)} %param.15) | copy-start | bytes 884740
  7.2 8.4 %copy-start.1 = (bf16[1,96,3,16,128]{4,3,2,1,0:T(8,128)(2,1)S(1)}, bf16[1,96,3,16,128]{4,3,2,1,0:T(8,128)(2,1)}, u32[]{:S(2)}) copy-start(bf16[1,96,3,16,128]{4,3,2,1,0:T(8,128)(2,1)} %param.9) | copy-start | bytes 3538948
  7.2 98.7 %all-gather.2.cloned.1.call-start = ((), (), s32[]{:S(2)}) async-start(), calls=%async_computation.3 | async-start | bytes 13369344 | tf_op jit(solution)/shard_map/all_gather | solution.py:60
  9.7 11.9 %all-to-all-start.1 = ((bf16[1,32,2,16,128]{4,1,2,0,3:T(8,128)(2,1)}), bf16[1,32,2,16,128]{4,1,2,0,3:T(8,128)(2,1)S(1)}, u32[]{:S(2)}, u32[]{:S(2)}) async-start(bf16[1,32,2,16,128]{4,1,2,0,3:T(8,128)(2,1)} %copy.33), calls=%async_computation.1 | async-start | bytes 524288 | tf_op jit(solution)/shard_map/all_to_all | solution.py:26
  21.6 18.4 %all-to-all-start = ((bf16[1,96,3,16,128]{4,1,2,0,3:T(8,128)(2,1)}), bf16[1,96,3,16,128]{4,1,2,0,3:T(8,128)(2,1)S(1)}, u32[]{:S(2)}, u32[]{:S(2)}) async-start(bf16[1,96,3,16,128]{4,1,2,0,3:T(8,128)(2,1)} %copy.31), calls=%async_computation | async-start | bytes 2359296 | tf_op jit(solution)/shard_map/all_to_all | solution.py:25
  48.4 8.2 %copy-start.5 = (f32[1,3,3072]{2,0,1:T(1,128)S(1)}, f32[1,3,3072]{2,0,1:T(1,128)}, u32[]{:S(2)}) copy-start(f32[1,3,3072]{2,0,1:T(1,128)} %param.14) | copy-start | bytes 110596
  49.5 16.5 %all-to-all-start.2 = ((bf16[1,768,2,128]{3,2,0,1:T(2,128)(2,1)}), bf16[1,768,2,128]{3,2,0,1:T(2,128)(2,1)S(1)}, u32[]{:S(2)}, u32[]{:S(2)}) async-start(bf16[1,768,2,128]{3,2,0,1:T(2,128)(2,1)} %copy.37), calls=%async_computation.2 | async-start | bytes 786432 | tf_op jit(solution)/shard_map/all_to_all | solution.py:55
  56.6 49.3 %copy-start.2 = (bf16[1,96,3072]{2,1,0:T(8,128)(2,1)S(1)}, bf16[1,96,3072]{2,1,0:T(8,128)(2,1)}, u32[]{:S(2)}) copy-start(bf16[1,96,3072]{2,1,0:T(8,128)(2,1)} %param.12) | copy-start | bytes 1769476
  114.6 3.8 %copy-start.3 = (f32[96,24]{0,1:T(8,128)S(1)}, f32[96,24]{0,1:T(8,128)}, u32[]{:S(2)}) copy-start(f32[96,24]{0,1:T(8,128)} %param.16) | copy-start | bytes 27652
  115.3 3.1 %collective-permute-start = (f32[96,24]{0,1:T(8,128)S(1)}, f32[96,24]{0,1:T(8,128)S(1)}, u32[]{:S(2)}, u32[]{:S(2)}) collective-permute-start(f32[96,24]{0,1:T(8,128)S(1)} %constant_dynamic-slice_fusion), channel_id=1, source_target_pairs={{0,8},{8,0},{1,9},{9,1},{2,10},{10,2},{3,11},{11,3},{4,12},{12,4},... | collective-permute-start | bytes 27656 | tf_op jit(solution)/shard_map/ppermute | solution.py:18
  119.0 0.6 copy-start.4
Sparse Core Ops, SparseCore 0:
  10.2 95.6 all-gather.1
where the time goes:
time: 127 us; the launch traced here: 126 us
  waiting for transfers between devices  68.3 us (54%)
  starting transfers between devices  18.7 us (15%)
  matrix products  17.2 us (14%)
  between operations  15.5 us (12%)
  local copies, waits for them, and re-layouts  5.22 us (4%)
  other arithmetic  1.52 us (1%)
    all_gather x1, waiting for transfers between devices, shards(): lax.all_gather(out_weight, ('cfg', 'sp'), axis=1, tiled=True)  39.2 us
    all_to_all x1, waiting for transfers between devices, shards(): lax.all_to_all(vis_qkv, 'sp', split_axis=3, concat_axis=1, tiled=True)  14.1 us
    all_to_all x1, waiting for transfers between devices, shards(): lax.all_to_all(attended[None], 'sp', split_axis=1, concat_axis=2, tiled=T...  9.39 us
    dot_general x1, matrix products, shards(): jnp.dot(own_rows, lax.all_gather(out_weight, ('cfg', 'sp'), axis=1, tiled...  8.65 us
    all_to_all x1, starting transfers between devices, shards(): lax.all_to_all(attended[None], 'sp', split_axis=1, concat_axis=2, tiled=T...  7.04 us
    all_to_all x1, starting transfers between devices, shards(): lax.all_to_all(text_kv, 'sp', split_axis=3, concat_axis=1, tiled=True)  5.86 us
    sub x1, matrix products, attend(): raised = jnp.exp(scores - row_peak)  4.72 us
    all_to_all x1, waiting for transfers between devices, shards(): lax.all_to_all(text_kv, 'sp', split_axis=3, concat_axis=1, tiled=True)  4.69 us
  transfers between devices with their start and end apart: 5, of which 5 were waited for; matrix products, arithmetic and copies ran while one was open for 11% of the time, Pallas kernels for 0%

commit v1 on v0

v1 whole, which is shorter than its diff:
```python
import functools
import math

import jax
import jax.numpy as jnp
from jax import lax
from jax.experimental import pallas as pl
from jax.experimental.pallas import tpu as pltpu
from jax.sharding import PartitionSpec as P

STEPS = 64
VMEM = 56 << 20
NEG = -1e30
BF = jnp.bfloat16
F32 = jnp.float32
ANY = pl.BlockSpec(memory_space=pl.ANY)
WHOLE = pl.BlockSpec(memory_space=pltpu.VMEM)
SCALARS = pl.BlockSpec(memory_space=pltpu.SMEM)
NT = (((1,), (1,)), ((), ()))


def pack_kernel(vis_ref, txt_ref, o_ref, v_ref, t_ref, out_ref, in_sem, out_sem):
    vis, txt = v_ref.shape[1], t_ref.shape[1]
    loads = [
        pltpu.make_async_copy(vis_ref.at[0, :, j], v_ref.at[j], in_sem.at[j]) for j in range(3)
    ] + [
        pltpu.make_async_copy(txt_ref.at[0, :, j], t_ref.at[j], in_sem.at[3 + j]) for j in range(2)
    ]
    for load in loads:
        load.start()
    stores = []
    at = 0
    for j in range(5):
        loads[j].wait()
        block = v_ref[j] if j < 3 else t_ref[j - 3]
        rows = vis if j < 3 else txt
        out_ref[:, at : at + rows, :] = jnp.swapaxes(block, 0, 1)
        stores.append(
            pltpu.make_async_copy(
                out_ref.at[:, at : at + rows, :], o_ref.at[:, at : at + rows, :], out_sem.at[j]
            )
        )
        stores[-1].start()
        at += rows
    for store in stores:
        store.wait()


def pack(vis_qkv, text_kv):
    _, vis, _, heads, width = vis_qkv.shape
    txt = text_kv.shape[1]
    rows = 3 * vis + 2 * txt
    return pl.pallas_call(
        pack_kernel,
        in_specs=[ANY, ANY],
        out_specs=ANY,
        out_shape=jax.ShapeDtypeStruct((heads, rows, width), BF),
        scratch_shapes=[
            pltpu.VMEM((3, vis, heads, width), BF),
            pltpu.VMEM((2, txt, heads, width), BF),
            pltpu.VMEM((heads, rows, width), BF),
            pltpu.SemaphoreType.DMA((5,)),
            pltpu.SemaphoreType.DMA((5,)),
        ],
        compiler_params=pltpu.CompilerParams(vmem_limit_bytes=VMEM),
        cost_estimate=pl.CostEstimate(
            flops=0, bytes_accessed=4 * heads * rows * width, transcendentals=0
        ),
        name="pack",
    )(vis_qkv, text_kv)


def attend_kernel(len_ref, x_ref, o_ref, k_ref, v_ref):
    src = x_ref.shape[0]
    cols = src // 2
    vis = o_ref.shape[2] // cols
    txt = (x_ref.shape[2] - 3 * vis) // 2
    nv = src * vis
    keys = k_ref.shape[0]
    for i in range(src):
        k_ref[i * vis : (i + 1) * vis, :] = x_ref[i, 0, vis : 2 * vis, :]
        v_ref[i * vis : (i + 1) * vis, :] = x_ref[i, 0, 2 * vis : 3 * vis, :]
        t0 = nv + i * txt
        k_ref[t0 : t0 + txt, :] = x_ref[i, 0, 3 * vis : 3 * vis + txt, :]
        v_ref[t0 : t0 + txt, :] = x_ref[i, 0, 3 * vis + txt : 3 * vis + 2 * txt, :]
    valid = lax.broadcasted_iota(jnp.int32, (1, keys - nv), 1) < len_ref[0]
    scale = math.log2(math.e) / math.sqrt(x_ref.shape[3])
    for i in range(src):
        j = i + 1
        if i % 2:
            continue
        q = jnp.concatenate([x_ref[i, 0, 0:vis, :], x_ref[j, 0, 0:vis, :]], axis=0)
        s = lax.dot_general(q, k_ref[...], NT, preferred_element_type=F32)
        s = jnp.concatenate([s[:, :nv], jnp.where(valid, s[:, nv:], NEG)], axis=1)
        e = jnp.exp2((s - jnp.max(s, axis=1, keepdims=True)) * scale)
        w = (e * (1.0 / jnp.sum(e, axis=1, keepdims=True))).astype(BF)
        o = jnp.dot(w, v_ref[...], preferred_element_type=F32).astype(BF)
        row, at = i // cols, i % cols
        for d in range(row * cols, (row + 1) * cols):
            o_ref[d, 0, at * vis : (at + 2) * vis] = o


def attend(length, x, vis):
    src, heads, rows, width = x.shape
    txt = (rows - 3 * vis) // 2
    keys = src * (vis + txt)
    return pl.pallas_call(
        attend_kernel,
        grid=(heads,),
        in_specs=[SCALARS, pl.BlockSpec((src, 1, rows, width), lambda h: (0, h, 0, 0))],
        out_specs=pl.BlockSpec((src, 1, src // 2 * vis, width), lambda h: (0, h, 0, 0)),
        out_shape=jax.ShapeDtypeStruct((src, heads, src // 2 * vis, width), BF),
        scratch_shapes=[pltpu.VMEM((keys, width), BF), pltpu.VMEM((keys, width), BF)],
        compiler_params=pltpu.CompilerParams(vmem_limit_bytes=VMEM),
        cost_estimate=pl.CostEstimate(
            flops=4 * heads * src * vis * keys * width,
            bytes_accessed=2 * x.size + 4 * heads * src * vis * width,
            transcendentals=heads * src * vis * keys,
        ),
        name="attend",
    )(length, x)


def split2(x):
    hi = x.astype(BF)
    return hi, (x - hi.astype(F32)).astype(BF)


def prepare_kernel(spot_ref, hid_hbm, mod_hbm, fin_hbm, send_hbm, tab_hbm, *refs):
    hid_ref, mod_ref, fin_ref, send_ref, tab_ref, sem = refs
    loads = [
        pltpu.make_async_copy(hid_hbm.at[0], hid_ref, sem.at[0]),
        pltpu.make_async_copy(mod_hbm.at[0], mod_ref, sem.at[1]),
        pltpu.make_async_copy(fin_hbm, fin_ref, sem.at[2]),
    ]
    for load in loads:
        load.start()
    for load in loads:
        load.wait()
    part = send_ref.shape[2] // 4
    patch = fin_ref.shape[0]
    core, row, col = spot_ref[0], spot_ref[1], spot_ref[2]
    windows = []
    for g in range(4):
        c = core if g < 2 else 1 - core
        r = row if g % 2 == 0 else 1 - row
        windows.append(pl.ds(pl.multiple_of((2 * c + r) * (4 * part), 128), 4 * part))
    for g in range(4):
        hid = hid_ref[:, windows[g]]
        for there in range(4):
            at = slice(there * part, (there + 1) * part)
            send_ref[there, :, g * part : (g + 1) * part] = hid[:, at]
    send = pltpu.make_async_copy(send_ref, send_hbm, sem.at[0])
    send.start()
    for me in range(4):

        @pl.when(col == me)
        def _():
            own = slice(me * part, (me + 1) * part)
            total, shift = 0.0, 0.0
            for g in range(4):
                f = fin_ref[:, windows[g]].astype(F32)[:, own]
                scaled = f * (1.0 + mod_ref[1:2, windows[g]][:, own])
                total = total + jnp.sum(scaled, axis=1, keepdims=True)
                moved = f * mod_ref[2:3, windows[g]][:, own]
                shift = shift + jnp.sum(moved, axis=1, keepdims=True)
                tab_ref[g, :patch, :part] = scaled
                gate = mod_ref[0:1, windows[g]][:, own]
                tab_ref[g, patch:, :part] = jnp.broadcast_to(gate, (8, part))
            lane = lax.broadcasted_iota(jnp.int32, (patch, 64), 1)
            tab_ref[0, :patch, part:] = jnp.where(lane == 0, total, shift)

    table = pltpu.make_async_copy(tab_ref, tab_hbm, sem.at[1])
    table.start()
    send.wait()
    table.wait()


def prepare(spot, hidden, modulation, final_t):
    _, vis, width = hidden.shape
    patch = final_t.shape[0]
    part = width // 16
    send, table = (4, vis, 4 * part), (4, patch + 8, part + 64)
    return pl.pallas_call(
        prepare_kernel,
        in_specs=[SCALARS, ANY, ANY, ANY],
        out_specs=[ANY, ANY],
        out_shape=[jax.ShapeDtypeStruct(send, BF), jax.ShapeDtypeStruct(table, F32)],
        scratch_shapes=[
            pltpu.VMEM((vis, width), BF),
            pltpu.VMEM(modulation.shape[1:], F32),
            pltpu.VMEM(final_t.shape, BF),
            pltpu.VMEM(send, BF),
            pltpu.VMEM(table, F32),
            pltpu.SemaphoreType.DMA((3,)),
        ],
        compiler_params=pltpu.CompilerParams(vmem_limit_bytes=VMEM),
        name="prepare",
    )(spot, hidden, modulation, final_t)


def project_kernel(a_ref, *refs):
    w_hbm, (got_hbm, tab_hbm, o_ref) = refs[:4], refs[4:7]
    w_ref, got_ref, tab_ref, lhs_ref, r_ref, sem = refs[7:]
    chunks, tokens, depth = a_ref.shape
    vis = tokens // 4
    part = r_ref.shape[2]
    patch = tab_ref.shape[1] - 8
    loads = [pltpu.make_async_copy(w_hbm[g], w_ref.at[g], sem.at[g]) for g in range(4)]
    loads.append(pltpu.make_async_copy(got_hbm, got_ref, sem.at[4]))
    loads.append(pltpu.make_async_copy(tab_hbm, tab_ref, sem.at[5]))
    for i in (0, 4, 5, 1, 2, 3):
        loads[i].start()
    for i in range(chunks):
        lhs_ref[:, i * depth : (i + 1) * depth] = a_ref[i]
    total = 0.0
    for g in range(4):
        loads[g].wait()
        p = lax.dot_general(lhs_ref[...], w_ref[g], NT, preferred_element_type=F32)
        if g == 0:
            loads[4].wait()
            loads[5].wait()
        h = jnp.concatenate([got_ref[k, :, g * part : (g + 1) * part] for k in range(4)], axis=0)
        r = h.astype(F32) + tab_ref[g, patch : patch + 1, :part] * p
        r_ref[g] = r
        total = total + jnp.sum(r, axis=1, keepdims=True)
    mean = total * (1.0 / (4 * part))
    spread = 0.0
    pred = jnp.zeros((patch, tokens), F32)
    for g in range(4):
        d = r_ref[g] - mean
        spread = spread + jnp.sum(d * d, axis=1, keepdims=True)
        hi, lo = split2(d)
        w_hi, w_lo = split2(tab_ref[g, :patch, :part])
        pred = pred + lax.dot_general(w_hi, hi, NT, preferred_element_type=F32)
        pred = pred + lax.dot_general(w_hi, lo, NT, preferred_element_type=F32)
        pred = pred + lax.dot_general(w_lo, hi, NT, preferred_element_type=F32)
    lane = lax.broadcasted_iota(jnp.int32, (tokens, 128), 1)
    stats = jnp.transpose(jnp.where(lane == 0, mean, spread))[:8]
    sums = tab_ref[0, :patch, part : part + 32]
    half = patch // 2
    for c in range(2):
        for k in range(4):
            at = slice(k * vis, (k + 1) * vis)
            rows = slice(c * half, (c + 1) * half)
            o_ref[c * 4 + k, :half] = jnp.concatenate([pred[rows, at], sums[rows]], axis=1)
            o_ref[c * 4 + k, half:] = jnp.concatenate([stats[:, at], stats[:, :32]], axis=1)


def project(att, blocks, got, table):
    chunks, tokens, width = att.shape
    cols, depth = blocks[0].shape
    patch = table.shape[1] - 8
    return pl.pallas_call(
        project_kernel,
        in_specs=[WHOLE] + [ANY] * 6,
        out_specs=WHOLE,
        out_shape=jax.ShapeDtypeStruct((8, patch // 2 + 8, 128), F32),
        scratch_shapes=[
            pltpu.VMEM((4, cols, depth), BF),
            pltpu.VMEM(got.shape, BF),
            pltpu.VMEM(table.shape, F32),
            pltpu.VMEM((tokens, depth), BF),
            pltpu.VMEM((4, tokens, cols), F32),
            pltpu.SemaphoreType.DMA((6,)),
        ],
        compiler_params=pltpu.CompilerParams(vmem_limit_bytes=VMEM),
        cost_estimate=pl.CostEstimate(
            flops=8 * cols * depth * tokens,
            bytes_accessed=8 * cols * depth,
            transcendentals=0,
        ),
        name="project",
    )(att, *blocks, got, table)


def update_kernel(step_ref, x_ref, lat_ref, vel_ref, next_ref, den_ref, *, count):
    half, vis = lat_ref.shape
    preds = []
    for b in range(2):
        parts = [x_ref[b * 4 + k] for k in range(4)]
        means = [t[half : half + 1, :vis] for t in parts]
        mean = 0.25 * (means[0] + means[1] + means[2] + means[3])
        spread, linear, shift = 0.0, 0.0, 0.0
        for k in range(4):
            off = means[k] - mean
            spread = spread + parts[k][half + 1 : half + 2, :vis] + (0.25 * count) * (off * off)
            linear = linear + parts[k][:half, :vis] + parts[k][:half, vis : vis + 1] * off
            shift = shift + parts[k][:half, vis + 1 : vis + 2]
        preds.append(linear * lax.rsqrt(spread * (1.0 / count) + 1e-06) + shift)
    cond, uncond = preds
    velocity = uncond + 4.5 * (cond - uncond)
    step_now = step_ref[0].astype(F32)
    remain_now = 1.0 - step_now * (1.0 / STEPS)
    remain_next = 1.0 - (step_now + 1.0) * (1.0 / STEPS)
    sigma_now = remain_now * remain_now
    sigma_next = remain_next * remain_next
    latent = lat_ref[...]
    vel_ref[...] = velocity
    next_ref[...] = latent + (sigma_next - sigma_now) * velocity
    den_ref[...] = latent - sigma_now * velocity


def update(timestep, parts, latent, count):
    return pl.pallas_call(
        functools.partial(update_kernel, count=count),
        in_specs=[SCALARS, WHOLE, WHOLE],
        out_specs=[WHOLE] * 3,
        out_shape=[jax.ShapeDtypeStruct(latent.shape, F32)] * 3,
        name="update",
    )(timestep, parts, latent)


def across_outer(reqs):
    deep = 8
    if reqs % deep:
        return None
    high = reqs // deep
    pairs = []
    for r in range(reqs):
        for s in range(8):
            y = 2 * (r // deep) + s // 4
            near = (y + 1 if y % 2 else y - 1) % (2 * high)
            pairs.append((r * 8 + s, (near // 2 * deep + r % deep) * 8 + near % 2 * 4 + s % 4))
    return pairs


def shards(
    vis_qkv, text_kv, text_len, vis_hidden, out_weight, modulation, final_weight, latent, timestep
):
    vis, txt = vis_qkv.shape[1], text_kv.shape[1]
    spot = jnp.stack([lax.axis_index(a) for a in ("cfg", "row", "col")])
    cores = [(0, 1), (1, 0)]
    outer = across_outer(lax.axis_size("req"))

    own = out_weight.T

    def across(block):
        if outer is None:
            return lax.ppermute(block, "row", cores)
        return lax.ppermute(block, ("req", "row", "col"), outer)

    far = across(own)
    own_other = lax.ppermute(own, "cfg", cores)
    packed, spot = lax.optimization_barrier((pack(vis_qkv, text_kv), spot))
    heads = lax.all_to_all(
        packed, ("row", "col"), split_axis=0, concat_axis=0, tiled=True
    ).reshape(8, 2, 3 * vis + 2 * txt, 128)
    send, table = prepare(spot, vis_hidden, modulation, final_weight.T)
    heads, own_other, send = lax.optimization_barrier((heads, own_other, send))
    got = lax.all_to_all(send, "col", split_axis=0, concat_axis=0, tiled=True)
    attended = attend(text_len[0], heads, vis)
    attended, far, got = lax.optimization_barrier((attended, far, got))
    far_other = lax.ppermute(far, "cfg", cores)
    att = lax.all_to_all(
        attended, ("row", "col"), split_axis=0, concat_axis=0, tiled=True
    ).reshape(16, 4 * vis, 128)
    parts = project(att, [own, far, own_other, far_other], got, table)
    parts = lax.all_to_all(parts, ("cfg", "col"), split_axis=0, concat_axis=0, tiled=True)
    outs = update(timestep, parts, latent.T, vis_hidden.shape[2])
    return tuple(o.T for o in outs)


def solution(mesh):
    req, cfg, sp = mesh.devices.shape
    fine = jax.sharding.Mesh(
        mesh.devices.reshape(req, cfg, 2, sp // 2), ("req", "cfg", "row", "col")
    )
    tokens = ("req", "row", "col")
    out = P(tokens, "cfg")
    return jax.shard_map(
        shards,
        mesh=fine,
        in_specs=(
            P("cfg", tokens, None, None, None),
            P("cfg", tokens, None, None, None),
            P("cfg", "req"),
            P("cfg", tokens, None),
            P(None, ("cfg", "row", "col")),
            P("cfg", "req", None),
            P(),
            out,
            P("req"),
        ),
        out_specs=(out, out, out),
        check_vma=False,
    )
```

time: 127 us -> 88 us (0.69)
  waiting for transfers between devices: 68.3 us -> 23.9 us
  Pallas kernels: 0 us -> 22.5 us
  matrix products: 17.2 us -> 0 us
  starting transfers between devices: 18.7 us -> 35.1 us
  between operations: 15.5 us -> 2.03 us
  local copies, waits for them, and re-layouts: 5.22 us -> 3.3 us
    all_gather x1 -> x0, waiting for transfers between devices: 39.2 us -> none  [shards(): lax.all_gather(out_weight, ('cfg', 'sp'), axis=1, tiled=True)]
    pallas_call x0 -> x5, Pallas kernels: none -> 22.5 us  [the longest x1 8.83 us: project(): pl.pallas_call(project_kernel, in_specs=[WHOLE] + [ANY] * 6, out_specs=WH...]
    dot_general x3 -> x0, matrix products: 12.5 us -> none  [the longest x1 8.65 us: shards(): jnp.dot(own_rows, lax.all_gather(out_weight, ('cfg', 'sp'), axis=1, tiled...]
    ppermute x1 -> x3, starting transfers between devices: 2.16 us -> 12.4 us  [the longest x1 6.51 us: shards(): own_other = lax.ppermute(own, 'cfg', cores)]
    all_to_all x3 -> x4, waiting for transfers between devices: 28.2 us -> 21 us  [the longest x1 14.3 us: shards(): lax.all_to_all(attended, ('row', 'col'), split_axis=0, concat_axis=0, til...]
    all_to_all x3 -> x4, starting transfers between devices: 16.5 us -> 22.7 us  [the longest x1 6.49 us: shards(): got = lax.all_to_all(send, 'col', split_axis=0, concat_axis=0, tiled=True)]
    sub x1 -> x0, matrix products: 4.72 us -> none  [attend(): raised = jnp.exp(scores - row_peak)]
    ppermute x1 -> x3, waiting for transfers between devices: 0.24 us -> 2.92 us  [the longest x1 2.1 us: shards(): far_other = lax.ppermute(far, 'cfg', cores)]
  transfers between devices with their start and end apart: 5 -> 7, of which waited for: 5 -> 5; matrix products, arithmetic and copies ran while one was open for 11% -> 1% of each run, Pallas kernels for 0% -> 11%
where the time goes in v1:
time: 88 us; the launch traced here: 87.4 us
  starting transfers between devices  35.1 us (40%)
  waiting for transfers between devices  23.9 us (27%)
  Pallas kernels  22.5 us (26%)
  local copies, waits for them, and re-layouts  3.3 us (4%)
  between operations  2.03 us (2%)
    all_to_all x1, waiting for transfers between devices, shards(): lax.all_to_all(attended, ('row', 'col'), split_axis=0, concat_axis=0, til...  14.3 us
    pallas_call x1, Pallas kernels, project(): pl.pallas_call(project_kernel, in_specs=[WHOLE] + [ANY] * 6, out_specs=WH...  8.83 us
    pallas_call x1, Pallas kernels, attend(): pl.pallas_call(attend_kernel, grid=(heads,), in_specs=[SCALARS, pl.BlockS...  6.56 us
    ppermute x1, starting transfers between devices, shards(): own_other = lax.ppermute(own, 'cfg', cores)  6.51 us
    all_to_all x1, starting transfers between devices, shards(): got = lax.all_to_all(send, 'col', split_axis=0, concat_axis=0, tiled=True)  6.49 us
    all_to_all x1, starting transfers between devices, shards(): lax.all_to_all(packed, ('row', 'col'), split_axis=0, concat_axis=0, tiled...  5.99 us
    all_to_all x1, starting transfers between devices, shards(): lax.all_to_all(attended, ('row', 'col'), split_axis=0, concat_axis=0, til...  5.94 us
    all_to_all x1, waiting for transfers between devices, shards(): lax.all_to_all(parts, ('cfg', 'col'), split_axis=0, concat_axis=0, tiled=...  4.51 us
  transfers between devices with their start and end apart: 7, of which 5 were waited for; matrix products, arithmetic and copies ran while one was open for 1% of the time, Pallas kernels for 11%

profile of v1, /device:TPU:1, one launch (start us, length us, event | category | flops | bytes accessed | tf_op | source)
XLA Modules:
  0.0 87.4 jit_solution(4698448701257360174)
XLA Ops:
  0.6 2.4 %pack.1 = bf16[16,352,128]{2,1,0:T(8,128)(2,1)} custom-call(bf16[1,96,3,16,128]{4,3,2,1,0:T(8,128)(2,1)} %vis_ref.1, bf16[1,32,2,16,128]{4,3,2,1,0:T(8,128)(2,1)} %txt_ref.1), custom_call_target="tpu_custom_call" | custom-call | bytes 2883584 | tf_op jit(solution)/shard_map/pack/pallas_call | solution.py:53
  3.0 0.6 pad_add_fusion.spot_ref
  3.6 0.0 copy-start.3
  3.6 0.0 copy-start.6
  3.6 6.0 %all-to-all-start = ((bf16[16,352,128]{2,1,0:T(8,128)(2,1)}), bf16[16,352,128]{2,1,0:T(8,128)(2,1)S(1)}, u32[]{:S(2)}, u32[]{:S(2)}) async-start(bf16[16,352,128]{2,1,0:T(8,128)(2,1)} %pack.1), calls=%async_computation | async-start | bytes 2883584 | tf_op jit(solution)/shard_map/all_to_all | solution.py:346
  9.6 0.0 copy-done.3
  9.6 6.5 %collective-permute-start = (bf16[192,2048]{1,0:T(8,128)(2,1)S(1)}, bf16[192,2048]{1,0:T(8,128)(2,1)}, u32[]{:S(2)}, u32[]{:S(2)}) collective-permute-start(bf16[192,2048]{1,0:T(8,128)(2,1)S(1)} %bitcast.16), channel_id=1, source_target_pairs={{0,8},{8,0},{1,9},{9,1},{2,10},{10,2},{3,11},{11,3},{4,12},{12,4},... | collective-permute-start | bytes 2359304 | tf_op jit(solution)/shard_map/ppermute | solution.py:344
  16.1 1.9 %collective-permute-start.1 = (bf16[192,2048]{1,0:T(8,128)(2,1)S(1)}, bf16[192,2048]{1,0:T(8,128)(2,1)}, u32[]{:S(2)}, u32[]{:S(2)}) collective-permute-start(bf16[192,2048]{1,0:T(8,128)(2,1)S(1)} %bitcast.17), channel_id=1, source_target_pairs={{0,388},{1,389},{2,390},{3,391},{4,128},{5,129},{6,130},{7,131},{1... | collective-permute-start | bytes 2359304 | tf_op jit(solution)/shard_map/ppermute | solution.py:341
  18.1 0.0 copy-done.6
  18.1 0.6 copy.12.mod_hbm
  18.7 3.1 %prepare.1 = (bf16[4,96,768]{2,1,0:T(8,128)(2,1)}, f32[4,56,256]{2,1,0:T(8,128)}) custom-call(s32[3]{0:T(128)} %pad_add_fusion.spot_ref, bf16[1,96,3072]{2,1,0:T(8,128)(2,1)} %hid_hbm.1, f32[1,3,3072]{2,1,0:T(4,128)} %copy.12.mod_hbm, bf16[48,3072]{1,0:T(8,128)(2,1)} %bitcast.18), custom_call_target="tpu_custom_call" | custom-call | tf_op jit(solution)/shard_map/prepare/pallas_call | solution.py:184
  21.8 0.0 collective-permute-done.refs_2_
  21.8 2.1 %all-to-all-done = bf16[16,352,128]{2,1,0:T(8,128)(2,1)S(1)} async-done(((bf16[16,352,128]{2,1,0:T(8,128)(2,1)}), bf16[16,352,128]{2,1,0:T(8,128)(2,1)S(1)}, u32[]{:S(2)}, u32[]{:S(2)}) %all-to-all-start) | async-done | bytes 1441824 | tf_op jit(solution)/shard_map/all_to_all | solution.py:346
  24.0 6.5 %all-to-all-start.1 = ((bf16[4,96,768]{2,1,0:T(8,128)(2,1)}), bf16[4,96,768]{2,1,0:T(8,128)(2,1)S(1)}, u32[]{:S(2)}, u32[]{:S(2)}) async-start(bf16[4,96,768]{2,1,0:T(8,128)(2,1)} %get-tuple-element.20), calls=%async_computation.1 | async-start | bytes 1179648 | tf_op jit(solution)/shard_map/all_to_all | solution.py:351
  31.1 0.0 copy-done.1
  31.1 6.6 %attend.1 = bf16[8,2,384,128]{3,2,1,0:T(8,128)(2,1)} custom-call(s32[1]{0:T(128)} %bitcast.12.len_ref, bf16[8,2,352,128]{3,2,1,0:T(8,128)(2,1)} %bitcast.14), custom_call_target="tpu_custom_call" | custom-call | flops 805306368 | bytes 2228224 | tf_op jit(solution)/shard_map/attend/pallas_call | solution.py:107
  37.7 0.8 collective-permute-done.1.refs_1_
  38.5 0.0 all-to-all-done.1.refs_4_
  38.5 0.0 copy-start.2
  38.5 0.8 copy-done.2
  39.3 5.9 %all-to-all-start.2 = ((bf16[8,2,384,128]{3,2,1,0:T(8,128)(2,1)}), bf16[8,2,384,128]{3,2,1,0:T(8,128)(2,1)S(1)}, u32[]{:S(2)}, u32[]{:S(2)}) async-start(bf16[8,2,384,128]{3,2,1,0:T(8,128)(2,1)} %attend.1), calls=%async_computation.2 | async-start | bytes 3145728 | tf_op jit(solution)/shard_map/all_to_all | solution.py:355
  45.3 4.0 %collective-permute-start.2 = (bf16[192,2048]{1,0:T(8,128)(2,1)}, bf16[192,2048]{1,0:T(8,128)(2,1)S(1)}, u32[]{:S(2)}, u32[]{:S(2)}) collective-permute-start(bf16[192,2048]{1,0:T(8,128)(2,1)} %collective-permute-done.1.refs_1_), channel_id=1, source_target_pairs={{0,8},{8,0},{1,9},{9,1},{2,10},{10,2},{3,11},{11,3},{4,12},{12,4},... | collective-permute-start | bytes 2359304 | tf_op jit(solution)/shard_map/ppermute | solution.py:354
  49.3 2.1 %collective-permute-done.2.refs_3_ = bf16[192,2048]{1,0:T(8,128)(2,1)S(1)} collective-permute-done((bf16[192,2048]{1,0:T(8,128)(2,1)}, bf16[192,2048]{1,0:T(8,128)(2,1)S(1)}, u32[]{:S(2)}, u32[]{:S(2)}) %collective-permute-start.2) | collective-permute-done | bytes 786464 | tf_op jit(solution)/shard_map/ppermute | solution.py:354
  51.4 0.0 copy-start.4
  51.4 14.3 %all-to-all-done.2 = bf16[8,2,384,128]{3,2,1,0:T(8,128)(2,1)S(1)} async-done(((bf16[8,2,384,128]{3,2,1,0:T(8,128)(2,1)}), bf16[8,2,384,128]{3,2,1,0:T(8,128)(2,1)S(1)}, u32[]{:S(2)}, u32[]{:S(2)}) %all-to-all-start.2) | async-done | bytes 1572896 | tf_op jit(solution)/shard_map/all_to_all | solution.py:355
  65.7 0.0 copy-done.4
  65.7 1.2 %copy-done = bf16[8,2,384,128]{3,2,1,0:T(8,128)(2,1)} copy-done((bf16[8,2,384,128]{3,2,1,0:T(8,128)(2,1)}, bf16[8,2,384,128]{3,2,1,0:T(8,128)(2,1)S(1)}, u32[]{:S(2)}) %copy-start) | copy-done | bytes 1572888
  66.9 8.8 %project.1 = f32[8,32,128]{2,1,0:T(8,128)} custom-call(bf16[16,384,128]{2,1,0:T(8,128)(2,1)} %bitcast.13, bf16[192,2048]{1,0:T(8,128)(2,1)} %bitcast.15, bf16[192,2048]{1,0:T(8,128)(2,1)} %collective-permute-done.1.refs_1_, bf16[192,2048]{1,0:T(8,128)(2,1)} %collective-permute-done.refs_2_, bf16[192,2048]{1,0:T(8,128)(2,1)} %copy-done.4, ...), custom_call_target="tpu_custom_call" | custom-call | flops 1207959552 | bytes 3145728 | tf_op jit(solution)/shard_map/project/pallas_call | solution.py:254
  75.7 4.2 %all-to-all-start.3 = ((f32[8,32,128]{2,1,0:T(8,128)}), f32[8,32,128]{2,1,0:T(8,128)S(1)}, u32[]{:S(2)}, u32[]{:S(2)}) async-start(f32[8,32,128]{2,1,0:T(8,128)} %project.1), calls=%async_computation.3 | async-start | bytes 262144 | tf_op jit(solution)/shard_map/all_to_all | solution.py:359
  80.6 4.5 %all-to-all-done.3.x_ref = f32[8,32,128]{2,1,0:T(8,128)S(1)} async-done(((f32[8,32,128]{2,1,0:T(8,128)}), f32[8,32,128]{2,1,0:T(8,128)S(1)}, u32[]{:S(2)}, u32[]{:S(2)}) %all-to-all-start.3) | async-done | bytes 131104 | tf_op jit(solution)/shard_map/all_to_all | solution.py:359
  85.1 0.7 copy-done.5
  85.8 1.6 %update.1 = (f32[24,96]{1,0:T(8,128)}, f32[24,96]{1,0:T(8,128)}, f32[24,96]{1,0:T(8,128)}) custom-call(s32[1]{0:T(128)S(6)} %copy.14.step_ref, f32[8,32,128]{2,1,0:T(8,128)} %copy-done.5, f32[24,96]{1,0:T(8,128)} %bitcast.19), custom_call_target="tpu_custom_call" | custom-call | tf_op jit(solution)/shard_map/update/pallas_call | solution.py:305
  (3 shorter events, 0.0 us)
Async XLA Ops:
  3.6 6.0 %copy-start.3 = (bf16[2048,192]{0,1:T(8,128)(2,1)S(1)}, bf16[2048,192]{0,1:T(8,128)(2,1)}, u32[]{:S(2)}) copy-start(bf16[2048,192]{0,1:T(8,128)(2,1)} %param.13) | copy-start | bytes 2359300
  3.6 14.5 %copy-start.6 = (f32[1,3,3072]{2,0,1:T(1,128)S(1)}, f32[1,3,3072]{2,0,1:T(1,128)}, u32[]{:S(2)}) copy-start(f32[1,3,3072]{2,0,1:T(1,128)} %param.14) | copy-start | bytes 110596
  3.6 20.4 %all-to-all-start = ((bf16[16,352,128]{2,1,0:T(8,128)(2,1)}), bf16[16,352,128]{2,1,0:T(8,128)(2,1)S(1)}, u32[]{:S(2)}, u32[]{:S(2)}) async-start(bf16[16,352,128]{2,1,0:T(8,128)(2,1)} %pack.1), calls=%async_computation | async-start | bytes 2883584 | tf_op jit(solution)/shard_map/all_to_all | solution.py:346
  9.6 12.2 %collective-permute-start = (bf16[192,2048]{1,0:T(8,128)(2,1)S(1)}, bf16[192,2048]{1,0:T(8,128)(2,1)}, u32[]{:S(2)}, u32[]{:S(2)}) collective-permute-start(bf16[192,2048]{1,0:T(8,128)(2,1)S(1)} %bitcast.16), channel_id=1, source_target_pairs={{0,8},{8,0},{1,9},{9,1},{2,10},{10,2},{3,11},{11,3},{4,12},{12,4},... | collective-permute-start | bytes 2359304 | tf_op jit(solution)/shard_map/ppermute | solution.py:344
  16.1 22.4 %collective-permute-start.1 = (bf16[192,2048]{1,0:T(8,128)(2,1)S(1)}, bf16[192,2048]{1,0:T(8,128)(2,1)}, u32[]{:S(2)}, u32[]{:S(2)}) collective-permute-start(bf16[192,2048]{1,0:T(8,128)(2,1)S(1)} %bitcast.17), channel_id=1, source_target_pairs={{0,388},{1,389},{2,390},{3,391},{4,128},{5,129},{6,130},{7,131},{1... | collective-permute-start | bytes 2359304 | tf_op jit(solution)/shard_map/ppermute | solution.py:341
  24.0 7.1 %copy-start.1 = (bf16[16,352,128]{2,1,0:T(8,128)(2,1)}, bf16[16,352,128]{2,1,0:T(8,128)(2,1)S(1)}, u32[]{:S(2)}) copy-start(bf16[16,352,128]{2,1,0:T(8,128)(2,1)S(1)} %all-to-all-done) | copy-start | bytes 4325380
  24.0 14.5 %all-to-all-start.1 = ((bf16[4,96,768]{2,1,0:T(8,128)(2,1)}), bf16[4,96,768]{2,1,0:T(8,128)(2,1)S(1)}, u32[]{:S(2)}, u32[]{:S(2)}) async-start(bf16[4,96,768]{2,1,0:T(8,128)(2,1)} %get-tuple-element.20), calls=%async_computation.1 | async-start | bytes 1179648 | tf_op jit(solution)/shard_map/all_to_all | solution.py:351
  38.5 0.8 copy-start.2
  39.3 26.4 %all-to-all-start.2 = ((bf16[8,2,384,128]{3,2,1,0:T(8,128)(2,1)}), bf16[8,2,384,128]{3,2,1,0:T(8,128)(2,1)S(1)}, u32[]{:S(2)}, u32[]{:S(2)}) async-start(bf16[8,2,384,128]{3,2,1,0:T(8,128)(2,1)} %attend.1), calls=%async_computation.2 | async-start | bytes 3145728 | tf_op jit(solution)/shard_map/all_to_all | solution.py:355
  45.3 6.1 %collective-permute-start.2 = (bf16[192,2048]{1,0:T(8,128)(2,1)}, bf16[192,2048]{1,0:T(8,128)(2,1)S(1)}, u32[]{:S(2)}, u32[]{:S(2)}) collective-permute-start(bf16[192,2048]{1,0:T(8,128)(2,1)} %collective-permute-done.1.refs_1_), channel_id=1, source_target_pairs={{0,8},{8,0},{1,9},{9,1},{2,10},{10,2},{3,11},{11,3},{4,12},{12,4},... | collective-permute-start | bytes 2359304 | tf_op jit(solution)/shard_map/ppermute | solution.py:354
  51.4 14.3 %copy-start.4 = (bf16[192,2048]{1,0:T(8,128)(2,1)}, bf16[192,2048]{1,0:T(8,128)(2,1)S(1)}, u32[]{:S(2)}) copy-start(bf16[192,2048]{1,0:T(8,128)(2,1)S(1)} %collective-permute-done.2.refs_3_) | copy-start | bytes 2359300
  65.7 1.2 %copy-start = (bf16[8,2,384,128]{3,2,1,0:T(8,128)(2,1)}, bf16[8,2,384,128]{3,2,1,0:T(8,128)(2,1)S(1)}, u32[]{:S(2)}) copy-start(bf16[8,2,384,128]{3,2,1,0:T(8,128)(2,1)S(1)} %all-to-all-done.2) | copy-start | bytes 4718596
  75.7 9.4 %all-to-all-start.3 = ((f32[8,32,128]{2,1,0:T(8,128)}), f32[8,32,128]{2,1,0:T(8,128)S(1)}, u32[]{:S(2)}, u32[]{:S(2)}) async-start(f32[8,32,128]{2,1,0:T(8,128)} %project.1), calls=%async_computation.3 | async-start | bytes 262144 | tf_op jit(solution)/shard_map/all_to_all | solution.py:359
  85.1 0.7 copy-start.5

commit v2 on v1

v2 whole, which is shorter than its diff:
```python
import functools
import math

import jax
import jax.numpy as jnp
from jax import lax
from jax.experimental import pallas as pl
from jax.experimental.pallas import tpu as pltpu
from jax.sharding import PartitionSpec as P

STEPS = 64
SMALL = 16 << 20
LARGE = 56 << 20
MOST = 51 << 20
NEG = -1e30
BF = jnp.bfloat16
F32 = jnp.float32
ANY = pl.BlockSpec(memory_space=pltpu.HBM)
WHOLE = pl.BlockSpec(memory_space=pltpu.VMEM)
SCALARS = pl.BlockSpec(memory_space=pltpu.SMEM)
NT = (((1,), (1,)), ((), ()))


def windows(core, row, width):
    starts = []
    for c in (core, 1 - core):
        for r in (row, 1 - row):
            starts.append(pl.ds(pl.multiple_of((2 * c + r) * width, 128), width))
    return starts


def pack_kernel(vis_ref, txt_ref, hid_hbm, o_ref, *refs):
    sends, (v_ref, t_ref, hid_ref, out_ref, send_ref, in_sem, out_sem) = refs[:4], refs[4:]
    vis, txt = v_ref.shape[1], t_ref.shape[1]
    loads = [
        pltpu.make_async_copy(vis_ref.at[0, :, j], v_ref.at[j], in_sem.at[j]) for j in range(3)
    ] + [
        pltpu.make_async_copy(txt_ref.at[0, :, j], t_ref.at[j], in_sem.at[3 + j]) for j in range(2)
    ]
    loads.append(pltpu.make_async_copy(hid_hbm.at[0], hid_ref, in_sem.at[5]))
    for load in loads:
        load.start()
    stores = []
    at = 0
    for j in range(5):
        loads[j].wait()
        block = v_ref[j] if j < 3 else t_ref[j - 3]
        rows = vis if j < 3 else txt
        out_ref[:, at : at + rows, :] = jnp.swapaxes(block, 0, 1)
        stores.append(
            pltpu.make_async_copy(
                out_ref.at[:, at : at + rows, :], o_ref.at[:, at : at + rows, :], out_sem.at[j]
            )
        )
        stores[-1].start()
        at += rows
    loads[5].wait()
    core, row, col = (lax.axis_index(a) for a in ("cfg", "row", "col"))
    part = send_ref.shape[2] // 4
    for me in range(4):

        @pl.when(col == me)
        def _():
            for g, window in enumerate(windows(core, row, 4 * part)):
                hid = hid_ref[:, window]
                for d in range(4):
                    there = me ^ d
                    at = slice(there * part, (there + 1) * part)
                    send_ref[d, :, g * part : (g + 1) * part] = hid[:, at]

    for d in range(4):
        stores.append(pltpu.make_async_copy(send_ref.at[d], sends[d], out_sem.at[5 + d]))
        stores[-1].start()
    for store in stores:
        store.wait()


def pack(vis_qkv, text_kv, hidden):
    _, vis, _, heads, width = vis_qkv.shape
    txt = text_kv.shape[1]
    rows = 3 * vis + 2 * txt
    quarter = hidden.shape[2] // 4
    return pl.pallas_call(
        pack_kernel,
        in_specs=[ANY] * 3,
        out_specs=[ANY] * 5,
        out_shape=[jax.ShapeDtypeStruct((heads, rows, width), BF)]
        + [jax.ShapeDtypeStruct((vis, quarter), BF)] * 4,
        scratch_shapes=[
            pltpu.VMEM((3, vis, heads, width), BF),
            pltpu.VMEM((2, txt, heads, width), BF),
            pltpu.VMEM(hidden.shape[1:], BF),
            pltpu.VMEM((heads, rows, width), BF),
            pltpu.VMEM((4, vis, quarter), BF),
            pltpu.SemaphoreType.DMA((6,)),
            pltpu.SemaphoreType.DMA((9,)),
        ],
        compiler_params=pltpu.CompilerParams(vmem_limit_bytes=LARGE),
        cost_estimate=pl.CostEstimate(
            flops=0, bytes_accessed=4 * heads * rows * width, transcendentals=0
        ),
        name="pack",
    )(vis_qkv, text_kv, hidden)


def attend_kernel(len_ref, x_ref, o_hbm, k_ref, v_ref, o_ref, sem):
    src, heads, rows, width = x_ref.shape
    cols = src // 2
    vis = o_ref.shape[2] // 2
    txt = (rows - 3 * vis) // 2
    nv = src * vis
    keys = k_ref.shape[1]
    valid = lax.broadcasted_iota(jnp.int32, (1, keys - nv), 1) < len_ref[0]
    scale = math.log2(math.e) / math.sqrt(width)
    ones = jnp.ones((keys, width), BF)
    stores = []
    for h in range(heads):
        for i in range(src):
            at, t0 = slice(i * vis, (i + 1) * vis), nv + i * txt
            k_ref[h, at, :] = x_ref[i, h, vis : 2 * vis, :]
            v_ref[h, at, :width] = x_ref[i, h, 2 * vis : 3 * vis, :]
            k_ref[h, t0 : t0 + txt, :] = x_ref[i, h, 3 * vis : 3 * vis + txt, :]
            v_ref[h, t0 : t0 + txt, :width] = x_ref[i, h, 3 * vis + txt : 3 * vis + 2 * txt, :]
        v_ref[h, :, width:] = ones
        for i in range(0, src, 2):
            q = jnp.concatenate([x_ref[i, h, 0:vis, :], x_ref[i + 1, h, 0:vis, :]], axis=0)
            s = lax.dot_general(q, k_ref[h], NT, preferred_element_type=F32)
            s = jnp.concatenate([s[:, :nv], jnp.where(valid, s[:, nv:], NEG)], axis=1)
            e = jnp.exp2((s - jnp.max(s, axis=1, keepdims=True)) * scale)
            o = jnp.dot(e.astype(BF), v_ref[h], preferred_element_type=F32)
            n = h * src + i
            o_ref[h, i // 2] = (o[:, :width] / o[:, width:]).astype(BF)
            row, at = i // cols, (i % cols) * vis
            for d in range(row * cols, (row + 1) * cols):
                stores.append(
                    pltpu.make_async_copy(
                        o_ref.at[h, i // 2], o_hbm.at[d, h, pl.ds(at, 2 * vis)], sem.at[n + d % 2]
                    )
                )
                stores[-1].start()
    for store in stores:
        store.wait()


def attend(length, x, vis):
    src, heads, rows, width = x.shape
    txt = (rows - 3 * vis) // 2
    keys = src * (vis + txt)
    return pl.pallas_call(
        attend_kernel,
        in_specs=[SCALARS, WHOLE],
        out_specs=ANY,
        out_shape=jax.ShapeDtypeStruct((src, heads, src // 2 * vis, width), BF),
        scratch_shapes=[
            pltpu.VMEM((heads, keys, width), BF),
            pltpu.VMEM((heads, keys, 2 * width), BF),
            pltpu.VMEM((heads, src // 2, 2 * vis, width), BF),
            pltpu.SemaphoreType.DMA((heads * src,)),
        ],
        compiler_params=pltpu.CompilerParams(vmem_limit_bytes=SMALL),
        cost_estimate=pl.CostEstimate(
            flops=4 * heads * src * vis * keys * width,
            bytes_accessed=2 * x.size + 4 * heads * src * vis * width,
            transcendentals=heads * src * vis * keys,
        ),
        name="attend",
    )(length, x)


def split2(x):
    hi = x.astype(BF)
    return hi, (x - hi.astype(F32)).astype(BF)


def split3(x):
    a = x.astype(BF)
    rest = x - a.astype(F32)
    b = rest.astype(BF)
    return a, b, (rest - b.astype(F32)).astype(BF)


def places(cols, vis, patch):
    rows = 2 * patch + 16
    blocks = [(slice(g * cols, (g + 1) * cols), slice(0, None)) for g in range(4)]
    hidden, tables = [], []
    for k in range(4):
        at, across = 4 * cols + (k // 2) * vis, (k % 2) * 4 * cols
        hidden.append((slice(at, at + vis), slice(across, across + 4 * cols)))
        at, across = 4 * cols + (k // 2) * rows, 8 * cols + (k % 2) * (cols + 64)
        tables.append((slice(at, at + rows), slice(across, across + cols + 64)))
    return blocks, hidden, tables


def stage_kernel(mod_hbm, fin_hbm, *refs):
    w_hbm, got_hbm, out_hbm = refs[:4], refs[4:8], refs[8]
    mod_ref, fin_ref, all_ref, sem = refs[9:]
    core, row, col = (lax.axis_index(a) for a in ("cfg", "row", "col"))
    part, vis = w_hbm[0].shape[0], got_hbm[0].shape[0]
    patch = fin_ref.shape[0]
    blocks, hidden, tables = places(part, vis, patch)
    loads = [
        pltpu.make_async_copy(mod_hbm.at[0], mod_ref, sem.at[0]),
        pltpu.make_async_copy(fin_hbm, fin_ref, sem.at[1]),
    ]
    moves = [pltpu.make_async_copy(w_hbm[g], all_ref.at[blocks[g]], sem.at[2 + g]) for g in range(4)]
    for load in loads + moves:
        load.start()
    for load in loads:
        load.wait()
    for me in range(4):

        @pl.when(col == me)
        def _():
            copies = [
                pltpu.make_async_copy(got_hbm[d], all_ref.at[hidden[me ^ d]], sem.at[6 + d])
                for d in range(4)
            ]
            for copy in copies:
                copy.start()
            own = slice(me * part, (me + 1) * part)
            total, shift = 0.0, 0.0
            for g, window in enumerate(windows(core, row, 4 * part)):
                f = fin_ref[:, window].astype(F32)[:, own]
                scaled = f * (1.0 + mod_ref[1:2, window][:, own])
                total = total + jnp.sum(scaled, axis=1, keepdims=True)
                moved = f * mod_ref[2:3, window][:, own]
                shift = shift + jnp.sum(moved, axis=1, keepdims=True)
                hi, lo = split2(scaled)
                gate = split3(jnp.broadcast_to(mod_ref[0:1, window][:, own], (16, part)))
                line = lax.broadcasted_iota(jnp.int32, (16, part), 0)
                gate = jnp.where(line == 0, gate[0], jnp.where(line == 1, gate[1], gate[2]))
                both = jnp.concatenate([hi, lo, gate], axis=0)
                extra = jnp.zeros((both.shape[0], 64), BF)
                if g == 3:
                    lane = lax.broadcasted_iota(jnp.int32, (patch, 64), 1)
                    pieces = split3(jnp.where(lane % 2 == 0, total, shift))
                    pieces = jnp.where(
                        lane < 2, pieces[0], jnp.where(lane < 4, pieces[1], pieces[2])
                    )
                    extra = jnp.concatenate([pieces, extra[patch:]], axis=0)
                all_ref[tables[g]] = jnp.concatenate([both, extra], axis=1)
            for copy in copies:
                copy.wait()

    for move in moves:
        move.wait()
    store = pltpu.make_async_copy(all_ref, out_hbm, sem.at[0])
    store.start()
    store.wait()


def stage(modulation, final_t, blocks, got):
    patch, width = final_t.shape
    cols, depth = blocks[0].shape
    rows = 4 * cols + 2 * max(got[0].shape[0], 2 * patch + 16)
    return pl.pallas_call(
        stage_kernel,
        in_specs=[ANY] * 10,
        out_specs=ANY,
        out_shape=jax.ShapeDtypeStruct((rows, depth), BF),
        scratch_shapes=[
            pltpu.VMEM(modulation.shape[1:], F32),
            pltpu.VMEM(final_t.shape, BF),
            pltpu.VMEM((rows, depth), BF),
            pltpu.SemaphoreType.DMA((10,)),
        ],
        compiler_params=pltpu.CompilerParams(vmem_limit_bytes=LARGE),
        cost_estimate=pl.CostEstimate(flops=2 * 10**10, bytes_accessed=0, transcendentals=0),
        name="stage",
    )(modulation, final_t, *blocks, *got)


def project_kernel(a_ref, all_hbm, o_ref, w_ref, hid_ref, tab_ref, lhs_ref, r_ref, sem):
    chunks, tokens, depth = a_ref.shape
    vis = tokens // 4
    part = r_ref.shape[2]
    patch = 2 * o_ref.shape[1] - 16
    blocks, hidden, tables = places(part, vis, patch)
    loads, rest = [], []
    for k in range(4):
        w = pltpu.make_async_copy(all_hbm.at[blocks[k]], w_ref.at[k], sem.at[k])
        h = pltpu.make_async_copy(all_hbm.at[hidden[k]], hid_ref.at[k], sem.at[4 + k])
        t = pltpu.make_async_copy(all_hbm.at[tables[k]], tab_ref.at[k], sem.at[8 + k])
        loads.append(w)
        rest += [h, t]
    for load in loads + rest:
        load.start()
    for i in range(chunks):
        lhs_ref[:, i * depth : (i + 1) * depth] = a_ref[i]
    for g in range(4):
        loads[g].wait()
        r_ref[g] = lax.dot_general(lhs_ref[...], w_ref[g], NT, preferred_element_type=F32)
    for load in rest:
        load.wait()
    total = 0.0
    for g in range(4):
        h = jnp.concatenate([hid_ref[k, :, g * part : (g + 1) * part] for k in range(4)], axis=0)
        gate = tab_ref[g, 2 * patch :, :part].astype(F32)
        r = h.astype(F32) + (gate[0:1] + gate[1:2] + gate[2:3]) * r_ref[g]
        r_ref[g] = r
        total = total + r
    mean = jnp.sum(total, axis=1, keepdims=True) * (1.0 / (4 * part))
    spread = 0.0
    pred = jnp.zeros((patch, tokens), F32)
    for g in range(4):
        d = r_ref[g] - mean
        spread = spread + d * d
        hi, lo = split2(d)
        w_hi, w_lo = tab_ref[g, :patch, :part], tab_ref[g, patch : 2 * patch, :part]
        pred = pred + lax.dot_general(w_hi, hi, NT, preferred_element_type=F32)
        pred = pred + lax.dot_general(w_hi, lo, NT, preferred_element_type=F32)
        pred = pred + lax.dot_general(w_lo, hi, NT, preferred_element_type=F32)
    spread = jnp.sum(spread, axis=1, keepdims=True)
    lane = lax.broadcasted_iota(jnp.int32, (tokens, 128), 1)
    stats = jnp.transpose(jnp.where(lane == 0, mean, spread))[:8]
    sums = tab_ref[3, :patch, part:].astype(F32)
    sums = (sums[:, :32] + sums[:, 2:34]) + sums[:, 4:36]
    half = patch // 2
    for c in range(2):
        for k in range(4):
            at = slice(k * vis, (k + 1) * vis)
            rows = slice(c * half, (c + 1) * half)
            o_ref[c * 4 + k, :half] = jnp.concatenate([pred[rows, at], sums[rows]], axis=1)
            o_ref[c * 4 + k, half:] = jnp.concatenate([stats[:, at], stats[:, :32]], axis=1)


def project(att, staged, patch):
    chunks, tokens, width = att.shape
    depth = chunks * width
    vis = tokens // 4
    cols = depth * 3 // 32
    return pl.pallas_call(
        project_kernel,
        in_specs=[WHOLE, ANY],
        out_specs=WHOLE,
        out_shape=jax.ShapeDtypeStruct((8, patch // 2 + 8, 128), F32),
        scratch_shapes=[
            pltpu.VMEM((4, cols, depth), BF),
            pltpu.VMEM((4, vis, 4 * cols), BF),
            pltpu.VMEM((4, 2 * patch + 16, cols + 64), BF),
            pltpu.VMEM((tokens, depth), BF),
            pltpu.VMEM((4, tokens, cols), F32),
            pltpu.SemaphoreType.DMA((12,)),
        ],
        compiler_params=pltpu.CompilerParams(vmem_limit_bytes=MOST),
        cost_estimate=pl.CostEstimate(
            flops=8 * cols * depth * tokens,
            bytes_accessed=8 * cols * depth,
            transcendentals=0,
        ),
        name="project",
    )(att, staged)


def update_kernel(step_ref, x_ref, lat_ref, vel_ref, next_ref, den_ref, *, count):
    half, vis = lat_ref.shape
    preds = []
    for b in range(2):
        parts = [x_ref[b * 4 + k] for k in range(4)]
        means = [t[half : half + 1, :vis] for t in parts]
        mean = 0.25 * (means[0] + means[1] + means[2] + means[3])
        spread, linear, shift = 0.0, 0.0, 0.0
        for k in range(4):
            off = means[k] - mean
            spread = spread + parts[k][half + 1 : half + 2, :vis] + (0.25 * count) * (off * off)
            linear = linear + parts[k][:half, :vis] + parts[k][:half, vis : vis + 1] * off
            shift = shift + parts[k][:half, vis + 1 : vis + 2]
        preds.append(linear * lax.rsqrt(spread * (1.0 / count) + 1e-06) + shift)
    cond, uncond = preds
    velocity = uncond + 4.5 * (cond - uncond)
    step_now = step_ref[0].astype(F32)
    remain_now = 1.0 - step_now * (1.0 / STEPS)
    remain_next = 1.0 - (step_now + 1.0) * (1.0 / STEPS)
    sigma_now = remain_now * remain_now
    sigma_next = remain_next * remain_next
    latent = lat_ref[...]
    vel_ref[...] = velocity
    next_ref[...] = latent + (sigma_next - sigma_now) * velocity
    den_ref[...] = latent - sigma_now * velocity


def update(timestep, parts, latent, count):
    return pl.pallas_call(
        functools.partial(update_kernel, count=count),
        in_specs=[SCALARS, WHOLE, WHOLE],
        out_specs=[WHOLE] * 3,
        out_shape=[jax.ShapeDtypeStruct(latent.shape, F32)] * 3,
        compiler_params=pltpu.CompilerParams(vmem_limit_bytes=2 << 20),
        name="update",
    )(timestep, parts, latent)


def across_outer(reqs):
    deep = 8
    if reqs % deep:
        return None
    high = reqs // deep
    pairs = []
    for r in range(reqs):
        for s in range(8):
            y = 2 * (r // deep) + s // 4
            near = (y + 1 if y % 2 else y - 1) % (2 * high)
            pairs.append((r * 8 + s, (near // 2 * deep + r % deep) * 8 + near % 2 * 4 + s % 4))
    return pairs


def shards(
    vis_qkv, text_kv, text_len, vis_hidden, out_weight, modulation, final_weight, latent, timestep
):
    vis, txt = vis_qkv.shape[1], text_kv.shape[1]
    cores = [(0, 1), (1, 0)]
    outer = across_outer(lax.axis_size("req"))

    own = out_weight.T

    def across(block):
        if outer is None:
            return lax.ppermute(block, "row", cores)
        return lax.ppermute(block, ("req", "row", "col"), outer)

    far = across(own)
    packed, mine, *sends = pack(vis_qkv, text_kv, vis_hidden)
    heads = lax.all_to_all(
        packed, ("row", "col"), split_axis=0, concat_axis=0, tiled=True
    ).reshape(8, 2, 3 * vis + 2 * txt, 128)
    got = [mine] + [
        lax.ppermute(block, "col", [(c, c ^ d) for c in range(4)])
        for d, block in zip((1, 2, 3), sends)
    ]
    attended = attend(text_len[0], heads, vis)
    far, modulation, *got = lax.optimization_barrier((far, modulation, *got))
    own_other, far_other = (lax.ppermute(b, "cfg", cores) for b in (own, far))
    staged = stage(modulation, final_weight.T, [own, far, own_other, far_other], got)
    att = lax.all_to_all(
        attended, ("row", "col"), split_axis=0, concat_axis=0, tiled=True
    ).reshape(16, 4 * vis, 128)
    parts = project(att, staged, final_weight.shape[1])
    parts = lax.all_to_all(parts, ("cfg", "col"), split_axis=0, concat_axis=0, tiled=True)
    outs = update(timestep, parts, latent.T, vis_hidden.shape[2])
    return tuple(o.T for o in outs)


def solution(mesh):
    req, cfg, sp = mesh.devices.shape
    fine = jax.sharding.Mesh(
        mesh.devices.reshape(req, cfg, 2, sp // 2), ("req", "cfg", "row", "col")
    )
    tokens = ("req", "row", "col")
    out = P(tokens, "cfg")
    return jax.shard_map(
        shards,
        mesh=fine,
        in_specs=(
            P("cfg", tokens, None, None, None),
            P("cfg", tokens, None, None, None),
            P("cfg", "req"),
            P("cfg", tokens, None),
            P(None, ("cfg", "row", "col")),
            P("cfg", "req", None),
            P(),
            out,
            P("req"),
        ),
        out_specs=(out, out, out),
        check_vma=False,
    )
```

time: 88 us -> 73.1 us (0.83)
  waiting for transfers between devices: 23.9 us -> 9.34 us
  starting transfers between devices: 35.1 us -> 41.2 us
  Pallas kernels: 22.5 us -> 18.2 us
  local copies, waits for them, and re-layouts: 3.3 us -> 1.54 us
    all_to_all x1, waiting for transfers between devices: 14.3 us -> 3.22 us  [shards(): lax.all_to_all(attended, ('row', 'col'), split_axis=0, concat_axis=0, til...]
    all_to_all x1 -> x0, starting transfers between devices: 6.49 us -> none  [shards(): got = lax.all_to_all(send, 'col', split_axis=0, concat_axis=0, tiled=True)]
    ppermute x2 -> x5, starting transfers between devices: 10.5 us -> 16.5 us  [the longest x3 9.58 us: shards(): lax.ppermute(block, 'col', [(c, c ^ d) for c in range(4)])]
    pallas_call x4, Pallas kernels: 20.8 us -> 17.5 us  [the longest x1 7.23 us: project(): pl.pallas_call(project_kernel, in_specs=[WHOLE, ANY], out_specs=WHOLE, ou...]
    ppermute x1, starting transfers between devices: 1.92 us -> 5.25 us  [across(): return lax.ppermute(block, ('req', 'row', 'col'), outer)]
    all_to_all x1, starting transfers between devices: 4.23 us -> 6.95 us  [shards(): lax.all_to_all(parts, ('cfg', 'col'), split_axis=0, concat_axis=0, tiled=...]
    unnamed x15 -> x16, local copies, waits for them, and re-layouts: 3.3 us -> 0.9 us
    all_to_all x1, waiting for transfers between devices: 2.15 us -> 0.01 us  [shards(): lax.all_to_all(packed, ('row', 'col'), split_axis=0, concat_axis=0, tiled...]
  transfers between devices with their start and end apart: 7 -> 9, of which waited for: 5 -> 3; matrix products, arithmetic and copies ran while one was open for 1% -> 1% of each run, Pallas kernels for 11% -> 10%
where the time goes in v2:
time: 73.1 us; the launch traced here: 72.4 us
  starting transfers between devices  41.2 us (56%)
  Pallas kernels  18.2 us (25%)
  waiting for transfers between devices  9.34 us (13%)
  between operations  2.12 us (3%)
  local copies, waits for them, and re-layouts  1.54 us (2%)
    ppermute x3, starting transfers between devices, shards(): lax.ppermute(block, 'col', [(c, c ^ d) for c in range(4)])  9.58 us
    pallas_call x1, Pallas kernels, project(): pl.pallas_call(project_kernel, in_specs=[WHOLE, ANY], out_specs=WHOLE, ou...  7.23 us
    ppermute x2, starting transfers between devices, shards(): own_other, far_other = (lax.ppermute(b, 'cfg', cores) for b in (own, far))  6.96 us
    all_to_all x1, starting transfers between devices, shards(): lax.all_to_all(parts, ('cfg', 'col'), split_axis=0, concat_axis=0, tiled=...  6.95 us
    all_to_all x1, starting transfers between devices, shards(): lax.all_to_all(attended, ('row', 'col'), split_axis=0, concat_axis=0, til...  6.49 us
    all_to_all x1, starting transfers between devices, shards(): lax.all_to_all(packed, ('row', 'col'), split_axis=0, concat_axis=0, tiled...  5.98 us
    ppermute x1, starting transfers between devices, across(): return lax.ppermute(block, ('req', 'row', 'col'), outer)  5.25 us
    all_to_all x1, waiting for transfers between devices, shards(): lax.all_to_all(parts, ('cfg', 'col'), split_axis=0, concat_axis=0, tiled=...  4.51 us
  transfers between devices with their start and end apart: 9, of which 3 were waited for; matrix products, arithmetic and copies ran while one was open for 1% of the time, Pallas kernels for 10%

profile of v2, /device:TPU:1, one launch (start us, length us, event | category | flops | bytes accessed | tf_op | source)
XLA Modules:
  0.0 72.4 jit_solution(13877816060963614839)
XLA Ops:
  0.6 2.8 %pack.1 = (bf16[16,352,128]{2,1,0:T(8,128)(2,1)}, bf16[96,768]{1,0:T(8,128)(2,1)}, bf16[96,768]{1,0:T(8,128)(2,1)}, bf16[96,768]{1,0:T(8,128)(2,1)}, bf16[96,768]{1,0:T(8,128)(2,1)}) custom-call(bf16[1,96,3,16,128]{4,3,2,1,0:T(8,128)(2,1)} %vis_ref.1, bf16[1,32,2,16,128]{4,3,2,1,0:T(8,128)(2,1)} %txt_ref.1, bf16[1,96,3072]{2,1,0:T(8,128)(2,1)} %hid_hbm.1), custom_call_target="tpu_custom_call" | custom-call | bytes 2883584 | tf_op jit(solution)/shard_map/pack/pallas_call | solution.py:83
  3.5 0.0 copy-start.2
  3.5 6.0 %all-to-all-start = ((bf16[16,352,128]{2,1,0:T(8,128)(2,1)}), bf16[16,352,128]{2,1,0:T(8,128)(2,1)S(1)}, u32[]{:S(2)}, u32[]{:S(2)}) async-start(bf16[16,352,128]{2,1,0:T(8,128)(2,1)} %get-tuple-element.17), calls=%async_computation | async-start | bytes 2883584 | tf_op jit(solution)/shard_map/all_to_all | solution.py:423
  9.5 0.0 copy-done.2
  9.5 5.2 %collective-permute-start = (bf16[192,2048]{1,0:T(8,128)(2,1)S(1)}, bf16[192,2048]{1,0:T(8,128)(2,1)S(1)}, u32[]{:S(2)}, u32[]{:S(2)}) collective-permute-start(bf16[192,2048]{1,0:T(8,128)(2,1)S(1)} %bitcast.14), channel_id=1, source_target_pairs={{0,388},{1,389},{2,390},{3,391},{4,128},{5,129},{6,130},{7,131},{1... | collective-permute-start | bytes 2359304 | tf_op jit(solution)/shard_map/ppermute | solution.py:419
  14.7 3.1 %collective-permute-start.1 = (bf16[96,768]{1,0:T(8,128)(2,1)}, bf16[96,768]{1,0:T(8,128)(2,1)S(1)}, u32[]{:S(2)}, u32[]{:S(2)}) collective-permute-start(bf16[96,768]{1,0:T(8,128)(2,1)} %get-tuple-element.19), channel_id=1, source_target_pairs={{0,1},{1,0},{2,3},{3,2},{4,5},{5,4},{6,7},{7,6},{8,9},{9,8},{10,11... | collective-permute-start | bytes 442376 | tf_op jit(solution)/shard_map/ppermute | solution.py:427
  17.8 4.3 %collective-permute-start.2 = (bf16[96,768]{1,0:T(8,128)(2,1)}, bf16[96,768]{1,0:T(8,128)(2,1)S(1)}, u32[]{:S(2)}, u32[]{:S(2)}) collective-permute-start(bf16[96,768]{1,0:T(8,128)(2,1)} %get-tuple-element.20), channel_id=1, source_target_pairs={{0,2},{1,3},{2,0},{3,1},{4,6},{5,7},{6,4},{7,5},{8,10},{9,11},{10,... | collective-permute-start | bytes 442376 | tf_op jit(solution)/shard_map/ppermute | solution.py:427
  22.1 2.2 %collective-permute-start.3 = (bf16[96,768]{1,0:T(8,128)(2,1)}, bf16[96,768]{1,0:T(8,128)(2,1)}, u32[]{:S(2)}, u32[]{:S(2)}) collective-permute-start(bf16[96,768]{1,0:T(8,128)(2,1)} %get-tuple-element.21), channel_id=1, source_target_pairs={{0,3},{1,2},{2,1},{3,0},{4,7},{5,6},{6,5},{7,4},{8,11},{9,10},{10,... | collective-permute-start | bytes 442376 | tf_op jit(solution)/shard_map/ppermute | solution.py:427
  25.0 0.0 all-to-all-done
  25.0 3.1 %attend.1 = bf16[8,2,384,128]{3,2,1,0:T(8,128)(2,1)} custom-call(s32[1]{0:T(128)} %bitcast.9.len_ref, bf16[8,2,352,128]{3,2,1,0:T(8,128)(2,1)S(1)} %bitcast.11), custom_call_target="tpu_custom_call" | custom-call | flops 805306368 | bytes 2228224 | tf_op jit(solution)/shard_map/attend/pallas_call | solution.py:149
  28.1 0.0 copy-start.1
  28.1 6.5 %all-to-all-start.1 = ((bf16[8,2,384,128]{3,2,1,0:T(8,128)(2,1)}), bf16[8,2,384,128]{3,2,1,0:T(8,128)(2,1)S(1)}, u32[]{:S(2)}, u32[]{:S(2)}) async-start(bf16[8,2,384,128]{3,2,1,0:T(8,128)(2,1)} %attend.1), calls=%async_computation.1 | async-start | bytes 3145728 | tf_op jit(solution)/shard_map/all_to_all | solution.py:434
  34.6 5.0 %collective-permute-start.4 = (bf16[192,2048]{1,0:T(8,128)(2,1)S(1)}, bf16[192,2048]{1,0:T(8,128)(2,1)S(1)}, u32[]{:S(2)}, u32[]{:S(2)}) collective-permute-start(bf16[192,2048]{1,0:T(8,128)(2,1)S(1)} %bitcast.15), channel_id=1, source_target_pairs={{0,8},{8,0},{1,9},{9,1},{2,10},{10,2},{3,11},{11,3},{4,12},{12,4},... | collective-permute-start | bytes 2359304 | tf_op jit(solution)/shard_map/ppermute | solution.py:432
  39.7 0.0 collective-permute-done.1.refs_5_
  39.7 0.0 copy-start.6
  39.7 0.0 collective-permute-done.2.refs_6_
  39.7 0.0 copy-start.7
  39.7 0.0 collective-permute-done.3.refs_7_
  39.7 0.0 collective-permute-done.refs_1_
  39.7 0.0 copy-start.3
  39.7 1.9 %collective-permute-start.5 = (bf16[192,2048]{1,0:T(8,128)(2,1)S(1)}, bf16[192,2048]{1,0:T(8,128)(2,1)S(1)}, u32[]{:S(2)}, u32[]{:S(2)}) collective-permute-start(bf16[192,2048]{1,0:T(8,128)(2,1)S(1)} %collective-permute-done.refs_1_), channel_id=1, source_target_pairs={{0,8},{8,0},{1,9},{9,1},{2,10},{10,2},{3,11},{11,3},{4,12},{12,4},... | collective-permute-start | bytes 2359304 | tf_op jit(solution)/shard_map/ppermute | solution.py:432
  41.7 0.0 copy-done.1
  41.7 0.6 copy.12.mod_hbm
  42.3 0.0 collective-permute-done.4.refs_2_
  42.3 1.6 %collective-permute-done.5.refs_3_ = bf16[192,2048]{1,0:T(8,128)(2,1)S(1)} collective-permute-done((bf16[192,2048]{1,0:T(8,128)(2,1)S(1)}, bf16[192,2048]{1,0:T(8,128)(2,1)S(1)}, u32[]{:S(2)}, u32[]{:S(2)}) %collective-permute-start.5) | collective-permute-done | bytes 786464 | tf_op jit(solution)/shard_map/ppermute | solution.py:432
  43.9 0.9 %copy-done.5 = bf16[192,2048]{1,0:T(8,128)(2,1)} copy-done((bf16[192,2048]{1,0:T(8,128)(2,1)}, bf16[192,2048]{1,0:T(8,128)(2,1)S(1)}, u32[]{:S(2)}) %copy-start.5) | copy-done | bytes 786456
  44.8 4.3 %stage.1.all_hbm = bf16[992,2048]{1,0:T(8,128)(2,1)} custom-call(f32[1,3,3072]{2,1,0:T(4,128)} %copy.12.mod_hbm, bf16[48,3072]{1,0:T(8,128)(2,1)} %bitcast.16, bf16[192,2048]{1,0:T(8,128)(2,1)} %bitcast.13, bf16[192,2048]{1,0:T(8,128)(2,1)} %copy-done.3, bf16[192,2048]{1,0:T(8,128)(2,1)} %copy-done.4, bf16[192,2048]{1,0:T(8,128)(2,1)} %copy-done.5, ...), custom_call_target="tpu_custom_call" | custom-call | flops 20000000000 | tf_op jit(solution)/shard_map/stage/pallas_call | solution.py:256
  49.1 3.2 %all-to-all-done.1 = bf16[8,2,384,128]{3,2,1,0:T(8,128)(2,1)S(1)} async-done(((bf16[8,2,384,128]{3,2,1,0:T(8,128)(2,1)}), bf16[8,2,384,128]{3,2,1,0:T(8,128)(2,1)S(1)}, u32[]{:S(2)}, u32[]{:S(2)}) %all-to-all-start.1) | async-done | bytes 1572896 | tf_op jit(solution)/shard_map/all_to_all | solution.py:434
  52.4 7.2 %project.1 = f32[8,32,128]{2,1,0:T(8,128)} custom-call(bf16[16,384,128]{2,1,0:T(8,128)(2,1)S(1)} %bitcast.10, bf16[992,2048]{1,0:T(8,128)(2,1)} %stage.1.all_hbm), custom_call_target="tpu_custom_call" | custom-call | flops 1207959552 | bytes 3145728 | tf_op jit(solution)/shard_map/project/pallas_call | solution.py:332
  59.6 6.9 %all-to-all-start.2 = ((f32[8,32,128]{2,1,0:T(8,128)}), f32[8,32,128]{2,1,0:T(8,128)S(1)}, u32[]{:S(2)}, u32[]{:S(2)}) async-start(f32[8,32,128]{2,1,0:T(8,128)} %project.1), calls=%async_computation.2 | async-start | bytes 262144 | tf_op jit(solution)/shard_map/all_to_all | solution.py:438
  67.2 4.5 %all-to-all-done.2.x_ref = f32[8,32,128]{2,1,0:T(8,128)S(1)} async-done(((f32[8,32,128]{2,1,0:T(8,128)}), f32[8,32,128]{2,1,0:T(8,128)S(1)}, u32[]{:S(2)}, u32[]{:S(2)}) %all-to-all-start.2) | async-done | bytes 131104 | tf_op jit(solution)/shard_map/all_to_all | solution.py:438
  71.7 0.7 update.1
  (8 shorter events, 0.0 us)
Async XLA Ops:
  3.5 6.0 %copy-start.2 = (bf16[2048,192]{0,1:T(8,128)(2,1)S(1)}, bf16[2048,192]{0,1:T(8,128)(2,1)}, u32[]{:S(2)}) copy-start(bf16[2048,192]{0,1:T(8,128)(2,1)} %param.13) | copy-start | bytes 2359300
  3.5 21.5 %all-to-all-start = ((bf16[16,352,128]{2,1,0:T(8,128)(2,1)}), bf16[16,352,128]{2,1,0:T(8,128)(2,1)S(1)}, u32[]{:S(2)}, u32[]{:S(2)}) async-start(bf16[16,352,128]{2,1,0:T(8,128)(2,1)} %get-tuple-element.17), calls=%async_computation | async-start | bytes 2883584 | tf_op jit(solution)/shard_map/all_to_all | solution.py:423
  9.5 30.2 %collective-permute-start = (bf16[192,2048]{1,0:T(8,128)(2,1)S(1)}, bf16[192,2048]{1,0:T(8,128)(2,1)S(1)}, u32[]{:S(2)}, u32[]{:S(2)}) collective-permute-start(bf16[192,2048]{1,0:T(8,128)(2,1)S(1)} %bitcast.14), channel_id=1, source_target_pairs={{0,388},{1,389},{2,390},{3,391},{4,128},{5,129},{6,130},{7,131},{1... | collective-permute-start | bytes 2359304 | tf_op jit(solution)/shard_map/ppermute | solution.py:419
  14.7 24.9 %collective-permute-start.1 = (bf16[96,768]{1,0:T(8,128)(2,1)}, bf16[96,768]{1,0:T(8,128)(2,1)S(1)}, u32[]{:S(2)}, u32[]{:S(2)}) collective-permute-start(bf16[96,768]{1,0:T(8,128)(2,1)} %get-tuple-element.19), channel_id=1, source_target_pairs={{0,1},{1,0},{2,3},{3,2},{4,5},{5,4},{6,7},{7,6},{8,9},{9,8},{10,11... | collective-permute-start | bytes 442376 | tf_op jit(solution)/shard_map/ppermute | solution.py:427
  17.8 21.9 %collective-permute-start.2 = (bf16[96,768]{1,0:T(8,128)(2,1)}, bf16[96,768]{1,0:T(8,128)(2,1)S(1)}, u32[]{:S(2)}, u32[]{:S(2)}) collective-permute-start(bf16[96,768]{1,0:T(8,128)(2,1)} %get-tuple-element.20), channel_id=1, source_target_pairs={{0,2},{1,3},{2,0},{3,1},{4,6},{5,7},{6,4},{7,5},{8,10},{9,11},{10,... | collective-permute-start | bytes 442376 | tf_op jit(solution)/shard_map/ppermute | solution.py:427
  22.1 17.6 %collective-permute-start.3 = (bf16[96,768]{1,0:T(8,128)(2,1)}, bf16[96,768]{1,0:T(8,128)(2,1)}, u32[]{:S(2)}, u32[]{:S(2)}) collective-permute-start(bf16[96,768]{1,0:T(8,128)(2,1)} %get-tuple-element.21), channel_id=1, source_target_pairs={{0,3},{1,2},{2,1},{3,0},{4,7},{5,6},{6,5},{7,4},{8,11},{9,10},{10,... | collective-permute-start | bytes 442376 | tf_op jit(solution)/shard_map/ppermute | solution.py:427
  28.1 13.5 %copy-start.1 = (f32[1,3,3072]{2,0,1:T(1,128)S(1)}, f32[1,3,3072]{2,0,1:T(1,128)}, u32[]{:S(2)}) copy-start(f32[1,3,3072]{2,0,1:T(1,128)} %param.14) | copy-start | bytes 110596
  28.1 24.2 %all-to-all-start.1 = ((bf16[8,2,384,128]{3,2,1,0:T(8,128)(2,1)}), bf16[8,2,384,128]{3,2,1,0:T(8,128)(2,1)S(1)}, u32[]{:S(2)}, u32[]{:S(2)}) async-start(bf16[8,2,384,128]{3,2,1,0:T(8,128)(2,1)} %attend.1), calls=%async_computation.1 | async-start | bytes 3145728 | tf_op jit(solution)/shard_map/all_to_all | solution.py:434
  34.6 7.7 %collective-permute-start.4 = (bf16[192,2048]{1,0:T(8,128)(2,1)S(1)}, bf16[192,2048]{1,0:T(8,128)(2,1)S(1)}, u32[]{:S(2)}, u32[]{:S(2)}) collective-permute-start(bf16[192,2048]{1,0:T(8,128)(2,1)S(1)} %bitcast.15), channel_id=1, source_target_pairs={{0,8},{8,0},{1,9},{9,1},{2,10},{10,2},{3,11},{11,3},{4,12},{12,4},... | collective-permute-start | bytes 2359304 | tf_op jit(solution)/shard_map/ppermute | solution.py:432
  39.7 4.2 %copy-start.6 = (bf16[96,768]{1,0:T(8,128)(2,1)}, bf16[96,768]{1,0:T(8,128)(2,1)S(1)}, u32[]{:S(2)}) copy-start(bf16[96,768]{1,0:T(8,128)(2,1)S(1)} %collective-permute-done.1.refs_5_) | copy-start | bytes 442372
  39.7 4.2 %copy-start.7 = (bf16[96,768]{1,0:T(8,128)(2,1)}, bf16[96,768]{1,0:T(8,128)(2,1)S(1)}, u32[]{:S(2)}) copy-start(bf16[96,768]{1,0:T(8,128)(2,1)S(1)} %collective-permute-done.2.refs_6_) | copy-start | bytes 442372
  39.7 4.2 %copy-start.3 = (bf16[192,2048]{1,0:T(8,128)(2,1)}, bf16[192,2048]{1,0:T(8,128)(2,1)S(1)}, u32[]{:S(2)}) copy-start(bf16[192,2048]{1,0:T(8,128)(2,1)S(1)} %collective-permute-done.refs_1_) | copy-start | bytes 2359300
  39.7 4.2 %collective-permute-start.5 = (bf16[192,2048]{1,0:T(8,128)(2,1)S(1)}, bf16[192,2048]{1,0:T(8,128)(2,1)S(1)}, u32[]{:S(2)}, u32[]{:S(2)}) collective-permute-start(bf16[192,2048]{1,0:T(8,128)(2,1)S(1)} %collective-permute-done.refs_1_), channel_id=1, source_target_pairs={{0,8},{8,0},{1,9},{9,1},{2,10},{10,2},{3,11},{11,3},{4,12},{12,4},... | collective-permute-start | bytes 2359304 | tf_op jit(solution)/shard_map/ppermute | solution.py:432
  42.3 1.6 %copy-start.4 = (bf16[192,2048]{1,0:T(8,128)(2,1)}, bf16[192,2048]{1,0:T(8,128)(2,1)S(1)}, u32[]{:S(2)}) copy-start(bf16[192,2048]{1,0:T(8,128)(2,1)S(1)} %collective-permute-done.4.refs_2_) | copy-start | bytes 2359300
  43.9 0.9 %copy-start.5 = (bf16[192,2048]{1,0:T(8,128)(2,1)}, bf16[192,2048]{1,0:T(8,128)(2,1)S(1)}, u32[]{:S(2)}) copy-start(bf16[192,2048]{1,0:T(8,128)(2,1)S(1)} %collective-permute-done.5.refs_3_) | copy-start | bytes 2359300
  52.4 19.3 %copy-start = (f32[96,24]{0,1:T(8,128)S(1)}, f32[96,24]{0,1:T(8,128)}, u32[]{:S(2)}) copy-start(f32[96,24]{0,1:T(8,128)} %param.16) | copy-start | bytes 27652
  59.6 12.1 %all-to-all-start.2 = ((f32[8,32,128]{2,1,0:T(8,128)}), f32[8,32,128]{2,1,0:T(8,128)S(1)}, u32[]{:S(2)}, u32[]{:S(2)}) async-start(f32[8,32,128]{2,1,0:T(8,128)} %project.1), calls=%async_computation.2 | async-start | bytes 262144 | tf_op jit(solution)/shard_map/all_to_all | solution.py:438

commit v3 on v2

--- a/solution.py
+++ b/solution.py
@@ -12,6 +12,7 @@
 SMALL = 16 << 20
 LARGE = 56 << 20
 MOST = 51 << 20
+STAGE = 10 << 20
 NEG = -1e30
 BF = jnp.bfloat16
 F32 = jnp.float32
@@ -29,15 +30,13 @@
     return starts
 
 
-def pack_kernel(vis_ref, txt_ref, hid_hbm, o_ref, *refs):
-    sends, (v_ref, t_ref, hid_ref, out_ref, send_ref, in_sem, out_sem) = refs[:4], refs[4:]
+def pack_kernel(vis_ref, txt_ref, o_ref, v_ref, t_ref, out_ref, in_sem, out_sem):
     vis, txt = v_ref.shape[1], t_ref.shape[1]
     loads = [
         pltpu.make_async_copy(vis_ref.at[0, :, j], v_ref.at[j], in_sem.at[j]) for j in range(3)
     ] + [
         pltpu.make_async_copy(txt_ref.at[0, :, j], t_ref.at[j], in_sem.at[3 + j]) for j in range(2)
     ]
-    loads.append(pltpu.make_async_copy(hid_hbm.at[0], hid_ref, in_sem.at[5]))
     for load in loads:
         load.start()
     stores = []
@@ -54,9 +53,41 @@
         )
         stores[-1].start()
         at += rows
-    loads[5].wait()
+    for store in stores:
+        store.wait()
+
+
+def pack(vis_qkv, text_kv):
+    _, vis, _, heads, width = vis_qkv.shape
+    txt = text_kv.shape[1]
+    rows = 3 * vis + 2 * txt
+    return pl.pallas_call(
+        pack_kernel,
+        in_specs=[ANY, ANY],
+        out_specs=ANY,
+        out_shape=jax.ShapeDtypeStruct((heads, rows, width), BF),
+        scratch_shapes=[
+            pltpu.VMEM((3, vis, heads, width), BF),
+            pltpu.VMEM((2, txt, heads, width), BF),
+            pltpu.VMEM((heads, rows, width), BF),
+            pltpu.SemaphoreType.DMA((5,)),
+            pltpu.SemaphoreType.DMA((5,)),
+        ],
+        compiler_params=pltpu.CompilerParams(vmem_limit_bytes=LARGE),
+        cost_estimate=pl.CostEstimate(
+            flops=0, bytes_accessed=4 * heads * rows * width, transcendentals=0
+        ),
+        name="pack",
+    )(vis_qkv, text_kv)
+
+
+def share_kernel(hid_hbm, *refs):
+    sends, (hid_ref, sem) = refs[:4], refs[4:]
+    load = pltpu.make_async_copy(hid_hbm.at[0], hid_ref, sem)
+    load.start()
     core, row, col = (lax.axis_index(a) for a in ("cfg", "row", "col"))
-    part = send_ref.shape[2] // 4
+    part = sends[0].shape[1] // 4
+    load.wait()
     for me in range(4):
 
         @pl.when(col == me)
@@ -66,41 +97,20 @@
                 for d in range(4):
                     there = me ^ d
                     at = slice(there * part, (there + 1) * part)
-                    send_ref[d, :, g * part : (g + 1) * part] = hid[:, at]
-
-    for d in range(4):
-        stores.append(pltpu.make_async_copy(send_ref.at[d], sends[d], out_sem.at[5 + d]))
-        stores[-1].start()
-    for store in stores:
-        store.wait()
-
-
-def pack(vis_qkv, text_kv, hidden):
-    _, vis, _, heads, width = vis_qkv.shape
-    txt = text_kv.shape[1]
-    rows = 3 * vis + 2 * txt
-    quarter = hidden.shape[2] // 4
-    return pl.pallas_call(
-        pack_kernel,
-        in_specs=[ANY] * 3,
-        out_specs=[ANY] * 5,
-        out_shape=[jax.ShapeDtypeStruct((heads, rows, width), BF)]
-        + [jax.ShapeDtypeStruct((vis, quarter), BF)] * 4,
-        scratch_shapes=[
-            pltpu.VMEM((3, vis, heads, width), BF),
-            pltpu.VMEM((2, txt, heads, width), BF),
-            pltpu.VMEM(hidden.shape[1:], BF),
-            pltpu.VMEM((heads, rows, width), BF),
-            pltpu.VMEM((4, vis, quarter), BF),
-            pltpu.SemaphoreType.DMA((6,)),
-            pltpu.SemaphoreType.DMA((9,)),
-        ],
+                    sends[d][:, g * part : (g + 1) * part] = hid[:, at]
+
+
+def share(hidden):
+    _, vis, width = hidden.shape
+    return pl.pallas_call(
+        share_kernel,
+        in_specs=[ANY],
+        out_specs=[WHOLE] * 4,
+        out_shape=[jax.ShapeDtypeStruct((vis, width // 4), BF)] * 4,
+        scratch_shapes=[pltpu.VMEM((vis, width), BF), pltpu.SemaphoreType.DMA],
         compiler_params=pltpu.CompilerParams(vmem_limit_bytes=LARGE),
-        cost_estimate=pl.CostEstimate(
-            flops=0, bytes_accessed=4 * heads * rows * width, transcendentals=0
-        ),
-        name="pack",
-    )(vis_qkv, text_kv, hidden)
+        name="share",
+    )(hidden)
 
 
 def attend_kernel(len_ref, x_ref, o_hbm, k_ref, v_ref, o_ref, sem):
@@ -181,28 +191,30 @@
 
 def places(cols, vis, patch):
     rows = 2 * patch + 16
-    blocks = [(slice(g * cols, (g + 1) * cols), slice(0, None)) for g in range(4)]
     hidden, tables = [], []
     for k in range(4):
-        at, across = 4 * cols + (k // 2) * vis, (k % 2) * 4 * cols
+        at, across = (k // 2) * vis, (k % 2) * 4 * cols
         hidden.append((slice(at, at + vis), slice(across, across + 4 * cols)))
-        at, across = 4 * cols + (k // 2) * rows, 8 * cols + (k % 2) * (cols + 64)
+        at, across = (k // 2) * rows, 8 * cols + (k % 2) * (cols + 64)
         tables.append((slice(at, at + rows), slice(across, across + cols + 64)))
-    return blocks, hidden, tables
+    return hidden, tables
 
 
 def stage_kernel(mod_hbm, fin_hbm, *refs):
-    w_hbm, got_hbm, out_hbm = refs[:4], refs[4:8], refs[8]
-    mod_ref, fin_ref, all_ref, sem = refs[9:]
+    w_hbm, got_hbm, (aux_ref, out_hbm) = refs[:4], refs[4:8], refs[8:10]
+    mod_ref, fin_ref, w_ref, sem = refs[10:]
     core, row, col = (lax.axis_index(a) for a in ("cfg", "row", "col"))
     part, vis = w_hbm[0].shape[0], got_hbm[0].shape[0]
     patch = fin_ref.shape[0]
-    blocks, hidden, tables = places(part, vis, patch)
+    hidden, tables = places(part, vis, patch)
     loads = [
         pltpu.make_async_copy(mod_hbm.at[0], mod_ref, sem.at[0]),
         pltpu.make_async_copy(fin_hbm, fin_ref, sem.at[1]),
     ]
-    moves = [pltpu.make_async_copy(w_hbm[g], all_ref.at[blocks[g]], sem.at[2 + g]) for g in range(4)]
+    moves = [
+        pltpu.make_async_copy(w_hbm[g], w_ref.at[g * part : (g + 1) * part], sem.at[2 + g])
+        for g in range(4)
+    ]
     for load in loads + moves:
         load.start()
     for load in loads:
@@ -212,7 +224,7 @@
         @pl.when(col == me)
         def _():
             copies = [
-                pltpu.make_async_copy(got_hbm[d], all_ref.at[hidden[me ^ d]], sem.at[6 + d])
+                pltpu.make_async_copy(got_hbm[d], aux_ref.at[hidden[me ^ d]], sem.at[6 + d])
                 for d in range(4)
             ]
             for copy in copies:
@@ -238,13 +250,13 @@
                         lane < 2, pieces[0], jnp.where(lane < 4, pieces[1], pieces[2])
                     )
                     extra = jnp.concatenate([pieces, extra[patch:]], axis=0)
-                all_ref[tables[g]] = jnp.concatenate([both, extra], axis=1)
+                aux_ref[tables[g]] = jnp.concatenate([both, extra], axis=1)
             for copy in copies:
                 copy.wait()
 
     for move in moves:
         move.wait()
-    store = pltpu.make_async_copy(all_ref, out_hbm, sem.at[0])
+    store = pltpu.make_async_copy(w_ref, out_hbm, sem.at[0])
     store.start()
     store.wait()
 
@@ -252,95 +264,93 @@
 def stage(modulation, final_t, blocks, got):
     patch, width = final_t.shape
     cols, depth = blocks[0].shape
-    rows = 4 * cols + 2 * max(got[0].shape[0], 2 * patch + 16)
+    rows = 2 * max(got[0].shape[0], 2 * patch + 16)
     return pl.pallas_call(
         stage_kernel,
         in_specs=[ANY] * 10,
-        out_specs=ANY,
-        out_shape=jax.ShapeDtypeStruct((rows, depth), BF),
+        out_specs=[WHOLE, ANY],
+        out_shape=[
+            jax.ShapeDtypeStruct((rows, depth), BF),
+            jax.ShapeDtypeStruct((4 * cols, depth), BF),
+        ],
         scratch_shapes=[
             pltpu.VMEM(modulation.shape[1:], F32),
             pltpu.VMEM(final_t.shape, BF),
-            pltpu.VMEM((rows, depth), BF),
+            pltpu.VMEM((4 * cols, depth), BF),
             pltpu.SemaphoreType.DMA((10,)),
         ],
-        compiler_params=pltpu.CompilerParams(vmem_limit_bytes=LARGE),
+        compiler_params=pltpu.CompilerParams(vmem_limit_bytes=STAGE),
         cost_estimate=pl.CostEstimate(flops=2 * 10**10, bytes_accessed=0, transcendentals=0),
         name="stage",
     )(modulation, final_t, *blocks, *got)
 
 
-def project_kernel(a_ref, all_hbm, o_ref, w_ref, hid_ref, tab_ref, lhs_ref, r_ref, sem):
+def project_kernel(a_ref, aux_ref, w_hbm, o_ref, w_ref, r_ref, sem):
     chunks, tokens, depth = a_ref.shape
-    vis = tokens // 4
     part = r_ref.shape[2]
-    patch = 2 * o_ref.shape[1] - 16
-    blocks, hidden, tables = places(part, vis, patch)
-    loads, rest = [], []
-    for k in range(4):
-        w = pltpu.make_async_copy(all_hbm.at[blocks[k]], w_ref.at[k], sem.at[k])
-        h = pltpu.make_async_copy(all_hbm.at[hidden[k]], hid_ref.at[k], sem.at[4 + k])
-        t = pltpu.make_async_copy(all_hbm.at[tables[k]], tab_ref.at[k], sem.at[8 + k])
-        loads.append(w)
-        rest += [h, t]
-    for load in loads + rest:
-        load.start()
-    for i in range(chunks):
-        lhs_ref[:, i * depth : (i + 1) * depth] = a_ref[i]
+    vis, patch = tokens // 4, 2 * o_ref.shape[1] - 16
+    hidden, tables = places(part, vis, patch)
+    loads = []
     for g in range(4):
-        loads[g].wait()
-        r_ref[g] = lax.dot_general(lhs_ref[...], w_ref[g], NT, preferred_element_type=F32)
-    for load in rest:
+        at = slice(g * part, (g + 1) * part)
+        loads.append(pltpu.make_async_copy(w_hbm.at[at], w_ref.at[at], sem.at[g]))
+        loads[g].start()
+    for g in range(4):
+        for k, (rows, c) in enumerate(hidden):
+            h = aux_ref[rows, c.start + g * part : c.start + (g + 1) * part]
+            r_ref[g, k * vis : (k + 1) * vis, :] = h.astype(F32)
+    lhs = jnp.concatenate([a_ref[i] for i in range(chunks)], axis=1)
+    for load in loads:
         load.wait()
     total = 0.0
     for g in range(4):
-        h = jnp.concatenate([hid_ref[k, :, g * part : (g + 1) * part] for k in range(4)], axis=0)
-        gate = tab_ref[g, 2 * patch :, :part].astype(F32)
-        r = h.astype(F32) + (gate[0:1] + gate[1:2] + gate[2:3]) * r_ref[g]
+        w = w_ref[g * part : (g + 1) * part, :]
+        p = lax.dot_general(lhs, w, NT, preferred_element_type=F32)
+        rows, c = tables[g]
+        gate = aux_ref[rows.start + 2 * patch : rows.stop, c.start : c.start + part].astype(F32)
+        r = r_ref[g] + (gate[0:1] + gate[1:2] + gate[2:3]) * p
         r_ref[g] = r
         total = total + r
     mean = jnp.sum(total, axis=1, keepdims=True) * (1.0 / (4 * part))
-    spread = 0.0
-    pred = jnp.zeros((patch, tokens), F32)
+    spread, both, fine = 0.0, 0.0, 0.0
     for g in range(4):
         d = r_ref[g] - mean
         spread = spread + d * d
         hi, lo = split2(d)
-        w_hi, w_lo = tab_ref[g, :patch, :part], tab_ref[g, patch : 2 * patch, :part]
-        pred = pred + lax.dot_general(w_hi, hi, NT, preferred_element_type=F32)
-        pred = pred + lax.dot_general(w_hi, lo, NT, preferred_element_type=F32)
-        pred = pred + lax.dot_general(w_lo, hi, NT, preferred_element_type=F32)
-    spread = jnp.sum(spread, axis=1, keepdims=True)
-    lane = lax.broadcasted_iota(jnp.int32, (tokens, 128), 1)
-    stats = jnp.transpose(jnp.where(lane == 0, mean, spread))[:8]
-    sums = tab_ref[3, :patch, part:].astype(F32)
+        rows, c = tables[g]
+        w = aux_ref[rows.start : rows.start + 2 * patch, c.start : c.start + part]
+        both = both + lax.dot_general(hi, w, NT, preferred_element_type=F32)
+        fine = fine + lax.dot_general(lo, w[:patch], NT, preferred_element_type=F32)
+    pred = both[:, :patch] + both[:, patch:] + fine
+    stats = [mean, jnp.sum(spread, axis=1, keepdims=True), jnp.zeros((tokens, 78), F32)]
+    pred = jnp.transpose(jnp.concatenate([pred, *stats], axis=1))
+    rows, c = tables[3]
+    sums = aux_ref[rows.start : rows.start + patch, c.start + part : c.stop].astype(F32)
     sums = (sums[:, :32] + sums[:, 2:34]) + sums[:, 4:36]
     half = patch // 2
-    for c in range(2):
+    for core in range(2):
         for k in range(4):
             at = slice(k * vis, (k + 1) * vis)
-            rows = slice(c * half, (c + 1) * half)
-            o_ref[c * 4 + k, :half] = jnp.concatenate([pred[rows, at], sums[rows]], axis=1)
-            o_ref[c * 4 + k, half:] = jnp.concatenate([stats[:, at], stats[:, :32]], axis=1)
-
-
-def project(att, staged, patch):
+            rows = slice(core * half, (core + 1) * half)
+            o_ref[core * 4 + k, :half] = jnp.concatenate([pred[rows, at], sums[rows]], axis=1)
+            o_ref[core * 4 + k, half:] = jnp.concatenate(
+                [pred[patch : patch + 8, at], sums[:8]], axis=1
+            )
+
+
+def project(att, aux, weights, patch):
     chunks, tokens, width = att.shape
     depth = chunks * width
-    vis = tokens // 4
-    cols = depth * 3 // 32
+    cols = weights.shape[0] // 4
     return pl.pallas_call(
         project_kernel,
-        in_specs=[WHOLE, ANY],
+        in_specs=[WHOLE, WHOLE, ANY],
         out_specs=WHOLE,
         out_shape=jax.ShapeDtypeStruct((8, patch // 2 + 8, 128), F32),
         scratch_shapes=[
-            pltpu.VMEM((4, cols, depth), BF),
-            pltpu.VMEM((4, vis, 4 * cols), BF),
-            pltpu.VMEM((4, 2 * patch + 16, cols + 64), BF),
-            pltpu.VMEM((tokens, depth), BF),
+            pltpu.VMEM(weights.shape, BF),
             pltpu.VMEM((4, tokens, cols), F32),
-            pltpu.SemaphoreType.DMA((12,)),
+            pltpu.SemaphoreType.DMA((4,)),
         ],
         compiler_params=pltpu.CompilerParams(vmem_limit_bytes=MOST),
         cost_estimate=pl.CostEstimate(
@@ -349,7 +359,7 @@
             transcendentals=0,
         ),
         name="project",
-    )(att, staged)
+    )(att, aux, weights)
 
 
 def update_kernel(step_ref, x_ref, lat_ref, vel_ref, next_ref, den_ref, *, count):
@@ -419,7 +429,8 @@
         return lax.ppermute(block, ("req", "row", "col"), outer)
 
     far = across(own)
-    packed, mine, *sends = pack(vis_qkv, text_kv, vis_hidden)
+    packed, hidden = lax.optimization_barrier((pack(vis_qkv, text_kv), vis_hidden))
+    mine, *sends = share(hidden)
     heads = lax.all_to_all(
         packed, ("row", "col"), split_axis=0, concat_axis=0, tiled=True
     ).reshape(8, 2, 3 * vis + 2 * txt, 128)
@@ -430,11 +441,11 @@
     attended = attend(text_len[0], heads, vis)
     far, modulation, *got = lax.optimization_barrier((far, modulation, *got))
     own_other, far_other = (lax.ppermute(b, "cfg", cores) for b in (own, far))
-    staged = stage(modulation, final_weight.T, [own, far, own_other, far_other], got)
+    aux, weights = stage(modulation, final_weight.T, [own, far, own_other, far_other], got)
     att = lax.all_to_all(
         attended, ("row", "col"), split_axis=0, concat_axis=0, tiled=True
     ).reshape(16, 4 * vis, 128)
-    parts = project(att, staged, final_weight.shape[1])
+    parts = project(att, aux, weights, final_weight.shape[1])
     parts = lax.all_to_all(parts, ("cfg", "col"), split_axis=0, concat_axis=0, tiled=True)
     outs = update(timestep, parts, latent.T, vis_hidden.shape[2])
     return tuple(o.T for o in outs)

time: 73.1 us -> 70.8 us (0.969)
  local copies, waits for them, and re-layouts: 1.54 us -> 4.65 us
  Pallas kernels: 18.2 us -> 15.2 us
  starting transfers between devices: 41.2 us -> 39.2 us
    unnamed x16, local copies, waits for them, and re-layouts: 0.9 us -> 4.64 us
    pallas_call x3 -> x4, Pallas kernels: 14.4 us -> 11.4 us  [the longest x1 5.22 us: project(): pl.pallas_call(project_kernel, in_specs=[WHOLE, WHOLE, ANY], out_specs=WH...]
    all_to_all x1, starting transfers between devices: 6.49 us -> 4.47 us  [shards(): lax.all_to_all(attended, ('row', 'col'), split_axis=0, concat_axis=0, til...]
  transfers between devices with their start and end apart: 9 -> 9, of which waited for: 3 -> 3; matrix products, arithmetic and copies ran while one was open for 1% -> 0% of each run, Pallas kernels for 10% -> 10%
where the time goes in v3:
time: 70.8 us; the launch traced here: 70.1 us
  starting transfers between devices  39.2 us (55%)
  Pallas kernels  15.2 us (21%)
  waiting for transfers between devices  8.85 us (12%)
  local copies, waits for them, and re-layouts  4.65 us (7%)
  between operations  2.12 us (3%)
    ppermute x3, starting transfers between devices, shards(): lax.ppermute(block, 'col', [(c, c ^ d) for c in range(4)])  9.59 us
    ppermute x2, starting transfers between devices, shards(): own_other, far_other = (lax.ppermute(b, 'cfg', cores) for b in (own, far))  6.95 us
    all_to_all x1, starting transfers between devices, shards(): lax.all_to_all(parts, ('cfg', 'col'), split_axis=0, concat_axis=0, tiled=...  6.94 us
    all_to_all x1, starting transfers between devices, shards(): lax.all_to_all(packed, ('row', 'col'), split_axis=0, concat_axis=0, tiled...  6.01 us
    ppermute x1, starting transfers between devices, across(): return lax.ppermute(block, ('req', 'row', 'col'), outer)  5.25 us
    pallas_call x1, Pallas kernels, project(): pl.pallas_call(project_kernel, in_specs=[WHOLE, WHOLE, ANY], out_specs=WH...  5.22 us
    unnamed x16, local copies, waits for them, and re-layouts  4.64 us
    all_to_all x1, waiting for transfers between devices, shards(): lax.all_to_all(parts, ('cfg', 'col'), split_axis=0, concat_axis=0, tiled=...  4.51 us
  transfers between devices with their start and end apart: 9, of which 3 were waited for; matrix products, arithmetic and copies ran while one was open for 0% of the time, Pallas kernels for 10%

profile of v3, /device:TPU:1, one launch (start us, length us, event | category | flops | bytes accessed | tf_op | source)
XLA Modules:
  0.0 70.1 jit_solution(6844385168447982961)
XLA Ops:
  0.6 2.4 %pack.1 = bf16[16,352,128]{2,1,0:T(8,128)(2,1)} custom-call(bf16[1,96,3,16,128]{4,3,2,1,0:T(8,128)(2,1)} %vis_ref.1, bf16[1,32,2,16,128]{4,3,2,1,0:T(8,128)(2,1)} %txt_ref.1), custom_call_target="tpu_custom_call" | custom-call | bytes 2883584 | tf_op jit(solution)/shard_map/pack/pallas_call | solution.py:64
  3.0 0.0 copy-start.2
  3.0 6.0 %all-to-all-start = ((bf16[16,352,128]{2,1,0:T(8,128)(2,1)}), bf16[16,352,128]{2,1,0:T(8,128)(2,1)S(1)}, u32[]{:S(2)}, u32[]{:S(2)}) async-start(bf16[16,352,128]{2,1,0:T(8,128)(2,1)} %pack.1), calls=%async_computation | async-start | bytes 2883584 | tf_op jit(solution)/shard_map/all_to_all | solution.py:434
  9.0 5.2 %collective-permute-start = (bf16[192,2048]{1,0:T(8,128)(2,1)S(1)}, bf16[192,2048]{1,0:T(8,128)(2,1)S(1)}, u32[]{:S(2)}, u32[]{:S(2)}) collective-permute-start(bf16[192,2048]{1,0:T(8,128)(2,1)S(1)} %bitcast.13), channel_id=1, source_target_pairs={{0,388},{1,389},{2,390},{3,391},{4,128},{5,129},{6,130},{7,131},{1... | collective-permute-start | bytes 2359304 | tf_op jit(solution)/shard_map/ppermute | solution.py:429
  14.3 2.1 %share.1 = (bf16[96,768]{1,0:T(8,128)(2,1)}, bf16[96,768]{1,0:T(8,128)(2,1)}, bf16[96,768]{1,0:T(8,128)(2,1)}, bf16[96,768]{1,0:T(8,128)(2,1)}) custom-call(bf16[1,96,3072]{2,1,0:T(8,128)(2,1)} %hid_hbm), custom_call_target="tpu_custom_call" | custom-call | tf_op jit(solution)/shard_map/share/pallas_call | solution.py:105
  16.4 3.1 %collective-permute-start.1 = (bf16[96,768]{1,0:T(8,128)(2,1)}, bf16[96,768]{1,0:T(8,128)(2,1)}, u32[]{:S(2)}, u32[]{:S(2)}) collective-permute-start(bf16[96,768]{1,0:T(8,128)(2,1)} %get-tuple-element.23), channel_id=1, source_target_pairs={{0,1},{1,0},{2,3},{3,2},{4,5},{5,4},{6,7},{7,6},{8,9},{9,8},{10,11... | collective-permute-start | bytes 442376 | tf_op jit(solution)/shard_map/ppermute | solution.py:438
  19.5 4.3 %collective-permute-start.2 = (bf16[96,768]{1,0:T(8,128)(2,1)}, bf16[96,768]{1,0:T(8,128)(2,1)}, u32[]{:S(2)}, u32[]{:S(2)}) collective-permute-start(bf16[96,768]{1,0:T(8,128)(2,1)} %get-tuple-element.24), channel_id=1, source_target_pairs={{0,2},{1,3},{2,0},{3,1},{4,6},{5,7},{6,4},{7,5},{8,10},{9,11},{10,... | collective-permute-start | bytes 442376 | tf_op jit(solution)/shard_map/ppermute | solution.py:438
  23.8 2.2 %collective-permute-start.3 = (bf16[96,768]{1,0:T(8,128)(2,1)}, bf16[96,768]{1,0:T(8,128)(2,1)}, u32[]{:S(2)}, u32[]{:S(2)}) collective-permute-start(bf16[96,768]{1,0:T(8,128)(2,1)} %get-tuple-element.25), channel_id=1, source_target_pairs={{0,3},{1,2},{2,1},{3,0},{4,7},{5,6},{6,5},{7,4},{8,11},{9,10},{10,... | collective-permute-start | bytes 442376 | tf_op jit(solution)/shard_map/ppermute | solution.py:438
  26.7 0.0 all-to-all-done
  26.7 3.1 %attend.1 = bf16[8,2,384,128]{3,2,1,0:T(8,128)(2,1)} custom-call(s32[1]{0:T(128)} %bitcast.9.len_ref, bf16[8,2,352,128]{3,2,1,0:T(8,128)(2,1)S(1)} %bitcast.11), custom_call_target="tpu_custom_call" | custom-call | flops 805306368 | bytes 2228224 | tf_op jit(solution)/shard_map/attend/pallas_call | solution.py:159
  29.8 0.0 copy-start.7
  29.8 4.5 %all-to-all-start.1 = ((bf16[8,2,384,128]{3,2,1,0:T(8,128)(2,1)}), bf16[8,2,384,128]{3,2,1,0:T(8,128)(2,1)S(1)}, u32[]{:S(2)}, u32[]{:S(2)}) async-start(bf16[8,2,384,128]{3,2,1,0:T(8,128)(2,1)} %attend.1), calls=%async_computation.1 | async-start | bytes 3145728 | tf_op jit(solution)/shard_map/all_to_all | solution.py:445
  34.3 5.0 %collective-permute-start.4 = (bf16[192,2048]{1,0:T(8,128)(2,1)S(1)}, bf16[192,2048]{1,0:T(8,128)(2,1)S(1)}, u32[]{:S(2)}, u32[]{:S(2)}) collective-permute-start(bf16[192,2048]{1,0:T(8,128)(2,1)S(1)} %bitcast.14), channel_id=1, source_target_pairs={{0,8},{8,0},{1,9},{9,1},{2,10},{10,2},{3,11},{11,3},{4,12},{12,4},... | collective-permute-start | bytes 2359304 | tf_op jit(solution)/shard_map/ppermute | solution.py:443
  39.3 0.0 collective-permute-done.1.refs_5_
  39.3 0.0 collective-permute-done.2.refs_6_
  39.3 0.0 collective-permute-done.3.refs_7_
  39.4 0.0 collective-permute-done.refs_1_
  39.4 1.9 %collective-permute-start.5 = (bf16[192,2048]{1,0:T(8,128)(2,1)S(1)}, bf16[192,2048]{1,0:T(8,128)(2,1)S(1)}, u32[]{:S(2)}, u32[]{:S(2)}) collective-permute-start(bf16[192,2048]{1,0:T(8,128)(2,1)S(1)} %collective-permute-done.refs_1_), channel_id=1, source_target_pairs={{0,8},{8,0},{1,9},{9,1},{2,10},{10,2},{3,11},{11,3},{4,12},{12,4},... | collective-permute-start | bytes 2359304 | tf_op jit(solution)/shard_map/ppermute | solution.py:443
  41.3 0.9 %copy-done.3 = bf16[192,2048]{1,0:T(8,128)(2,1)} copy-done((bf16[192,2048]{1,0:T(8,128)(2,1)}, bf16[192,2048]{1,0:T(8,128)(2,1)S(1)}, u32[]{:S(2)}) %copy-start.3) | copy-done | bytes 786456
  42.2 0.0 copy-done.7
  42.2 0.0 collective-permute-done.4.refs_2_
  42.2 1.3 %collective-permute-done.5.refs_3_ = bf16[192,2048]{1,0:T(8,128)(2,1)S(1)} collective-permute-done((bf16[192,2048]{1,0:T(8,128)(2,1)S(1)}, bf16[192,2048]{1,0:T(8,128)(2,1)S(1)}, u32[]{:S(2)}, u32[]{:S(2)}) %collective-permute-start.5) | collective-permute-done | bytes 786464 | tf_op jit(solution)/shard_map/ppermute | solution.py:443
  43.5 1.1 %copy-done.4 = bf16[192,2048]{1,0:T(8,128)(2,1)S(1)} copy-done((bf16[192,2048]{1,0:T(8,128)(2,1)S(1)}, bf16[192,2048]{1,0:T(8,128)(2,1)}, u32[]{:S(2)}) %copy-start.4) | copy-done | bytes 786456
  44.7 1.0 %copy-done.5 = bf16[3072,48]{0,1:T(8,128)(2,1)S(1)} copy-done((bf16[3072,48]{0,1:T(8,128)(2,1)S(1)}, bf16[3072,48]{0,1:T(8,128)(2,1)}, u32[]{:S(2)}) %copy-start.5) | copy-done | bytes 294936
  45.6 1.7 %stage.1 = (bf16[224,2048]{1,0:T(8,128)(2,1)S(1)}, bf16[768,2048]{1,0:T(8,128)(2,1)S(1)}) custom-call(f32[1,3,3072]{2,1,0:T(4,128)S(1)} %copy.12.mod_hbm, bf16[48,3072]{1,0:T(8,128)(2,1)S(1)} %bitcast.16, bf16[192,2048]{1,0:T(8,128)(2,1)S(1)} %bitcast.15, bf16[192,2048]{1,0:T(8,128)(2,1)S(1)} %copy-done.4, ...), custom_call_target="tpu_custom_call" | custom-call | flops 20000000000 | tf_op jit(solution)/shard_map/stage/pallas_call | solution.py:268
  47.4 0.0 copy-start
  47.4 1.6 %copy-done = bf16[768,2048]{1,0:T(8,128)(2,1)} copy-done((bf16[768,2048]{1,0:T(8,128)(2,1)}, bf16[768,2048]{1,0:T(8,128)(2,1)S(1)}, u32[]{:S(2)}) %copy-start) | copy-done | bytes 3145752
  49.0 3.0 %all-to-all-done.1 = bf16[8,2,384,128]{3,2,1,0:T(8,128)(2,1)S(1)} async-done(((bf16[8,2,384,128]{3,2,1,0:T(8,128)(2,1)}), bf16[8,2,384,128]{3,2,1,0:T(8,128)(2,1)S(1)}, u32[]{:S(2)}, u32[]{:S(2)}) %all-to-all-start.1) | async-done | bytes 1572896 | tf_op jit(solution)/shard_map/all_to_all | solution.py:445
  52.0 5.2 %project.1 = f32[8,32,128]{2,1,0:T(8,128)} custom-call(bf16[16,384,128]{2,1,0:T(8,128)(2,1)S(1)} %bitcast.10, bf16[224,2048]{1,0:T(8,128)(2,1)S(1)} %get-tuple-element.32.aux_ref, bf16[768,2048]{1,0:T(8,128)(2,1)} %copy-done), custom_call_target="tpu_custom_call" | custom-call | flops 1207959552 | bytes 3145728 | tf_op jit(solution)/shard_map/project/pallas_call | solution.py:345
  57.3 6.9 %all-to-all-start.2 = ((f32[8,32,128]{2,1,0:T(8,128)}), f32[8,32,128]{2,1,0:T(8,128)S(1)}, u32[]{:S(2)}, u32[]{:S(2)}) async-start(f32[8,32,128]{2,1,0:T(8,128)} %project.1), calls=%async_computation.2 | async-start | bytes 262144 | tf_op jit(solution)/shard_map/all_to_all | solution.py:449
  64.9 4.5 %all-to-all-done.2.x_ref = f32[8,32,128]{2,1,0:T(8,128)S(1)} async-done(((f32[8,32,128]{2,1,0:T(8,128)}), f32[8,32,128]{2,1,0:T(8,128)S(1)}, u32[]{:S(2)}, u32[]{:S(2)}) %all-to-all-start.2) | async-done | bytes 131104 | tf_op jit(solution)/shard_map/all_to_all | solution.py:449
  69.4 0.7 %update.1 = (f32[24,96]{1,0:T(8,128)}, f32[24,96]{1,0:T(8,128)}, f32[24,96]{1,0:T(8,128)}) custom-call(s32[1]{0:T(128)S(6)} %copy.14.step_ref, f32[8,32,128]{2,1,0:T(8,128)S(1)} %all-to-all-done.2.x_ref, f32[24,96]{1,0:T(8,128)S(1)} %bitcast.12), custom_call_target="tpu_custom_call" | custom-call | tf_op jit(solution)/shard_map/update/pallas_call | solution.py:393
  (9 shorter events, 0.0 us)
Async XLA Ops:
  3.0 6.0 %copy-start.2 = (bf16[2048,192]{0,1:T(8,128)(2,1)S(1)}, bf16[2048,192]{0,1:T(8,128)(2,1)}, u32[]{:S(2)}) copy-start(bf16[2048,192]{0,1:T(8,128)(2,1)} %param.13) | copy-start | bytes 2359300
  3.0 23.7 %all-to-all-start = ((bf16[16,352,128]{2,1,0:T(8,128)(2,1)}), bf16[16,352,128]{2,1,0:T(8,128)(2,1)S(1)}, u32[]{:S(2)}, u32[]{:S(2)}) async-start(bf16[16,352,128]{2,1,0:T(8,128)(2,1)} %pack.1), calls=%async_computation | async-start | bytes 2883584 | tf_op jit(solution)/shard_map/all_to_all | solution.py:434
  9.0 30.3 %collective-permute-start = (bf16[192,2048]{1,0:T(8,128)(2,1)S(1)}, bf16[192,2048]{1,0:T(8,128)(2,1)S(1)}, u32[]{:S(2)}, u32[]{:S(2)}) collective-permute-start(bf16[192,2048]{1,0:T(8,128)(2,1)S(1)} %bitcast.13), channel_id=1, source_target_pairs={{0,388},{1,389},{2,390},{3,391},{4,128},{5,129},{6,130},{7,131},{1... | collective-permute-start | bytes 2359304 | tf_op jit(solution)/shard_map/ppermute | solution.py:429
  16.4 22.9 %collective-permute-start.1 = (bf16[96,768]{1,0:T(8,128)(2,1)}, bf16[96,768]{1,0:T(8,128)(2,1)}, u32[]{:S(2)}, u32[]{:S(2)}) collective-permute-start(bf16[96,768]{1,0:T(8,128)(2,1)} %get-tuple-element.23), channel_id=1, source_target_pairs={{0,1},{1,0},{2,3},{3,2},{4,5},{5,4},{6,7},{7,6},{8,9},{9,8},{10,11... | collective-permute-start | bytes 442376 | tf_op jit(solution)/shard_map/ppermute | solution.py:438
  19.5 19.8 %collective-permute-start.2 = (bf16[96,768]{1,0:T(8,128)(2,1)}, bf16[96,768]{1,0:T(8,128)(2,1)}, u32[]{:S(2)}, u32[]{:S(2)}) collective-permute-start(bf16[96,768]{1,0:T(8,128)(2,1)} %get-tuple-element.24), channel_id=1, source_target_pairs={{0,2},{1,3},{2,0},{3,1},{4,6},{5,7},{6,4},{7,5},{8,10},{9,11},{10,... | collective-permute-start | bytes 442376 | tf_op jit(solution)/shard_map/ppermute | solution.py:438
  23.8 15.5 %collective-permute-start.3 = (bf16[96,768]{1,0:T(8,128)(2,1)}, bf16[96,768]{1,0:T(8,128)(2,1)}, u32[]{:S(2)}, u32[]{:S(2)}) collective-permute-start(bf16[96,768]{1,0:T(8,128)(2,1)} %get-tuple-element.25), channel_id=1, source_target_pairs={{0,3},{1,2},{2,1},{3,0},{4,7},{5,6},{6,5},{7,4},{8,11},{9,10},{10,... | collective-permute-start | bytes 442376 | tf_op jit(solution)/shard_map/ppermute | solution.py:438
  29.8 12.4 %copy-start.7 = (f32[1,3,3072]{2,0,1:T(1,128)S(1)}, f32[1,3,3072]{2,0,1:T(1,128)}, u32[]{:S(2)}) copy-start(f32[1,3,3072]{2,0,1:T(1,128)} %param.14) | copy-start | bytes 110596
  29.8 13.7 %copy-start.6 = (bf16[96,768]{1,0:T(8,128)(2,1)S(1)}, bf16[96,768]{1,0:T(8,128)(2,1)}, u32[]{:S(2)}) copy-start(bf16[96,768]{1,0:T(8,128)(2,1)} %get-tuple-element.28.refs_4_) | copy-start | bytes 442372
  29.8 22.2 %all-to-all-start.1 = ((bf16[8,2,384,128]{3,2,1,0:T(8,128)(2,1)}), bf16[8,2,384,128]{3,2,1,0:T(8,128)(2,1)S(1)}, u32[]{:S(2)}, u32[]{:S(2)}) async-start(bf16[8,2,384,128]{3,2,1,0:T(8,128)(2,1)} %attend.1), calls=%async_computation.1 | async-start | bytes 3145728 | tf_op jit(solution)/shard_map/all_to_all | solution.py:445
  34.3 7.9 %collective-permute-start.4 = (bf16[192,2048]{1,0:T(8,128)(2,1)S(1)}, bf16[192,2048]{1,0:T(8,128)(2,1)S(1)}, u32[]{:S(2)}, u32[]{:S(2)}) collective-permute-start(bf16[192,2048]{1,0:T(8,128)(2,1)S(1)} %bitcast.14), channel_id=1, source_target_pairs={{0,8},{8,0},{1,9},{9,1},{2,10},{10,2},{3,11},{11,3},{4,12},{12,4},... | collective-permute-start | bytes 2359304 | tf_op jit(solution)/shard_map/ppermute | solution.py:443
  39.4 4.2 %collective-permute-start.5 = (bf16[192,2048]{1,0:T(8,128)(2,1)S(1)}, bf16[192,2048]{1,0:T(8,128)(2,1)S(1)}, u32[]{:S(2)}, u32[]{:S(2)}) collective-permute-start(bf16[192,2048]{1,0:T(8,128)(2,1)S(1)} %collective-permute-done.refs_1_), channel_id=1, source_target_pairs={{0,8},{8,0},{1,9},{9,1},{2,10},{10,2},{3,11},{11,3},{4,12},{12,4},... | collective-permute-start | bytes 2359304 | tf_op jit(solution)/shard_map/ppermute | solution.py:443
  41.3 0.9 %copy-start.3 = (bf16[192,2048]{1,0:T(8,128)(2,1)}, bf16[192,2048]{1,0:T(8,128)(2,1)S(1)}, u32[]{:S(2)}) copy-start(bf16[192,2048]{1,0:T(8,128)(2,1)S(1)} %collective-permute-done.refs_1_) | copy-start | bytes 2359300
  43.5 1.1 %copy-start.4 = (bf16[192,2048]{1,0:T(8,128)(2,1)S(1)}, bf16[192,2048]{1,0:T(8,128)(2,1)}, u32[]{:S(2)}) copy-start(bf16[192,2048]{1,0:T(8,128)(2,1)} %copy-done.3) | copy-start | bytes 2359300
  44.7 1.0 %copy-start.5 = (bf16[3072,48]{0,1:T(8,128)(2,1)S(1)}, bf16[3072,48]{0,1:T(8,128)(2,1)}, u32[]{:S(2)}) copy-start(bf16[3072,48]{0,1:T(8,128)(2,1)} %param.15) | copy-start | bytes 884740
  47.4 1.6 %copy-start = (bf16[768,2048]{1,0:T(8,128)(2,1)}, bf16[768,2048]{1,0:T(8,128)(2,1)S(1)}, u32[]{:S(2)}) copy-start(bf16[768,2048]{1,0:T(8,128)(2,1)S(1)} %get-tuple-element.33.w_hbm) | copy-start | bytes 9437188
  52.0 17.3 %copy-start.1 = (f32[96,24]{0,1:T(8,128)S(1)}, f32[96,24]{0,1:T(8,128)}, u32[]{:S(2)}) copy-start(f32[96,24]{0,1:T(8,128)} %param.16) | copy-start | bytes 27652
  57.3 12.1 %all-to-all-start.2 = ((f32[8,32,128]{2,1,0:T(8,128)}), f32[8,32,128]{2,1,0:T(8,128)S(1)}, u32[]{:S(2)}, u32[]{:S(2)}) async-start(f32[8,32,128]{2,1,0:T(8,128)} %project.1), calls=%async_computation.2 | async-start | bytes 262144 | tf_op jit(solution)/shard_map/all_to_all | solution.py:449

commit v4 on v3

--- a/solution.py
+++ b/solution.py
@@ -300,10 +300,11 @@
             h = aux_ref[rows, c.start + g * part : c.start + (g + 1) * part]
             r_ref[g, k * vis : (k + 1) * vis, :] = h.astype(F32)
     lhs = jnp.concatenate([a_ref[i] for i in range(chunks)], axis=1)
-    for load in loads:
-        load.wait()
     total = 0.0
     for g in range(4):
+        if g % 2 == 0:
+            loads[g].wait()
+            loads[g + 1].wait()
         w = w_ref[g * part : (g + 1) * part, :]
         p = lax.dot_general(lhs, w, NT, preferred_element_type=F32)
         rows, c = tables[g]

time: 70.8 us -> 70.5 us (level)
  no operation moved by 1% of the time
where the time goes in v4:
time: 70.5 us; the launch traced here: 69.8 us
  starting transfers between devices  39.2 us (56%)
  Pallas kernels  15 us (21%)
  waiting for transfers between devices  8.85 us (13%)
  local copies, waits for them, and re-layouts  4.65 us (7%)
  between operations  2.12 us (3%)
    ppermute x3, starting transfers between devices, shards(): lax.ppermute(block, 'col', [(c, c ^ d) for c in range(4)])  9.59 us
    ppermute x2, starting transfers between devices, shards(): own_other, far_other = (lax.ppermute(b, 'cfg', cores) for b in (own, far))  6.95 us
    all_to_all x1, starting transfers between devices, shards(): lax.all_to_all(parts, ('cfg', 'col'), split_axis=0, concat_axis=0, tiled=...  6.94 us
    all_to_all x1, starting transfers between devices, shards(): lax.all_to_all(packed, ('row', 'col'), split_axis=0, concat_axis=0, tiled...  6.01 us
    ppermute x1, starting transfers between devices, across(): return lax.ppermute(block, ('req', 'row', 'col'), outer)  5.25 us
    pallas_call x1, Pallas kernels, project(): pl.pallas_call(project_kernel, in_specs=[WHOLE, WHOLE, ANY], out_specs=WH...  4.93 us
    unnamed x16, local copies, waits for them, and re-layouts  4.64 us
    all_to_all x1, waiting for transfers between devices, shards(): lax.all_to_all(parts, ('cfg', 'col'), split_axis=0, concat_axis=0, tiled=...  4.51 us
  transfers between devices with their start and end apart: 9, of which 3 were waited for; matrix products, arithmetic and copies ran while one was open for 0% of the time, Pallas kernels for 10%

profile of v4, /device:TPU:1, one launch (start us, length us, event | category | flops | bytes accessed | tf_op | source)
XLA Modules:
  0.0 69.8 jit_solution(13281296494924445265)
XLA Ops:
  0.6 2.4 %pack.1 = bf16[16,352,128]{2,1,0:T(8,128)(2,1)} custom-call(bf16[1,96,3,16,128]{4,3,2,1,0:T(8,128)(2,1)} %vis_ref.1, bf16[1,32,2,16,128]{4,3,2,1,0:T(8,128)(2,1)} %txt_ref.1), custom_call_target="tpu_custom_call" | custom-call | bytes 2883584 | tf_op jit(solution)/shard_map/pack/pallas_call | solution.py:64
  3.0 0.0 copy-start.2
  3.0 6.0 %all-to-all-start = ((bf16[16,352,128]{2,1,0:T(8,128)(2,1)}), bf16[16,352,128]{2,1,0:T(8,128)(2,1)S(1)}, u32[]{:S(2)}, u32[]{:S(2)}) async-start(bf16[16,352,128]{2,1,0:T(8,128)(2,1)} %pack.1), calls=%async_computation | async-start | bytes 2883584 | tf_op jit(solution)/shard_map/all_to_all | solution.py:435
  9.0 0.0 copy-done.2
  9.0 5.2 %collective-permute-start = (bf16[192,2048]{1,0:T(8,128)(2,1)S(1)}, bf16[192,2048]{1,0:T(8,128)(2,1)S(1)}, u32[]{:S(2)}, u32[]{:S(2)}) collective-permute-start(bf16[192,2048]{1,0:T(8,128)(2,1)S(1)} %bitcast.13), channel_id=1, source_target_pairs={{0,388},{1,389},{2,390},{3,391},{4,128},{5,129},{6,130},{7,131},{1... | collective-permute-start | bytes 2359304 | tf_op jit(solution)/shard_map/ppermute | solution.py:430
  14.3 2.1 %share.1 = (bf16[96,768]{1,0:T(8,128)(2,1)}, bf16[96,768]{1,0:T(8,128)(2,1)}, bf16[96,768]{1,0:T(8,128)(2,1)}, bf16[96,768]{1,0:T(8,128)(2,1)}) custom-call(bf16[1,96,3072]{2,1,0:T(8,128)(2,1)} %hid_hbm), custom_call_target="tpu_custom_call" | custom-call | tf_op jit(solution)/shard_map/share/pallas_call | solution.py:105
  16.4 3.1 %collective-permute-start.1 = (bf16[96,768]{1,0:T(8,128)(2,1)}, bf16[96,768]{1,0:T(8,128)(2,1)}, u32[]{:S(2)}, u32[]{:S(2)}) collective-permute-start(bf16[96,768]{1,0:T(8,128)(2,1)} %get-tuple-element.23), channel_id=1, source_target_pairs={{0,1},{1,0},{2,3},{3,2},{4,5},{5,4},{6,7},{7,6},{8,9},{9,8},{10,11... | collective-permute-start | bytes 442376 | tf_op jit(solution)/shard_map/ppermute | solution.py:439
  19.5 4.3 %collective-permute-start.2 = (bf16[96,768]{1,0:T(8,128)(2,1)}, bf16[96,768]{1,0:T(8,128)(2,1)}, u32[]{:S(2)}, u32[]{:S(2)}) collective-permute-start(bf16[96,768]{1,0:T(8,128)(2,1)} %get-tuple-element.24), channel_id=1, source_target_pairs={{0,2},{1,3},{2,0},{3,1},{4,6},{5,7},{6,4},{7,5},{8,10},{9,11},{10,... | collective-permute-start | bytes 442376 | tf_op jit(solution)/shard_map/ppermute | solution.py:439
  23.8 2.2 %collective-permute-start.3 = (bf16[96,768]{1,0:T(8,128)(2,1)}, bf16[96,768]{1,0:T(8,128)(2,1)}, u32[]{:S(2)}, u32[]{:S(2)}) collective-permute-start(bf16[96,768]{1,0:T(8,128)(2,1)} %get-tuple-element.25), channel_id=1, source_target_pairs={{0,3},{1,2},{2,1},{3,0},{4,7},{5,6},{6,5},{7,4},{8,11},{9,10},{10,... | collective-permute-start | bytes 442376 | tf_op jit(solution)/shard_map/ppermute | solution.py:439
  26.7 0.0 all-to-all-done
  26.7 3.1 %attend.1 = bf16[8,2,384,128]{3,2,1,0:T(8,128)(2,1)} custom-call(s32[1]{0:T(128)} %bitcast.9.len_ref, bf16[8,2,352,128]{3,2,1,0:T(8,128)(2,1)S(1)} %bitcast.11), custom_call_target="tpu_custom_call" | custom-call | flops 805306368 | bytes 2228224 | tf_op jit(solution)/shard_map/attend/pallas_call | solution.py:159
  29.8 0.0 copy-start.7
  29.8 4.5 %all-to-all-start.1 = ((bf16[8,2,384,128]{3,2,1,0:T(8,128)(2,1)}), bf16[8,2,384,128]{3,2,1,0:T(8,128)(2,1)S(1)}, u32[]{:S(2)}, u32[]{:S(2)}) async-start(bf16[8,2,384,128]{3,2,1,0:T(8,128)(2,1)} %attend.1), calls=%async_computation.1 | async-start | bytes 3145728 | tf_op jit(solution)/shard_map/all_to_all | solution.py:446
  34.3 5.0 %collective-permute-start.4 = (bf16[192,2048]{1,0:T(8,128)(2,1)S(1)}, bf16[192,2048]{1,0:T(8,128)(2,1)S(1)}, u32[]{:S(2)}, u32[]{:S(2)}) collective-permute-start(bf16[192,2048]{1,0:T(8,128)(2,1)S(1)} %bitcast.14), channel_id=1, source_target_pairs={{0,8},{8,0},{1,9},{9,1},{2,10},{10,2},{3,11},{11,3},{4,12},{12,4},... | collective-permute-start | bytes 2359304 | tf_op jit(solution)/shard_map/ppermute | solution.py:444
  39.3 0.0 collective-permute-done.1.refs_5_
  39.3 0.0 collective-permute-done.2.refs_6_
  39.3 0.0 collective-permute-done.3.refs_7_
  39.4 0.0 collective-permute-done.refs_1_
  39.4 1.9 %collective-permute-start.5 = (bf16[192,2048]{1,0:T(8,128)(2,1)S(1)}, bf16[192,2048]{1,0:T(8,128)(2,1)S(1)}, u32[]{:S(2)}, u32[]{:S(2)}) collective-permute-start(bf16[192,2048]{1,0:T(8,128)(2,1)S(1)} %collective-permute-done.refs_1_), channel_id=1, source_target_pairs={{0,8},{8,0},{1,9},{9,1},{2,10},{10,2},{3,11},{11,3},{4,12},{12,4},... | collective-permute-start | bytes 2359304 | tf_op jit(solution)/shard_map/ppermute | solution.py:444
  41.3 0.0 copy-start.3
  41.3 0.9 %copy-done.3 = bf16[192,2048]{1,0:T(8,128)(2,1)} copy-done((bf16[192,2048]{1,0:T(8,128)(2,1)}, bf16[192,2048]{1,0:T(8,128)(2,1)S(1)}, u32[]{:S(2)}) %copy-start.3) | copy-done | bytes 786456
  42.2 0.0 collective-permute-done.4.refs_2_
  42.2 1.3 %collective-permute-done.5.refs_3_ = bf16[192,2048]{1,0:T(8,128)(2,1)S(1)} collective-permute-done((bf16[192,2048]{1,0:T(8,128)(2,1)S(1)}, bf16[192,2048]{1,0:T(8,128)(2,1)S(1)}, u32[]{:S(2)}, u32[]{:S(2)}) %collective-permute-start.5) | collective-permute-done | bytes 786464 | tf_op jit(solution)/shard_map/ppermute | solution.py:444
  43.5 1.1 %copy-done.4 = bf16[192,2048]{1,0:T(8,128)(2,1)S(1)} copy-done((bf16[192,2048]{1,0:T(8,128)(2,1)S(1)}, bf16[192,2048]{1,0:T(8,128)(2,1)}, u32[]{:S(2)}) %copy-start.4) | copy-done | bytes 786456
  44.7 1.0 %copy-done.5 = bf16[3072,48]{0,1:T(8,128)(2,1)S(1)} copy-done((bf16[3072,48]{0,1:T(8,128)(2,1)S(1)}, bf16[3072,48]{0,1:T(8,128)(2,1)}, u32[]{:S(2)}) %copy-start.5) | copy-done | bytes 294936
  45.6 1.7 %stage.1 = (bf16[224,2048]{1,0:T(8,128)(2,1)S(1)}, bf16[768,2048]{1,0:T(8,128)(2,1)S(1)}) custom-call(f32[1,3,3072]{2,1,0:T(4,128)S(1)} %copy.12.mod_hbm, bf16[48,3072]{1,0:T(8,128)(2,1)S(1)} %bitcast.16, bf16[192,2048]{1,0:T(8,128)(2,1)S(1)} %bitcast.15, bf16[192,2048]{1,0:T(8,128)(2,1)S(1)} %copy-done.4, ...), custom_call_target="tpu_custom_call" | custom-call | flops 20000000000 | tf_op jit(solution)/shard_map/stage/pallas_call | solution.py:268
  47.4 1.6 %copy-done = bf16[768,2048]{1,0:T(8,128)(2,1)} copy-done((bf16[768,2048]{1,0:T(8,128)(2,1)}, bf16[768,2048]{1,0:T(8,128)(2,1)S(1)}, u32[]{:S(2)}) %copy-start) | copy-done | bytes 3145752
  49.0 3.0 %all-to-all-done.1 = bf16[8,2,384,128]{3,2,1,0:T(8,128)(2,1)S(1)} async-done(((bf16[8,2,384,128]{3,2,1,0:T(8,128)(2,1)}), bf16[8,2,384,128]{3,2,1,0:T(8,128)(2,1)S(1)}, u32[]{:S(2)}, u32[]{:S(2)}) %all-to-all-start.1) | async-done | bytes 1572896 | tf_op jit(solution)/shard_map/all_to_all | solution.py:446
  52.0 4.9 %project.1 = f32[8,32,128]{2,1,0:T(8,128)} custom-call(bf16[16,384,128]{2,1,0:T(8,128)(2,1)S(1)} %bitcast.10, bf16[224,2048]{1,0:T(8,128)(2,1)S(1)} %get-tuple-element.32.aux_ref, bf16[768,2048]{1,0:T(8,128)(2,1)} %copy-done), custom_call_target="tpu_custom_call" | custom-call | flops 1207959552 | bytes 3145728 | tf_op jit(solution)/shard_map/project/pallas_call | solution.py:346
  57.0 6.9 %all-to-all-start.2 = ((f32[8,32,128]{2,1,0:T(8,128)}), f32[8,32,128]{2,1,0:T(8,128)S(1)}, u32[]{:S(2)}, u32[]{:S(2)}) async-start(f32[8,32,128]{2,1,0:T(8,128)} %project.1), calls=%async_computation.2 | async-start | bytes 262144 | tf_op jit(solution)/shard_map/all_to_all | solution.py:450
  64.6 4.5 %all-to-all-done.2.x_ref = f32[8,32,128]{2,1,0:T(8,128)S(1)} async-done(((f32[8,32,128]{2,1,0:T(8,128)}), f32[8,32,128]{2,1,0:T(8,128)S(1)}, u32[]{:S(2)}, u32[]{:S(2)}) %all-to-all-start.2) | async-done | bytes 131104 | tf_op jit(solution)/shard_map/all_to_all | solution.py:450
  69.1 0.7 %update.1 = (f32[24,96]{1,0:T(8,128)}, f32[24,96]{1,0:T(8,128)}, f32[24,96]{1,0:T(8,128)}) custom-call(s32[1]{0:T(128)S(6)} %copy.14.step_ref, f32[8,32,128]{2,1,0:T(8,128)S(1)} %all-to-all-done.2.x_ref, f32[24,96]{1,0:T(8,128)S(1)} %bitcast.12), custom_call_target="tpu_custom_call" | custom-call | tf_op jit(solution)/shard_map/update/pallas_call | solution.py:394
  (9 shorter events, 0.0 us)
Async XLA Ops:
  3.0 6.0 %copy-start.2 = (bf16[2048,192]{0,1:T(8,128)(2,1)S(1)}, bf16[2048,192]{0,1:T(8,128)(2,1)}, u32[]{:S(2)}) copy-start(bf16[2048,192]{0,1:T(8,128)(2,1)} %param.13) | copy-start | bytes 2359300
  3.0 23.7 %all-to-all-start = ((bf16[16,352,128]{2,1,0:T(8,128)(2,1)}), bf16[16,352,128]{2,1,0:T(8,128)(2,1)S(1)}, u32[]{:S(2)}, u32[]{:S(2)}) async-start(bf16[16,352,128]{2,1,0:T(8,128)(2,1)} %pack.1), calls=%async_computation | async-start | bytes 2883584 | tf_op jit(solution)/shard_map/all_to_all | solution.py:435
  9.0 30.3 %collective-permute-start = (bf16[192,2048]{1,0:T(8,128)(2,1)S(1)}, bf16[192,2048]{1,0:T(8,128)(2,1)S(1)}, u32[]{:S(2)}, u32[]{:S(2)}) collective-permute-start(bf16[192,2048]{1,0:T(8,128)(2,1)S(1)} %bitcast.13), channel_id=1, source_target_pairs={{0,388},{1,389},{2,390},{3,391},{4,128},{5,129},{6,130},{7,131},{1... | collective-permute-start | bytes 2359304 | tf_op jit(solution)/shard_map/ppermute | solution.py:430
  16.4 22.9 %collective-permute-start.1 = (bf16[96,768]{1,0:T(8,128)(2,1)}, bf16[96,768]{1,0:T(8,128)(2,1)}, u32[]{:S(2)}, u32[]{:S(2)}) collective-permute-start(bf16[96,768]{1,0:T(8,128)(2,1)} %get-tuple-element.23), channel_id=1, source_target_pairs={{0,1},{1,0},{2,3},{3,2},{4,5},{5,4},{6,7},{7,6},{8,9},{9,8},{10,11... | collective-permute-start | bytes 442376 | tf_op jit(solution)/shard_map/ppermute | solution.py:439
  19.5 19.8 %collective-permute-start.2 = (bf16[96,768]{1,0:T(8,128)(2,1)}, bf16[96,768]{1,0:T(8,128)(2,1)}, u32[]{:S(2)}, u32[]{:S(2)}) collective-permute-start(bf16[96,768]{1,0:T(8,128)(2,1)} %get-tuple-element.24), channel_id=1, source_target_pairs={{0,2},{1,3},{2,0},{3,1},{4,6},{5,7},{6,4},{7,5},{8,10},{9,11},{10,... | collective-permute-start | bytes 442376 | tf_op jit(solution)/shard_map/ppermute | solution.py:439
  23.8 15.5 %collective-permute-start.3 = (bf16[96,768]{1,0:T(8,128)(2,1)}, bf16[96,768]{1,0:T(8,128)(2,1)}, u32[]{:S(2)}, u32[]{:S(2)}) collective-permute-start(bf16[96,768]{1,0:T(8,128)(2,1)} %get-tuple-element.25), channel_id=1, source_target_pairs={{0,3},{1,2},{2,1},{3,0},{4,7},{5,6},{6,5},{7,4},{8,11},{9,10},{10,... | collective-permute-start | bytes 442376 | tf_op jit(solution)/shard_map/ppermute | solution.py:439
  29.8 12.4 %copy-start.7 = (f32[1,3,3072]{2,0,1:T(1,128)S(1)}, f32[1,3,3072]{2,0,1:T(1,128)}, u32[]{:S(2)}) copy-start(f32[1,3,3072]{2,0,1:T(1,128)} %param.14) | copy-start | bytes 110596
  29.8 13.7 %copy-start.6 = (bf16[96,768]{1,0:T(8,128)(2,1)S(1)}, bf16[96,768]{1,0:T(8,128)(2,1)}, u32[]{:S(2)}) copy-start(bf16[96,768]{1,0:T(8,128)(2,1)} %get-tuple-element.28.refs_4_) | copy-start | bytes 442372
  29.8 22.2 %all-to-all-start.1 = ((bf16[8,2,384,128]{3,2,1,0:T(8,128)(2,1)}), bf16[8,2,384,128]{3,2,1,0:T(8,128)(2,1)S(1)}, u32[]{:S(2)}, u32[]{:S(2)}) async-start(bf16[8,2,384,128]{3,2,1,0:T(8,128)(2,1)} %attend.1), calls=%async_computation.1 | async-start | bytes 3145728 | tf_op jit(solution)/shard_map/all_to_all | solution.py:446
  34.3 7.9 %collective-permute-start.4 = (bf16[192,2048]{1,0:T(8,128)(2,1)S(1)}, bf16[192,2048]{1,0:T(8,128)(2,1)S(1)}, u32[]{:S(2)}, u32[]{:S(2)}) collective-permute-start(bf16[192,2048]{1,0:T(8,128)(2,1)S(1)} %bitcast.14), channel_id=1, source_target_pairs={{0,8},{8,0},{1,9},{9,1},{2,10},{10,2},{3,11},{11,3},{4,12},{12,4},... | collective-permute-start | bytes 2359304 | tf_op jit(solution)/shard_map/ppermute | solution.py:444
  39.4 4.2 %collective-permute-start.5 = (bf16[192,2048]{1,0:T(8,128)(2,1)S(1)}, bf16[192,2048]{1,0:T(8,128)(2,1)S(1)}, u32[]{:S(2)}, u32[]{:S(2)}) collective-permute-start(bf16[192,2048]{1,0:T(8,128)(2,1)S(1)} %collective-permute-done.refs_1_), channel_id=1, source_target_pairs={{0,8},{8,0},{1,9},{9,1},{2,10},{10,2},{3,11},{11,3},{4,12},{12,4},... | collective-permute-start | bytes 2359304 | tf_op jit(solution)/shard_map/ppermute | solution.py:444
  41.3 0.9 %copy-start.3 = (bf16[192,2048]{1,0:T(8,128)(2,1)}, bf16[192,2048]{1,0:T(8,128)(2,1)S(1)}, u32[]{:S(2)}) copy-start(bf16[192,2048]{1,0:T(8,128)(2,1)S(1)} %collective-permute-done.refs_1_) | copy-start | bytes 2359300
  43.5 1.1 %copy-start.4 = (bf16[192,2048]{1,0:T(8,128)(2,1)S(1)}, bf16[192,2048]{1,0:T(8,128)(2,1)}, u32[]{:S(2)}) copy-start(bf16[192,2048]{1,0:T(8,128)(2,1)} %copy-done.3) | copy-start | bytes 2359300
  44.7 1.0 %copy-start.5 = (bf16[3072,48]{0,1:T(8,128)(2,1)S(1)}, bf16[3072,48]{0,1:T(8,128)(2,1)}, u32[]{:S(2)}) copy-start(bf16[3072,48]{0,1:T(8,128)(2,1)} %param.15) | copy-start | bytes 884740
  47.4 1.6 %copy-start = (bf16[768,2048]{1,0:T(8,128)(2,1)}, bf16[768,2048]{1,0:T(8,128)(2,1)S(1)}, u32[]{:S(2)}) copy-start(bf16[768,2048]{1,0:T(8,128)(2,1)S(1)} %get-tuple-element.33.w_hbm) | copy-start | bytes 9437188
  52.0 17.0 %copy-start.1 = (f32[96,24]{0,1:T(8,128)S(1)}, f32[96,24]{0,1:T(8,128)}, u32[]{:S(2)}) copy-start(f32[96,24]{0,1:T(8,128)} %param.16) | copy-start | bytes 27652
  57.0 12.1 %all-to-all-start.2 = ((f32[8,32,128]{2,1,0:T(8,128)}), f32[8,32,128]{2,1,0:T(8,128)S(1)}, u32[]{:S(2)}, u32[]{:S(2)}) async-start(f32[8,32,128]{2,1,0:T(8,128)} %project.1), calls=%async_computation.2 | async-start | bytes 262144 | tf_op jit(solution)/shard_map/all_to_all | solution.py:450

commit v5 on v4

--- a/solution.py
+++ b/solution.py
@@ -108,7 +108,7 @@
         out_specs=[WHOLE] * 4,
         out_shape=[jax.ShapeDtypeStruct((vis, width // 4), BF)] * 4,
         scratch_shapes=[pltpu.VMEM((vis, width), BF), pltpu.SemaphoreType.DMA],
-        compiler_params=pltpu.CompilerParams(vmem_limit_bytes=LARGE),
+        compiler_params=pltpu.CompilerParams(vmem_limit_bytes=STAGE),
         name="share",
     )(hidden)
 
@@ -279,7 +279,7 @@
             pltpu.VMEM((4 * cols, depth), BF),
             pltpu.SemaphoreType.DMA((10,)),
         ],
-        compiler_params=pltpu.CompilerParams(vmem_limit_bytes=STAGE),
+        compiler_params=pltpu.CompilerParams(vmem_limit_bytes=48 << 20),
         cost_estimate=pl.CostEstimate(flops=2 * 10**10, bytes_accessed=0, transcendentals=0),
         name="stage",
     )(modulation, final_t, *blocks, *got)

time: 70.5 us -> 70.5 us (level)
  waiting for transfers between devices: 8.85 us -> 6.94 us
  starting transfers between devices: 39.2 us -> 40.5 us
  local copies, waits for them, and re-layouts: 4.65 us -> 5.69 us
    all_to_all x1, waiting for transfers between devices: 3 us -> 0.01 us  [shards(): lax.all_to_all(attended, ('row', 'col'), split_axis=0, concat_axis=0, til...]
    pallas_call x1, Pallas kernels: 2.13 us -> 0.38 us  [share(): pl.pallas_call(share_kernel, in_specs=[ANY], out_specs=[WHOLE] * 4, out_s...]
    all_to_all x1, starting transfers between devices: 4.47 us -> 6.19 us  [shards(): lax.all_to_all(attended, ('row', 'col'), split_axis=0, concat_axis=0, til...]
    pallas_call x1, Pallas kernels: 1.72 us -> 2.99 us  [stage(): pl.pallas_call(stage_kernel, in_specs=[ANY] * 10, out_specs=[WHOLE, ANY],...]
    ppermute x2, waiting for transfers between devices: 1.33 us -> 2.42 us  [shards(): own_other, far_other = (lax.ppermute(b, 'cfg', cores) for b in (own, far))]
    unnamed x16 -> x22, local copies, waits for them, and re-layouts: 4.64 us -> 5.67 us
  transfers between devices with their start and end apart: 9 -> 9, of which waited for: 3 -> 2; matrix products, arithmetic and copies ran while one was open for 0% -> 0% of each run, Pallas kernels for 10% -> 9%
where the time goes in v5:
time: 70.5 us; the launch traced here: 69.8 us
  starting transfers between devices  40.5 us (57%)
  Pallas kernels  14.5 us (21%)
  waiting for transfers between devices  6.94 us (10%)
  local copies, waits for them, and re-layouts  5.69 us (8%)
  between operations  2.12 us (3%)
    ppermute x3, starting transfers between devices, shards(): lax.ppermute(block, 'col', [(c, c ^ d) for c in range(4)])  9.58 us
    ppermute x2, starting transfers between devices, shards(): own_other, far_other = (lax.ppermute(b, 'cfg', cores) for b in (own, far))  6.84 us
    all_to_all x1, starting transfers between devices, shards(): lax.all_to_all(parts, ('cfg', 'col'), split_axis=0, concat_axis=0, tiled=...  6.65 us
    all_to_all x1, starting transfers between devices, shards(): lax.all_to_all(attended, ('row', 'col'), split_axis=0, concat_axis=0, til...  6.19 us
    all_to_all x1, starting transfers between devices, shards(): lax.all_to_all(packed, ('row', 'col'), split_axis=0, concat_axis=0, tiled...  6.01 us
    unnamed x22, local copies, waits for them, and re-layouts  5.67 us
    ppermute x1, starting transfers between devices, across(): return lax.ppermute(block, ('req', 'row', 'col'), outer)  5.25 us
    pallas_call x1, Pallas kernels, project(): pl.pallas_call(project_kernel, in_specs=[WHOLE, WHOLE, ANY], out_specs=WH...  4.92 us
  transfers between devices with their start and end apart: 9, of which 2 were waited for; matrix products, arithmetic and copies ran while one was open for 0% of the time, Pallas kernels for 9%

profile of v5, /device:TPU:1, one launch (start us, length us, event | category | flops | bytes accessed | tf_op | source)
XLA Modules:
  0.0 69.8 jit_solution(18149099665729598567)
XLA Ops:
  0.6 2.4 %pack.1 = bf16[16,352,128]{2,1,0:T(8,128)(2,1)} custom-call(bf16[1,96,3,16,128]{4,3,2,1,0:T(8,128)(2,1)} %vis_ref.1, bf16[1,32,2,16,128]{4,3,2,1,0:T(8,128)(2,1)} %txt_ref.1), custom_call_target="tpu_custom_call" | custom-call | bytes 2883584 | tf_op jit(solution)/shard_map/pack/pallas_call | solution.py:64
  3.0 0.0 copy-start.2
  3.0 0.0 copy-start
  3.0 6.0 %all-to-all-start = ((bf16[16,352,128]{2,1,0:T(8,128)(2,1)}), bf16[16,352,128]{2,1,0:T(8,128)(2,1)S(1)}, u32[]{:S(2)}, u32[]{:S(2)}) async-start(bf16[16,352,128]{2,1,0:T(8,128)(2,1)} %pack.1), calls=%async_computation | async-start | bytes 2883584 | tf_op jit(solution)/shard_map/all_to_all | solution.py:435
  9.0 5.3 %collective-permute-start = (bf16[192,2048]{1,0:T(8,128)(2,1)S(1)}, bf16[192,2048]{1,0:T(8,128)(2,1)}, u32[]{:S(2)}, u32[]{:S(2)}) collective-permute-start(bf16[192,2048]{1,0:T(8,128)(2,1)S(1)} %bitcast.13), channel_id=1, source_target_pairs={{0,388},{1,389},{2,390},{3,391},{4,128},{5,129},{6,130},{7,131},{1... | collective-permute-start | bytes 2359304 | tf_op jit(solution)/shard_map/ppermute | solution.py:430
  14.3 0.4 share.1
  14.7 3.1 %collective-permute-start.1 = (bf16[96,768]{1,0:T(8,128)(2,1)S(1)}, bf16[96,768]{1,0:T(8,128)(2,1)S(1)}, u32[]{:S(2)}, u32[]{:S(2)}) collective-permute-start(bf16[96,768]{1,0:T(8,128)(2,1)S(1)} %get-tuple-element.23), channel_id=1, source_target_pairs={{0,1},{1,0},{2,3},{3,2},{4,5},{5,4},{6,7},{7,6},{8,9},{9,8},{10,11... | collective-permute-start | bytes 442376 | tf_op jit(solution)/shard_map/ppermute | solution.py:439
  17.8 4.3 %collective-permute-start.2 = (bf16[96,768]{1,0:T(8,128)(2,1)S(1)}, bf16[96,768]{1,0:T(8,128)(2,1)S(1)}, u32[]{:S(2)}, u32[]{:S(2)}) collective-permute-start(bf16[96,768]{1,0:T(8,128)(2,1)S(1)} %get-tuple-element.24), channel_id=1, source_target_pairs={{0,2},{1,3},{2,0},{3,1},{4,6},{5,7},{6,4},{7,5},{8,10},{9,11},{10,... | collective-permute-start | bytes 442376 | tf_op jit(solution)/shard_map/ppermute | solution.py:439
  22.1 2.2 %collective-permute-start.3 = (bf16[96,768]{1,0:T(8,128)(2,1)S(1)}, bf16[96,768]{1,0:T(8,128)(2,1)S(1)}, u32[]{:S(2)}, u32[]{:S(2)}) collective-permute-start(bf16[96,768]{1,0:T(8,128)(2,1)S(1)} %get-tuple-element.25), channel_id=1, source_target_pairs={{0,3},{1,2},{2,1},{3,0},{4,7},{5,6},{6,5},{7,4},{8,11},{9,10},{10,... | collective-permute-start | bytes 442376 | tf_op jit(solution)/shard_map/ppermute | solution.py:439
  25.0 3.1 %attend.1 = bf16[8,2,384,128]{3,2,1,0:T(8,128)(2,1)} custom-call(s32[1]{0:T(128)} %bitcast.9.len_ref, bf16[8,2,352,128]{3,2,1,0:T(8,128)(2,1)S(1)} %bitcast.11), custom_call_target="tpu_custom_call" | custom-call | flops 805306368 | bytes 2228224 | tf_op jit(solution)/shard_map/attend/pallas_call | solution.py:159
  28.1 0.0 copy-start.10
  28.1 6.2 %all-to-all-start.1 = ((bf16[8,2,384,128]{3,2,1,0:T(8,128)(2,1)}), bf16[8,2,384,128]{3,2,1,0:T(8,128)(2,1)S(1)}, u32[]{:S(2)}, u32[]{:S(2)}) async-start(bf16[8,2,384,128]{3,2,1,0:T(8,128)(2,1)} %attend.1), calls=%async_computation.1 | async-start | bytes 3145728 | tf_op jit(solution)/shard_map/all_to_all | solution.py:446
  34.3 4.9 %collective-permute-start.4 = (bf16[192,2048]{1,0:T(8,128)(2,1)S(1)}, bf16[192,2048]{1,0:T(8,128)(2,1)S(1)}, u32[]{:S(2)}, u32[]{:S(2)}) collective-permute-start(bf16[192,2048]{1,0:T(8,128)(2,1)S(1)} %bitcast.14), channel_id=1, source_target_pairs={{0,8},{8,0},{1,9},{9,1},{2,10},{10,2},{3,11},{11,3},{4,12},{12,4},... | collective-permute-start | bytes 2359304 | tf_op jit(solution)/shard_map/ppermute | solution.py:444
  39.2 0.0 collective-permute-done.1.refs_5_
  39.3 0.6 copy-done.4
  39.9 0.7 copy-done.6
  40.6 0.7 copy-done.8
  41.2 0.0 collective-permute-done.refs_1_
  41.2 1.9 %collective-permute-start.5 = (bf16[192,2048]{1,0:T(8,128)(2,1)}, bf16[192,2048]{1,0:T(8,128)(2,1)S(1)}, u32[]{:S(2)}, u32[]{:S(2)}) collective-permute-start(bf16[192,2048]{1,0:T(8,128)(2,1)} %collective-permute-done.refs_1_), channel_id=1, source_target_pairs={{0,8},{8,0},{1,9},{9,1},{2,10},{10,2},{3,11},{11,3},{4,12},{12,4},... | collective-permute-start | bytes 2359304 | tf_op jit(solution)/shard_map/ppermute | solution.py:444
  43.2 0.0 collective-permute-done.4.refs_2_
  43.2 2.4 %collective-permute-done.5.refs_3_ = bf16[192,2048]{1,0:T(8,128)(2,1)S(1)} collective-permute-done((bf16[192,2048]{1,0:T(8,128)(2,1)}, bf16[192,2048]{1,0:T(8,128)(2,1)S(1)}, u32[]{:S(2)}, u32[]{:S(2)}) %collective-permute-start.5) | collective-permute-done | bytes 786464 | tf_op jit(solution)/shard_map/ppermute | solution.py:444
  45.6 1.0 %copy-done.3 = bf16[3072,48]{0,1:T(8,128)(2,1)S(1)} copy-done((bf16[3072,48]{0,1:T(8,128)(2,1)S(1)}, bf16[3072,48]{0,1:T(8,128)(2,1)}, u32[]{:S(2)}) %copy-start.3) | copy-done | bytes 294936
  46.6 0.9 %copy-done.5 = bf16[96,768]{1,0:T(8,128)(2,1)S(1)} copy-done((bf16[96,768]{1,0:T(8,128)(2,1)S(1)}, bf16[96,768]{1,0:T(8,128)(2,1)}, u32[]{:S(2)}) %copy-start.5) | copy-done | bytes 147480
  47.5 0.9 %copy-done.7 = bf16[96,768]{1,0:T(8,128)(2,1)S(1)} copy-done((bf16[96,768]{1,0:T(8,128)(2,1)S(1)}, bf16[96,768]{1,0:T(8,128)(2,1)}, u32[]{:S(2)}) %copy-start.7) | copy-done | bytes 147480
  48.4 0.9 %copy-done.9 = bf16[96,768]{1,0:T(8,128)(2,1)S(1)} copy-done((bf16[96,768]{1,0:T(8,128)(2,1)S(1)}, bf16[96,768]{1,0:T(8,128)(2,1)}, u32[]{:S(2)}) %copy-start.9) | copy-done | bytes 147480
  49.3 3.0 %stage.1 = (bf16[224,2048]{1,0:T(8,128)(2,1)S(1)}, bf16[768,2048]{1,0:T(8,128)(2,1)}) custom-call(f32[1,3,3072]{2,1,0:T(4,128)S(1)} %copy.12.mod_hbm, bf16[48,3072]{1,0:T(8,128)(2,1)S(1)} %bitcast.16, bf16[192,2048]{1,0:T(8,128)(2,1)S(1)} %bitcast.15, bf16[192,2048]{1,0:T(8,128)(2,1)} %collective-permute-done.refs_1_, ...), custom_call_target="tpu_custom_call" | custom-call | flops 20000000000 | tf_op jit(solution)/shard_map/stage/pallas_call | solution.py:268
  52.3 0.0 all-to-all-done.1
  52.3 0.0 copy-start.1
  52.3 4.9 %project.1 = f32[8,32,128]{2,1,0:T(8,128)} custom-call(bf16[16,384,128]{2,1,0:T(8,128)(2,1)S(1)} %bitcast.10, bf16[224,2048]{1,0:T(8,128)(2,1)S(1)} %get-tuple-element.32.aux_ref, bf16[768,2048]{1,0:T(8,128)(2,1)} %get-tuple-element.33.w_hbm), custom_call_target="tpu_custom_call" | custom-call | flops 1207959552 | bytes 3145728 | tf_op jit(solution)/shard_map/project/pallas_call | solution.py:346
  57.2 6.7 %all-to-all-start.2 = ((f32[8,32,128]{2,1,0:T(8,128)}), f32[8,32,128]{2,1,0:T(8,128)S(1)}, u32[]{:S(2)}, u32[]{:S(2)}) async-start(f32[8,32,128]{2,1,0:T(8,128)} %project.1), calls=%async_computation.2 | async-start | bytes 262144 | tf_op jit(solution)/shard_map/all_to_all | solution.py:450
  64.6 4.5 %all-to-all-done.2.x_ref = f32[8,32,128]{2,1,0:T(8,128)S(1)} async-done(((f32[8,32,128]{2,1,0:T(8,128)}), f32[8,32,128]{2,1,0:T(8,128)S(1)}, u32[]{:S(2)}, u32[]{:S(2)}) %all-to-all-start.2) | async-done | bytes 131104 | tf_op jit(solution)/shard_map/all_to_all | solution.py:450
  69.1 0.7 %update.1 = (f32[24,96]{1,0:T(8,128)}, f32[24,96]{1,0:T(8,128)}, f32[24,96]{1,0:T(8,128)}) custom-call(s32[1]{0:T(128)S(6)} %copy.14.step_ref, f32[8,32,128]{2,1,0:T(8,128)S(1)} %all-to-all-done.2.x_ref, f32[24,96]{1,0:T(8,128)S(1)} %bitcast.12), custom_call_target="tpu_custom_call" | custom-call | tf_op jit(solution)/shard_map/update/pallas_call | solution.py:394
  (15 shorter events, 0.0 us)
Async XLA Ops:
  3.0 6.0 %copy-start.2 = (bf16[2048,192]{0,1:T(8,128)(2,1)S(1)}, bf16[2048,192]{0,1:T(8,128)(2,1)}, u32[]{:S(2)}) copy-start(bf16[2048,192]{0,1:T(8,128)(2,1)} %param.13) | copy-start | bytes 2359300
  3.0 11.3 %copy-start = (bf16[1,96,3072]{2,1,0:T(8,128)(2,1)S(1)}, bf16[1,96,3072]{2,1,0:T(8,128)(2,1)}, u32[]{:S(2)}) copy-start(bf16[1,96,3072]{2,1,0:T(8,128)(2,1)} %hid_hbm) | copy-start | bytes 1769476
  3.0 21.9 %all-to-all-start = ((bf16[16,352,128]{2,1,0:T(8,128)(2,1)}), bf16[16,352,128]{2,1,0:T(8,128)(2,1)S(1)}, u32[]{:S(2)}, u32[]{:S(2)}) async-start(bf16[16,352,128]{2,1,0:T(8,128)(2,1)} %pack.1), calls=%async_computation | async-start | bytes 2883584 | tf_op jit(solution)/shard_map/all_to_all | solution.py:435
  9.0 32.2 %collective-permute-start = (bf16[192,2048]{1,0:T(8,128)(2,1)S(1)}, bf16[192,2048]{1,0:T(8,128)(2,1)}, u32[]{:S(2)}, u32[]{:S(2)}) collective-permute-start(bf16[192,2048]{1,0:T(8,128)(2,1)S(1)} %bitcast.13), channel_id=1, source_target_pairs={{0,388},{1,389},{2,390},{3,391},{4,128},{5,129},{6,130},{7,131},{1... | collective-permute-start | bytes 2359304 | tf_op jit(solution)/shard_map/ppermute | solution.py:430
  14.7 24.5 %collective-permute-start.1 = (bf16[96,768]{1,0:T(8,128)(2,1)S(1)}, bf16[96,768]{1,0:T(8,128)(2,1)S(1)}, u32[]{:S(2)}, u32[]{:S(2)}) collective-permute-start(bf16[96,768]{1,0:T(8,128)(2,1)S(1)} %get-tuple-element.23), channel_id=1, source_target_pairs={{0,1},{1,0},{2,3},{3,2},{4,5},{5,4},{6,7},{7,6},{8,9},{9,8},{10,11... | collective-permute-start | bytes 442376 | tf_op jit(solution)/shard_map/ppermute | solution.py:439
  17.8 22.1 %collective-permute-start.2 = (bf16[96,768]{1,0:T(8,128)(2,1)S(1)}, bf16[96,768]{1,0:T(8,128)(2,1)S(1)}, u32[]{:S(2)}, u32[]{:S(2)}) collective-permute-start(bf16[96,768]{1,0:T(8,128)(2,1)S(1)} %get-tuple-element.24), channel_id=1, source_target_pairs={{0,2},{1,3},{2,0},{3,1},{4,6},{5,7},{6,4},{7,5},{8,10},{9,11},{10,... | collective-permute-start | bytes 442376 | tf_op jit(solution)/shard_map/ppermute | solution.py:439
  22.1 18.4 %collective-permute-start.3 = (bf16[96,768]{1,0:T(8,128)(2,1)S(1)}, bf16[96,768]{1,0:T(8,128)(2,1)S(1)}, u32[]{:S(2)}, u32[]{:S(2)}) collective-permute-start(bf16[96,768]{1,0:T(8,128)(2,1)S(1)} %get-tuple-element.25), channel_id=1, source_target_pairs={{0,3},{1,2},{2,1},{3,0},{4,7},{5,6},{6,5},{7,4},{8,11},{9,10},{10,... | collective-permute-start | bytes 442376 | tf_op jit(solution)/shard_map/ppermute | solution.py:439
  28.1 15.0 %copy-start.10 = (f32[1,3,3072]{2,0,1:T(1,128)S(1)}, f32[1,3,3072]{2,0,1:T(1,128)}, u32[]{:S(2)}) copy-start(f32[1,3,3072]{2,0,1:T(1,128)} %param.14) | copy-start | bytes 110596
  28.1 24.2 %all-to-all-start.1 = ((bf16[8,2,384,128]{3,2,1,0:T(8,128)(2,1)}), bf16[8,2,384,128]{3,2,1,0:T(8,128)(2,1)S(1)}, u32[]{:S(2)}, u32[]{:S(2)}) async-start(bf16[8,2,384,128]{3,2,1,0:T(8,128)(2,1)} %attend.1), calls=%async_computation.1 | async-start | bytes 3145728 | tf_op jit(solution)/shard_map/all_to_all | solution.py:446
  34.3 8.9 %collective-permute-start.4 = (bf16[192,2048]{1,0:T(8,128)(2,1)S(1)}, bf16[192,2048]{1,0:T(8,128)(2,1)S(1)}, u32[]{:S(2)}, u32[]{:S(2)}) collective-permute-start(bf16[192,2048]{1,0:T(8,128)(2,1)S(1)} %bitcast.14), channel_id=1, source_target_pairs={{0,8},{8,0},{1,9},{9,1},{2,10},{10,2},{3,11},{11,3},{4,12},{12,4},... | collective-permute-start | bytes 2359304 | tf_op jit(solution)/shard_map/ppermute | solution.py:444
  39.2 0.7 copy-start.4
  39.9 0.7 copy-start.6
  40.6 0.7 copy-start.8
  41.2 4.4 %collective-permute-start.5 = (bf16[192,2048]{1,0:T(8,128)(2,1)}, bf16[192,2048]{1,0:T(8,128)(2,1)S(1)}, u32[]{:S(2)}, u32[]{:S(2)}) collective-permute-start(bf16[192,2048]{1,0:T(8,128)(2,1)} %collective-permute-done.refs_1_), channel_id=1, source_target_pairs={{0,8},{8,0},{1,9},{9,1},{2,10},{10,2},{3,11},{11,3},{4,12},{12,4},... | collective-permute-start | bytes 2359304 | tf_op jit(solution)/shard_map/ppermute | solution.py:444
  45.6 1.0 %copy-start.3 = (bf16[3072,48]{0,1:T(8,128)(2,1)S(1)}, bf16[3072,48]{0,1:T(8,128)(2,1)}, u32[]{:S(2)}) copy-start(bf16[3072,48]{0,1:T(8,128)(2,1)} %param.15) | copy-start | bytes 884740
  46.6 0.9 %copy-start.5 = (bf16[96,768]{1,0:T(8,128)(2,1)S(1)}, bf16[96,768]{1,0:T(8,128)(2,1)}, u32[]{:S(2)}) copy-start(bf16[96,768]{1,0:T(8,128)(2,1)} %copy-done.4) | copy-start | bytes 442372
  47.5 0.9 %copy-start.7 = (bf16[96,768]{1,0:T(8,128)(2,1)S(1)}, bf16[96,768]{1,0:T(8,128)(2,1)}, u32[]{:S(2)}) copy-start(bf16[96,768]{1,0:T(8,128)(2,1)} %copy-done.6) | copy-start | bytes 442372
  48.4 0.9 %copy-start.9 = (bf16[96,768]{1,0:T(8,128)(2,1)S(1)}, bf16[96,768]{1,0:T(8,128)(2,1)}, u32[]{:S(2)}) copy-start(bf16[96,768]{1,0:T(8,128)(2,1)} %copy-done.8) | copy-start | bytes 442372
  52.3 16.8 %copy-start.1 = (f32[96,24]{0,1:T(8,128)S(1)}, f32[96,24]{0,1:T(8,128)}, u32[]{:S(2)}) copy-start(f32[96,24]{0,1:T(8,128)} %param.16) | copy-start | bytes 27652
  57.2 11.8 %all-to-all-start.2 = ((f32[8,32,128]{2,1,0:T(8,128)}), f32[8,32,128]{2,1,0:T(8,128)S(1)}, u32[]{:S(2)}, u32[]{:S(2)}) async-start(f32[8,32,128]{2,1,0:T(8,128)} %project.1), calls=%async_computation.2 | async-start | bytes 262144 | tf_op jit(solution)/shard_map/all_to_all | solution.py:450

commit v6 on v5

--- a/solution.py
+++ b/solution.py
@@ -108,7 +108,7 @@
         out_specs=[WHOLE] * 4,
         out_shape=[jax.ShapeDtypeStruct((vis, width // 4), BF)] * 4,
         scratch_shapes=[pltpu.VMEM((vis, width), BF), pltpu.SemaphoreType.DMA],
-        compiler_params=pltpu.CompilerParams(vmem_limit_bytes=STAGE),
+        compiler_params=pltpu.CompilerParams(vmem_limit_bytes=53 << 20),
         name="share",
     )(hidden)
 

time: 70.5 us -> 70.4 us (level)
  local copies, waits for them, and re-layouts: 5.69 us -> 3 us
  waiting for transfers between devices: 6.94 us -> 9.07 us
  Pallas kernels: 14.5 us -> 16.4 us
  starting transfers between devices: 40.5 us -> 39.1 us
    all_to_all x1, waiting for transfers between devices: 0.01 us -> 3.21 us  [shards(): lax.all_to_all(attended, ('row', 'col'), split_axis=0, concat_axis=0, til...]
    unnamed x22 -> x12, local copies, waits for them, and re-layouts: 5.67 us -> 2.99 us
    all_to_all x1, starting transfers between devices: 6.19 us -> 4.4 us  [shards(): lax.all_to_all(attended, ('row', 'col'), split_axis=0, concat_axis=0, til...]
    pallas_call x1, Pallas kernels: 0.38 us -> 2.07 us  [share(): pl.pallas_call(share_kernel, in_specs=[ANY], out_specs=[WHOLE] * 4, out_s...]
    ppermute x2, waiting for transfers between devices: 2.42 us -> 1.34 us  [shards(): own_other, far_other = (lax.ppermute(b, 'cfg', cores) for b in (own, far))]
  transfers between devices with their start and end apart: 9 -> 9, of which waited for: 2 -> 3; matrix products, arithmetic and copies ran while one was open for 0% -> 0% of each run, Pallas kernels for 9% -> 12%
where the time goes in v6:
time: 70.4 us; the launch traced here: 69.7 us
  starting transfers between devices  39.1 us (56%)
  Pallas kernels  16.4 us (23%)
  waiting for transfers between devices  9.07 us (13%)
  local copies, waits for them, and re-layouts  3 us (4%)
  between operations  2.1 us (3%)
    ppermute x3, starting transfers between devices, shards(): lax.ppermute(block, 'col', [(c, c ^ d) for c in range(4)])  9.59 us
    ppermute x2, starting transfers between devices, shards(): own_other, far_other = (lax.ppermute(b, 'cfg', cores) for b in (own, far))  6.95 us
    all_to_all x1, starting transfers between devices, shards(): lax.all_to_all(parts, ('cfg', 'col'), split_axis=0, concat_axis=0, tiled=...  6.95 us
    all_to_all x1, starting transfers between devices, shards(): lax.all_to_all(packed, ('row', 'col'), split_axis=0, concat_axis=0, tiled...  6.01 us
    ppermute x1, starting transfers between devices, across(): return lax.ppermute(block, ('req', 'row', 'col'), outer)  5.25 us
    pallas_call x1, Pallas kernels, project(): pl.pallas_call(project_kernel, in_specs=[WHOLE, WHOLE, ANY], out_specs=WH...  4.93 us
    all_to_all x1, waiting for transfers between devices, shards(): lax.all_to_all(parts, ('cfg', 'col'), split_axis=0, concat_axis=0, tiled=...  4.51 us
    all_to_all x1, starting transfers between devices, shards(): lax.all_to_all(attended, ('row', 'col'), split_axis=0, concat_axis=0, til...  4.4 us
  transfers between devices with their start and end apart: 9, of which 3 were waited for; matrix products, arithmetic and copies ran while one was open for 0% of the time, Pallas kernels for 12%

profile of v6, /device:TPU:1, one launch (start us, length us, event | category | flops | bytes accessed | tf_op | source)
XLA Modules:
  0.0 69.7 jit_solution(2772168995066680415)
XLA Ops:
  0.6 2.4 %pack.1 = bf16[16,352,128]{2,1,0:T(8,128)(2,1)} custom-call(bf16[1,96,3,16,128]{4,3,2,1,0:T(8,128)(2,1)} %vis_ref.1, bf16[1,32,2,16,128]{4,3,2,1,0:T(8,128)(2,1)} %txt_ref.1), custom_call_target="tpu_custom_call" | custom-call | bytes 2883584 | tf_op jit(solution)/shard_map/pack/pallas_call | solution.py:64
  3.0 0.0 copy-start.1
  3.0 6.0 %all-to-all-start = ((bf16[16,352,128]{2,1,0:T(8,128)(2,1)}), bf16[16,352,128]{2,1,0:T(8,128)(2,1)S(1)}, u32[]{:S(2)}, u32[]{:S(2)}) async-start(bf16[16,352,128]{2,1,0:T(8,128)(2,1)} %pack.1), calls=%async_computation | async-start | bytes 2883584 | tf_op jit(solution)/shard_map/all_to_all | solution.py:435
  9.0 0.0 copy-done.1
  9.0 5.2 %collective-permute-start = (bf16[192,2048]{1,0:T(8,128)(2,1)S(1)}, bf16[192,2048]{1,0:T(8,128)(2,1)S(1)}, u32[]{:S(2)}, u32[]{:S(2)}) collective-permute-start(bf16[192,2048]{1,0:T(8,128)(2,1)S(1)} %bitcast.13), channel_id=1, source_target_pairs={{0,388},{1,389},{2,390},{3,391},{4,128},{5,129},{6,130},{7,131},{1... | collective-permute-start | bytes 2359304 | tf_op jit(solution)/shard_map/ppermute | solution.py:430
  14.3 2.1 %share.1 = (bf16[96,768]{1,0:T(8,128)(2,1)S(1)}, bf16[96,768]{1,0:T(8,128)(2,1)}, bf16[96,768]{1,0:T(8,128)(2,1)}, bf16[96,768]{1,0:T(8,128)(2,1)}) custom-call(bf16[1,96,3072]{2,1,0:T(8,128)(2,1)} %hid_hbm), custom_call_target="tpu_custom_call" | custom-call | tf_op jit(solution)/shard_map/share/pallas_call | solution.py:105
  16.4 3.1 %collective-permute-start.1 = (bf16[96,768]{1,0:T(8,128)(2,1)}, bf16[96,768]{1,0:T(8,128)(2,1)}, u32[]{:S(2)}, u32[]{:S(2)}) collective-permute-start(bf16[96,768]{1,0:T(8,128)(2,1)} %get-tuple-element.23), channel_id=1, source_target_pairs={{0,1},{1,0},{2,3},{3,2},{4,5},{5,4},{6,7},{7,6},{8,9},{9,8},{10,11... | collective-permute-start | bytes 442376 | tf_op jit(solution)/shard_map/ppermute | solution.py:439
  19.5 4.3 %collective-permute-start.2 = (bf16[96,768]{1,0:T(8,128)(2,1)}, bf16[96,768]{1,0:T(8,128)(2,1)}, u32[]{:S(2)}, u32[]{:S(2)}) collective-permute-start(bf16[96,768]{1,0:T(8,128)(2,1)} %get-tuple-element.24), channel_id=1, source_target_pairs={{0,2},{1,3},{2,0},{3,1},{4,6},{5,7},{6,4},{7,5},{8,10},{9,11},{10,... | collective-permute-start | bytes 442376 | tf_op jit(solution)/shard_map/ppermute | solution.py:439
  23.8 2.2 %collective-permute-start.3 = (bf16[96,768]{1,0:T(8,128)(2,1)}, bf16[96,768]{1,0:T(8,128)(2,1)}, u32[]{:S(2)}, u32[]{:S(2)}) collective-permute-start(bf16[96,768]{1,0:T(8,128)(2,1)} %get-tuple-element.25), channel_id=1, source_target_pairs={{0,3},{1,2},{2,1},{3,0},{4,7},{5,6},{6,5},{7,4},{8,11},{9,10},{10,... | collective-permute-start | bytes 442376 | tf_op jit(solution)/shard_map/ppermute | solution.py:439
  26.6 0.0 all-to-all-done
  26.6 3.1 %attend.1 = bf16[8,2,384,128]{3,2,1,0:T(8,128)(2,1)} custom-call(s32[1]{0:T(128)} %bitcast.9.len_ref, bf16[8,2,352,128]{3,2,1,0:T(8,128)(2,1)S(1)} %bitcast.11), custom_call_target="tpu_custom_call" | custom-call | flops 805306368 | bytes 2228224 | tf_op jit(solution)/shard_map/attend/pallas_call | solution.py:159
  29.7 0.0 copy-start.5
  29.8 4.4 %all-to-all-start.1 = ((bf16[8,2,384,128]{3,2,1,0:T(8,128)(2,1)}), bf16[8,2,384,128]{3,2,1,0:T(8,128)(2,1)S(1)}, u32[]{:S(2)}, u32[]{:S(2)}) async-start(bf16[8,2,384,128]{3,2,1,0:T(8,128)(2,1)} %attend.1), calls=%async_computation.1 | async-start | bytes 3145728 | tf_op jit(solution)/shard_map/all_to_all | solution.py:446
  34.2 5.0 %collective-permute-start.4 = (bf16[192,2048]{1,0:T(8,128)(2,1)S(1)}, bf16[192,2048]{1,0:T(8,128)(2,1)S(1)}, u32[]{:S(2)}, u32[]{:S(2)}) collective-permute-start(bf16[192,2048]{1,0:T(8,128)(2,1)S(1)} %bitcast.14), channel_id=1, source_target_pairs={{0,8},{8,0},{1,9},{9,1},{2,10},{10,2},{3,11},{11,3},{4,12},{12,4},... | collective-permute-start | bytes 2359304 | tf_op jit(solution)/shard_map/ppermute | solution.py:444
  39.2 0.0 collective-permute-done.1.refs_5_
  39.2 0.0 collective-permute-done.2.refs_6_
  39.2 0.0 collective-permute-done.3.refs_7_
  39.2 0.0 collective-permute-done.refs_1_
  39.2 1.9 %collective-permute-start.5 = (bf16[192,2048]{1,0:T(8,128)(2,1)S(1)}, bf16[192,2048]{1,0:T(8,128)(2,1)S(1)}, u32[]{:S(2)}, u32[]{:S(2)}) collective-permute-start(bf16[192,2048]{1,0:T(8,128)(2,1)S(1)} %collective-permute-done.refs_1_), channel_id=1, source_target_pairs={{0,8},{8,0},{1,9},{9,1},{2,10},{10,2},{3,11},{11,3},{4,12},{12,4},... | collective-permute-start | bytes 2359304 | tf_op jit(solution)/shard_map/ppermute | solution.py:444
  41.2 0.0 copy-start.2
  41.2 0.9 %copy-done.2 = bf16[192,2048]{1,0:T(8,128)(2,1)} copy-done((bf16[192,2048]{1,0:T(8,128)(2,1)}, bf16[192,2048]{1,0:T(8,128)(2,1)S(1)}, u32[]{:S(2)}) %copy-start.2) | copy-done | bytes 786456
  42.1 0.0 collective-permute-done.4.refs_2_
  42.1 1.3 %collective-permute-done.5.refs_3_ = bf16[192,2048]{1,0:T(8,128)(2,1)S(1)} collective-permute-done((bf16[192,2048]{1,0:T(8,128)(2,1)S(1)}, bf16[192,2048]{1,0:T(8,128)(2,1)S(1)}, u32[]{:S(2)}, u32[]{:S(2)}) %collective-permute-start.5) | collective-permute-done | bytes 786464 | tf_op jit(solution)/shard_map/ppermute | solution.py:444
  43.4 1.1 %copy-done.3 = bf16[192,2048]{1,0:T(8,128)(2,1)S(1)} copy-done((bf16[192,2048]{1,0:T(8,128)(2,1)S(1)}, bf16[192,2048]{1,0:T(8,128)(2,1)}, u32[]{:S(2)}) %copy-start.3) | copy-done | bytes 786456
  44.6 1.0 %copy-done.4 = bf16[3072,48]{0,1:T(8,128)(2,1)S(1)} copy-done((bf16[3072,48]{0,1:T(8,128)(2,1)S(1)}, bf16[3072,48]{0,1:T(8,128)(2,1)}, u32[]{:S(2)}) %copy-start.4) | copy-done | bytes 294936
  45.5 3.2 %stage.1 = (bf16[224,2048]{1,0:T(8,128)(2,1)S(1)}, bf16[768,2048]{1,0:T(8,128)(2,1)}) custom-call(f32[1,3,3072]{2,1,0:T(4,128)S(1)} %copy.12.mod_hbm, bf16[48,3072]{1,0:T(8,128)(2,1)S(1)} %bitcast.16, bf16[192,2048]{1,0:T(8,128)(2,1)S(1)} %bitcast.15, bf16[192,2048]{1,0:T(8,128)(2,1)S(1)} %copy-done.3, bf16[192,2048]{1,0:T(8,128)(2,1)S(1)} %collective-permute-done.4.refs_2_, ...), custom_call_target="tpu_custom_call" | custom-call | flops 20000000000 | tf_op jit(solution)/shard_map/stage/pallas_call | solution.py:268
  48.7 3.2 %all-to-all-done.1 = bf16[8,2,384,128]{3,2,1,0:T(8,128)(2,1)S(1)} async-done(((bf16[8,2,384,128]{3,2,1,0:T(8,128)(2,1)}), bf16[8,2,384,128]{3,2,1,0:T(8,128)(2,1)S(1)}, u32[]{:S(2)}, u32[]{:S(2)}) %all-to-all-start.1) | async-done | bytes 1572896 | tf_op jit(solution)/shard_map/all_to_all | solution.py:446
  51.9 4.9 %project.1 = f32[8,32,128]{2,1,0:T(8,128)} custom-call(bf16[16,384,128]{2,1,0:T(8,128)(2,1)S(1)} %bitcast.10, bf16[224,2048]{1,0:T(8,128)(2,1)S(1)} %get-tuple-element.32.aux_ref, bf16[768,2048]{1,0:T(8,128)(2,1)} %get-tuple-element.33.w_hbm), custom_call_target="tpu_custom_call" | custom-call | flops 1207959552 | bytes 3145728 | tf_op jit(solution)/shard_map/project/pallas_call | solution.py:346
  56.8 6.9 %all-to-all-start.2 = ((f32[8,32,128]{2,1,0:T(8,128)}), f32[8,32,128]{2,1,0:T(8,128)S(1)}, u32[]{:S(2)}, u32[]{:S(2)}) async-start(f32[8,32,128]{2,1,0:T(8,128)} %project.1), calls=%async_computation.2 | async-start | bytes 262144 | tf_op jit(solution)/shard_map/all_to_all | solution.py:450
  64.4 4.5 %all-to-all-done.2.x_ref = f32[8,32,128]{2,1,0:T(8,128)S(1)} async-done(((f32[8,32,128]{2,1,0:T(8,128)}), f32[8,32,128]{2,1,0:T(8,128)S(1)}, u32[]{:S(2)}, u32[]{:S(2)}) %all-to-all-start.2) | async-done | bytes 131104 | tf_op jit(solution)/shard_map/all_to_all | solution.py:450
  68.9 0.0 copy-done
  69.0 0.7 %update.1 = (f32[24,96]{1,0:T(8,128)}, f32[24,96]{1,0:T(8,128)}, f32[24,96]{1,0:T(8,128)}) custom-call(s32[1]{0:T(128)S(6)} %copy.14.step_ref, f32[8,32,128]{2,1,0:T(8,128)S(1)} %all-to-all-done.2.x_ref, f32[24,96]{1,0:T(8,128)S(1)} %bitcast.12), custom_call_target="tpu_custom_call" | custom-call | tf_op jit(solution)/shard_map/update/pallas_call | solution.py:394
  (5 shorter events, 0.0 us)
Async XLA Ops:
  3.0 6.0 %copy-start.1 = (bf16[2048,192]{0,1:T(8,128)(2,1)S(1)}, bf16[2048,192]{0,1:T(8,128)(2,1)}, u32[]{:S(2)}) copy-start(bf16[2048,192]{0,1:T(8,128)(2,1)} %param.13) | copy-start | bytes 2359300
  3.0 23.6 %all-to-all-start = ((bf16[16,352,128]{2,1,0:T(8,128)(2,1)}), bf16[16,352,128]{2,1,0:T(8,128)(2,1)S(1)}, u32[]{:S(2)}, u32[]{:S(2)}) async-start(bf16[16,352,128]{2,1,0:T(8,128)(2,1)} %pack.1), calls=%async_computation | async-start | bytes 2883584 | tf_op jit(solution)/shard_map/all_to_all | solution.py:435
  9.0 30.2 %collective-permute-start = (bf16[192,2048]{1,0:T(8,128)(2,1)S(1)}, bf16[192,2048]{1,0:T(8,128)(2,1)S(1)}, u32[]{:S(2)}, u32[]{:S(2)}) collective-permute-start(bf16[192,2048]{1,0:T(8,128)(2,1)S(1)} %bitcast.13), channel_id=1, source_target_pairs={{0,388},{1,389},{2,390},{3,391},{4,128},{5,129},{6,130},{7,131},{1... | collective-permute-start | bytes 2359304 | tf_op jit(solution)/shard_map/ppermute | solution.py:430
  16.4 22.8 %collective-permute-start.1 = (bf16[96,768]{1,0:T(8,128)(2,1)}, bf16[96,768]{1,0:T(8,128)(2,1)}, u32[]{:S(2)}, u32[]{:S(2)}) collective-permute-start(bf16[96,768]{1,0:T(8,128)(2,1)} %get-tuple-element.23), channel_id=1, source_target_pairs={{0,1},{1,0},{2,3},{3,2},{4,5},{5,4},{6,7},{7,6},{8,9},{9,8},{10,11... | collective-permute-start | bytes 442376 | tf_op jit(solution)/shard_map/ppermute | solution.py:439
  19.5 19.8 %collective-permute-start.2 = (bf16[96,768]{1,0:T(8,128)(2,1)}, bf16[96,768]{1,0:T(8,128)(2,1)}, u32[]{:S(2)}, u32[]{:S(2)}) collective-permute-start(bf16[96,768]{1,0:T(8,128)(2,1)} %get-tuple-element.24), channel_id=1, source_target_pairs={{0,2},{1,3},{2,0},{3,1},{4,6},{5,7},{6,4},{7,5},{8,10},{9,11},{10,... | collective-permute-start | bytes 442376 | tf_op jit(solution)/shard_map/ppermute | solution.py:439
  23.8 15.5 %collective-permute-start.3 = (bf16[96,768]{1,0:T(8,128)(2,1)}, bf16[96,768]{1,0:T(8,128)(2,1)}, u32[]{:S(2)}, u32[]{:S(2)}) collective-permute-start(bf16[96,768]{1,0:T(8,128)(2,1)} %get-tuple-element.25), channel_id=1, source_target_pairs={{0,3},{1,2},{2,1},{3,0},{4,7},{5,6},{6,5},{7,4},{8,11},{9,10},{10,... | collective-permute-start | bytes 442376 | tf_op jit(solution)/shard_map/ppermute | solution.py:439
  29.7 12.3 %copy-start.5 = (f32[1,3,3072]{2,0,1:T(1,128)S(1)}, f32[1,3,3072]{2,0,1:T(1,128)}, u32[]{:S(2)}) copy-start(f32[1,3,3072]{2,0,1:T(1,128)} %param.14) | copy-start | bytes 110596
  29.8 22.1 %all-to-all-start.1 = ((bf16[8,2,384,128]{3,2,1,0:T(8,128)(2,1)}), bf16[8,2,384,128]{3,2,1,0:T(8,128)(2,1)S(1)}, u32[]{:S(2)}, u32[]{:S(2)}) async-start(bf16[8,2,384,128]{3,2,1,0:T(8,128)(2,1)} %attend.1), calls=%async_computation.1 | async-start | bytes 3145728 | tf_op jit(solution)/shard_map/all_to_all | solution.py:446
  34.2 7.9 %collective-permute-start.4 = (bf16[192,2048]{1,0:T(8,128)(2,1)S(1)}, bf16[192,2048]{1,0:T(8,128)(2,1)S(1)}, u32[]{:S(2)}, u32[]{:S(2)}) collective-permute-start(bf16[192,2048]{1,0:T(8,128)(2,1)S(1)} %bitcast.14), channel_id=1, source_target_pairs={{0,8},{8,0},{1,9},{9,1},{2,10},{10,2},{3,11},{11,3},{4,12},{12,4},... | collective-permute-start | bytes 2359304 | tf_op jit(solution)/shard_map/ppermute | solution.py:444
  39.2 4.2 %collective-permute-start.5 = (bf16[192,2048]{1,0:T(8,128)(2,1)S(1)}, bf16[192,2048]{1,0:T(8,128)(2,1)S(1)}, u32[]{:S(2)}, u32[]{:S(2)}) collective-permute-start(bf16[192,2048]{1,0:T(8,128)(2,1)S(1)} %collective-permute-done.refs_1_), channel_id=1, source_target_pairs={{0,8},{8,0},{1,9},{9,1},{2,10},{10,2},{3,11},{11,3},{4,12},{12,4},... | collective-permute-start | bytes 2359304 | tf_op jit(solution)/shard_map/ppermute | solution.py:444
  41.2 0.9 %copy-start.2 = (bf16[192,2048]{1,0:T(8,128)(2,1)}, bf16[192,2048]{1,0:T(8,128)(2,1)S(1)}, u32[]{:S(2)}) copy-start(bf16[192,2048]{1,0:T(8,128)(2,1)S(1)} %collective-permute-done.refs_1_) | copy-start | bytes 2359300
  43.4 1.1 %copy-start.3 = (bf16[192,2048]{1,0:T(8,128)(2,1)S(1)}, bf16[192,2048]{1,0:T(8,128)(2,1)}, u32[]{:S(2)}) copy-start(bf16[192,2048]{1,0:T(8,128)(2,1)} %copy-done.2) | copy-start | bytes 2359300
  44.6 1.0 %copy-start.4 = (bf16[3072,48]{0,1:T(8,128)(2,1)S(1)}, bf16[3072,48]{0,1:T(8,128)(2,1)}, u32[]{:S(2)}) copy-start(bf16[3072,48]{0,1:T(8,128)(2,1)} %param.15) | copy-start | bytes 884740
  51.9 17.1 %copy-start = (f32[96,24]{0,1:T(8,128)S(1)}, f32[96,24]{0,1:T(8,128)}, u32[]{:S(2)}) copy-start(f32[96,24]{0,1:T(8,128)} %param.16) | copy-start | bytes 27652
  56.8 12.1 %all-to-all-start.2 = ((f32[8,32,128]{2,1,0:T(8,128)}), f32[8,32,128]{2,1,0:T(8,128)S(1)}, u32[]{:S(2)}, u32[]{:S(2)}) async-start(f32[8,32,128]{2,1,0:T(8,128)} %project.1), calls=%async_computation.2 | async-start | bytes 262144 | tf_op jit(solution)/shard_map/all_to_all | solution.py:450

commit v7 on v4

--- a/solution.py
+++ b/solution.py
@@ -333,8 +333,8 @@
         for k in range(4):
             at = slice(k * vis, (k + 1) * vis)
             rows = slice(core * half, (core + 1) * half)
-            o_ref[core * 4 + k, :half] = jnp.concatenate([pred[rows, at], sums[rows]], axis=1)
-            o_ref[core * 4 + k, half:] = jnp.concatenate(
+            o_ref[k * 2 + core, :half] = jnp.concatenate([pred[rows, at], sums[rows]], axis=1)
+            o_ref[k * 2 + core, half:] = jnp.concatenate(
                 [pred[patch : patch + 8, at], sums[:8]], axis=1
             )
 
@@ -367,7 +367,7 @@
     half, vis = lat_ref.shape
     preds = []
     for b in range(2):
-        parts = [x_ref[b * 4 + k] for k in range(4)]
+        parts = [x_ref[k * 2 + b] for k in range(4)]
         means = [t[half : half + 1, :vis] for t in parts]
         mean = 0.25 * (means[0] + means[1] + means[2] + means[3])
         spread, linear, shift = 0.0, 0.0, 0.0
@@ -447,7 +447,7 @@
         attended, ("row", "col"), split_axis=0, concat_axis=0, tiled=True
     ).reshape(16, 4 * vis, 128)
     parts = project(att, aux, weights, final_weight.shape[1])
-    parts = lax.all_to_all(parts, ("cfg", "col"), split_axis=0, concat_axis=0, tiled=True)
+    parts = lax.all_to_all(parts, ("col", "cfg"), split_axis=0, concat_axis=0, tiled=True)
     outs = update(timestep, parts, latent.T, vis_hidden.shape[2])
     return tuple(o.T for o in outs)
 

time: 70.5 us -> 70.8 us (level)
  no operation moved by 1% of the time
where the time goes in v7:
time: 70.8 us; the launch traced here: 69.9 us
  starting transfers between devices  39.2 us (55%)
  Pallas kernels  15 us (21%)
  waiting for transfers between devices  8.99 us (13%)
  local copies, waits for them, and re-layouts  4.65 us (7%)
  between operations  2.12 us (3%)
    ppermute x3, starting transfers between devices, shards(): lax.ppermute(block, 'col', [(c, c ^ d) for c in range(4)])  9.59 us
    ppermute x2, starting transfers between devices, shards(): own_other, far_other = (lax.ppermute(b, 'cfg', cores) for b in (own, far))  6.95 us
    all_to_all x1, starting transfers between devices, shards(): lax.all_to_all(parts, ('col', 'cfg'), split_axis=0, concat_axis=0, tiled=...  6.92 us
    all_to_all x1, starting transfers between devices, shards(): lax.all_to_all(packed, ('row', 'col'), split_axis=0, concat_axis=0, tiled...  6.01 us
    ppermute x1, starting transfers between devices, across(): return lax.ppermute(block, ('req', 'row', 'col'), outer)  5.25 us
    pallas_call x1, Pallas kernels, project(): pl.pallas_call(project_kernel, in_specs=[WHOLE, WHOLE, ANY], out_specs=WH...  4.93 us
    all_to_all x1, waiting for transfers between devices, shards(): lax.all_to_all(parts, ('col', 'cfg'), split_axis=0, concat_axis=0, tiled=...  4.64 us
    unnamed x16, local copies, waits for them, and re-layouts  4.64 us
  transfers between devices with their start and end apart: 9, of which 3 were waited for; matrix products, arithmetic and copies ran while one was open for 0% of the time, Pallas kernels for 10%

profile of v7, /device:TPU:1, one launch (start us, length us, event | category | flops | bytes accessed | tf_op | source)
XLA Modules:
  0.0 69.9 jit_solution(7524760264591998201)
XLA Ops:
  0.6 2.4 %pack.1 = bf16[16,352,128]{2,1,0:T(8,128)(2,1)} custom-call(bf16[1,96,3,16,128]{4,3,2,1,0:T(8,128)(2,1)} %vis_ref.1, bf16[1,32,2,16,128]{4,3,2,1,0:T(8,128)(2,1)} %txt_ref.1), custom_call_target="tpu_custom_call" | custom-call | bytes 2883584 | tf_op jit(solution)/shard_map/pack/pallas_call | solution.py:64
  3.0 0.0 copy-start.2
  3.0 6.0 %all-to-all-start = ((bf16[16,352,128]{2,1,0:T(8,128)(2,1)}), bf16[16,352,128]{2,1,0:T(8,128)(2,1)S(1)}, u32[]{:S(2)}, u32[]{:S(2)}) async-start(bf16[16,352,128]{2,1,0:T(8,128)(2,1)} %pack.1), calls=%async_computation | async-start | bytes 2883584 | tf_op jit(solution)/shard_map/all_to_all | solution.py:435
  9.0 5.2 %collective-permute-start = (bf16[192,2048]{1,0:T(8,128)(2,1)S(1)}, bf16[192,2048]{1,0:T(8,128)(2,1)S(1)}, u32[]{:S(2)}, u32[]{:S(2)}) collective-permute-start(bf16[192,2048]{1,0:T(8,128)(2,1)S(1)} %bitcast.13), channel_id=1, source_target_pairs={{0,388},{1,389},{2,390},{3,391},{4,128},{5,129},{6,130},{7,131},{1... | collective-permute-start | bytes 2359304 | tf_op jit(solution)/shard_map/ppermute | solution.py:430
  14.3 2.1 %share.1 = (bf16[96,768]{1,0:T(8,128)(2,1)}, bf16[96,768]{1,0:T(8,128)(2,1)}, bf16[96,768]{1,0:T(8,128)(2,1)}, bf16[96,768]{1,0:T(8,128)(2,1)}) custom-call(bf16[1,96,3072]{2,1,0:T(8,128)(2,1)} %hid_hbm), custom_call_target="tpu_custom_call" | custom-call | tf_op jit(solution)/shard_map/share/pallas_call | solution.py:105
  16.4 3.1 %collective-permute-start.1 = (bf16[96,768]{1,0:T(8,128)(2,1)}, bf16[96,768]{1,0:T(8,128)(2,1)}, u32[]{:S(2)}, u32[]{:S(2)}) collective-permute-start(bf16[96,768]{1,0:T(8,128)(2,1)} %get-tuple-element.23), channel_id=1, source_target_pairs={{0,1},{1,0},{2,3},{3,2},{4,5},{5,4},{6,7},{7,6},{8,9},{9,8},{10,11... | collective-permute-start | bytes 442376 | tf_op jit(solution)/shard_map/ppermute | solution.py:439
  19.5 4.3 %collective-permute-start.2 = (bf16[96,768]{1,0:T(8,128)(2,1)}, bf16[96,768]{1,0:T(8,128)(2,1)}, u32[]{:S(2)}, u32[]{:S(2)}) collective-permute-start(bf16[96,768]{1,0:T(8,128)(2,1)} %get-tuple-element.24), channel_id=1, source_target_pairs={{0,2},{1,3},{2,0},{3,1},{4,6},{5,7},{6,4},{7,5},{8,10},{9,11},{10,... | collective-permute-start | bytes 442376 | tf_op jit(solution)/shard_map/ppermute | solution.py:439
  23.8 2.2 %collective-permute-start.3 = (bf16[96,768]{1,0:T(8,128)(2,1)}, bf16[96,768]{1,0:T(8,128)(2,1)}, u32[]{:S(2)}, u32[]{:S(2)}) collective-permute-start(bf16[96,768]{1,0:T(8,128)(2,1)} %get-tuple-element.25), channel_id=1, source_target_pairs={{0,3},{1,2},{2,1},{3,0},{4,7},{5,6},{6,5},{7,4},{8,11},{9,10},{10,... | collective-permute-start | bytes 442376 | tf_op jit(solution)/shard_map/ppermute | solution.py:439
  26.7 0.0 all-to-all-done
  26.7 3.1 %attend.1 = bf16[8,2,384,128]{3,2,1,0:T(8,128)(2,1)} custom-call(s32[1]{0:T(128)} %bitcast.9.len_ref, bf16[8,2,352,128]{3,2,1,0:T(8,128)(2,1)S(1)} %bitcast.11), custom_call_target="tpu_custom_call" | custom-call | flops 805306368 | bytes 2228224 | tf_op jit(solution)/shard_map/attend/pallas_call | solution.py:159
  29.8 0.0 copy-start.7
  29.8 4.5 %all-to-all-start.1 = ((bf16[8,2,384,128]{3,2,1,0:T(8,128)(2,1)}), bf16[8,2,384,128]{3,2,1,0:T(8,128)(2,1)S(1)}, u32[]{:S(2)}, u32[]{:S(2)}) async-start(bf16[8,2,384,128]{3,2,1,0:T(8,128)(2,1)} %attend.1), calls=%async_computation.1 | async-start | bytes 3145728 | tf_op jit(solution)/shard_map/all_to_all | solution.py:446
  34.3 5.0 %collective-permute-start.4 = (bf16[192,2048]{1,0:T(8,128)(2,1)S(1)}, bf16[192,2048]{1,0:T(8,128)(2,1)S(1)}, u32[]{:S(2)}, u32[]{:S(2)}) collective-permute-start(bf16[192,2048]{1,0:T(8,128)(2,1)S(1)} %bitcast.14), channel_id=1, source_target_pairs={{0,8},{8,0},{1,9},{9,1},{2,10},{10,2},{3,11},{11,3},{4,12},{12,4},... | collective-permute-start | bytes 2359304 | tf_op jit(solution)/shard_map/ppermute | solution.py:444
  39.3 0.0 collective-permute-done.1.refs_5_
  39.3 0.0 collective-permute-done.2.refs_6_
  39.3 0.0 collective-permute-done.3.refs_7_
  39.4 0.0 collective-permute-done.refs_1_
  39.4 1.9 %collective-permute-start.5 = (bf16[192,2048]{1,0:T(8,128)(2,1)S(1)}, bf16[192,2048]{1,0:T(8,128)(2,1)S(1)}, u32[]{:S(2)}, u32[]{:S(2)}) collective-permute-start(bf16[192,2048]{1,0:T(8,128)(2,1)S(1)} %collective-permute-done.refs_1_), channel_id=1, source_target_pairs={{0,8},{8,0},{1,9},{9,1},{2,10},{10,2},{3,11},{11,3},{4,12},{12,4},... | collective-permute-start | bytes 2359304 | tf_op jit(solution)/shard_map/ppermute | solution.py:444
  41.3 0.9 %copy-done.3 = bf16[192,2048]{1,0:T(8,128)(2,1)} copy-done((bf16[192,2048]{1,0:T(8,128)(2,1)}, bf16[192,2048]{1,0:T(8,128)(2,1)S(1)}, u32[]{:S(2)}) %copy-start.3) | copy-done | bytes 786456
  42.2 0.0 copy-done.7
  42.2 0.0 collective-permute-done.4.refs_2_
  42.2 1.3 %collective-permute-done.5.refs_3_ = bf16[192,2048]{1,0:T(8,128)(2,1)S(1)} collective-permute-done((bf16[192,2048]{1,0:T(8,128)(2,1)S(1)}, bf16[192,2048]{1,0:T(8,128)(2,1)S(1)}, u32[]{:S(2)}, u32[]{:S(2)}) %collective-permute-start.5) | collective-permute-done | bytes 786464 | tf_op jit(solution)/shard_map/ppermute | solution.py:444
  43.5 1.1 %copy-done.4 = bf16[192,2048]{1,0:T(8,128)(2,1)S(1)} copy-done((bf16[192,2048]{1,0:T(8,128)(2,1)S(1)}, bf16[192,2048]{1,0:T(8,128)(2,1)}, u32[]{:S(2)}) %copy-start.4) | copy-done | bytes 786456
  44.7 1.0 %copy-done.5 = bf16[3072,48]{0,1:T(8,128)(2,1)S(1)} copy-done((bf16[3072,48]{0,1:T(8,128)(2,1)S(1)}, bf16[3072,48]{0,1:T(8,128)(2,1)}, u32[]{:S(2)}) %copy-start.5) | copy-done | bytes 294936
  45.6 1.7 %stage.1 = (bf16[224,2048]{1,0:T(8,128)(2,1)S(1)}, bf16[768,2048]{1,0:T(8,128)(2,1)S(1)}) custom-call(f32[1,3,3072]{2,1,0:T(4,128)S(1)} %copy.12.mod_hbm, bf16[48,3072]{1,0:T(8,128)(2,1)S(1)} %bitcast.16, bf16[192,2048]{1,0:T(8,128)(2,1)S(1)} %bitcast.15, bf16[192,2048]{1,0:T(8,128)(2,1)S(1)} %copy-done.4, ...), custom_call_target="tpu_custom_call" | custom-call | flops 20000000000 | tf_op jit(solution)/shard_map/stage/pallas_call | solution.py:268
  47.4 0.0 copy-start
  47.4 1.6 %copy-done = bf16[768,2048]{1,0:T(8,128)(2,1)} copy-done((bf16[768,2048]{1,0:T(8,128)(2,1)}, bf16[768,2048]{1,0:T(8,128)(2,1)S(1)}, u32[]{:S(2)}) %copy-start) | copy-done | bytes 3145752
  49.0 3.0 %all-to-all-done.1 = bf16[8,2,384,128]{3,2,1,0:T(8,128)(2,1)S(1)} async-done(((bf16[8,2,384,128]{3,2,1,0:T(8,128)(2,1)}), bf16[8,2,384,128]{3,2,1,0:T(8,128)(2,1)S(1)}, u32[]{:S(2)}, u32[]{:S(2)}) %all-to-all-start.1) | async-done | bytes 1572896 | tf_op jit(solution)/shard_map/all_to_all | solution.py:446
  52.0 4.9 %project.1 = f32[8,32,128]{2,1,0:T(8,128)} custom-call(bf16[16,384,128]{2,1,0:T(8,128)(2,1)S(1)} %bitcast.10, bf16[224,2048]{1,0:T(8,128)(2,1)S(1)} %get-tuple-element.32.aux_ref, bf16[768,2048]{1,0:T(8,128)(2,1)} %copy-done), custom_call_target="tpu_custom_call" | custom-call | flops 1207959552 | bytes 3145728 | tf_op jit(solution)/shard_map/project/pallas_call | solution.py:346
  57.0 6.9 %all-to-all-start.2 = ((f32[8,32,128]{2,1,0:T(8,128)}), f32[8,32,128]{2,1,0:T(8,128)S(1)}, u32[]{:S(2)}, u32[]{:S(2)}) async-start(f32[8,32,128]{2,1,0:T(8,128)} %project.1), calls=%async_computation.2 | async-start | bytes 262144 | tf_op jit(solution)/shard_map/all_to_all | solution.py:450
  64.5 4.6 %all-to-all-done.2.x_ref = f32[8,32,128]{2,1,0:T(8,128)S(1)} async-done(((f32[8,32,128]{2,1,0:T(8,128)}), f32[8,32,128]{2,1,0:T(8,128)S(1)}, u32[]{:S(2)}, u32[]{:S(2)}) %all-to-all-start.2) | async-done | bytes 131104 | tf_op jit(solution)/shard_map/all_to_all | solution.py:450
  69.2 0.7 %update.1 = (f32[24,96]{1,0:T(8,128)}, f32[24,96]{1,0:T(8,128)}, f32[24,96]{1,0:T(8,128)}) custom-call(s32[1]{0:T(128)S(6)} %copy.14.step_ref, f32[8,32,128]{2,1,0:T(8,128)S(1)} %all-to-all-done.2.x_ref, f32[24,96]{1,0:T(8,128)S(1)} %bitcast.12), custom_call_target="tpu_custom_call" | custom-call | tf_op jit(solution)/shard_map/update/pallas_call | solution.py:394
  (9 shorter events, 0.0 us)
Async XLA Ops:
  3.0 6.0 %copy-start.2 = (bf16[2048,192]{0,1:T(8,128)(2,1)S(1)}, bf16[2048,192]{0,1:T(8,128)(2,1)}, u32[]{:S(2)}) copy-start(bf16[2048,192]{0,1:T(8,128)(2,1)} %param.13) | copy-start | bytes 2359300
  3.0 23.7 %all-to-all-start = ((bf16[16,352,128]{2,1,0:T(8,128)(2,1)}), bf16[16,352,128]{2,1,0:T(8,128)(2,1)S(1)}, u32[]{:S(2)}, u32[]{:S(2)}) async-start(bf16[16,352,128]{2,1,0:T(8,128)(2,1)} %pack.1), calls=%async_computation | async-start | bytes 2883584 | tf_op jit(solution)/shard_map/all_to_all | solution.py:435
  9.0 30.3 %collective-permute-start = (bf16[192,2048]{1,0:T(8,128)(2,1)S(1)}, bf16[192,2048]{1,0:T(8,128)(2,1)S(1)}, u32[]{:S(2)}, u32[]{:S(2)}) collective-permute-start(bf16[192,2048]{1,0:T(8,128)(2,1)S(1)} %bitcast.13), channel_id=1, source_target_pairs={{0,388},{1,389},{2,390},{3,391},{4,128},{5,129},{6,130},{7,131},{1... | collective-permute-start | bytes 2359304 | tf_op jit(solution)/shard_map/ppermute | solution.py:430
  16.4 22.9 %collective-permute-start.1 = (bf16[96,768]{1,0:T(8,128)(2,1)}, bf16[96,768]{1,0:T(8,128)(2,1)}, u32[]{:S(2)}, u32[]{:S(2)}) collective-permute-start(bf16[96,768]{1,0:T(8,128)(2,1)} %get-tuple-element.23), channel_id=1, source_target_pairs={{0,1},{1,0},{2,3},{3,2},{4,5},{5,4},{6,7},{7,6},{8,9},{9,8},{10,11... | collective-permute-start | bytes 442376 | tf_op jit(solution)/shard_map/ppermute | solution.py:439
  19.5 19.8 %collective-permute-start.2 = (bf16[96,768]{1,0:T(8,128)(2,1)}, bf16[96,768]{1,0:T(8,128)(2,1)}, u32[]{:S(2)}, u32[]{:S(2)}) collective-permute-start(bf16[96,768]{1,0:T(8,128)(2,1)} %get-tuple-element.24), channel_id=1, source_target_pairs={{0,2},{1,3},{2,0},{3,1},{4,6},{5,7},{6,4},{7,5},{8,10},{9,11},{10,... | collective-permute-start | bytes 442376 | tf_op jit(solution)/shard_map/ppermute | solution.py:439
  23.8 15.5 %collective-permute-start.3 = (bf16[96,768]{1,0:T(8,128)(2,1)}, bf16[96,768]{1,0:T(8,128)(2,1)}, u32[]{:S(2)}, u32[]{:S(2)}) collective-permute-start(bf16[96,768]{1,0:T(8,128)(2,1)} %get-tuple-element.25), channel_id=1, source_target_pairs={{0,3},{1,2},{2,1},{3,0},{4,7},{5,6},{6,5},{7,4},{8,11},{9,10},{10,... | collective-permute-start | bytes 442376 | tf_op jit(solution)/shard_map/ppermute | solution.py:439
  29.8 12.4 %copy-start.7 = (f32[1,3,3072]{2,0,1:T(1,128)S(1)}, f32[1,3,3072]{2,0,1:T(1,128)}, u32[]{:S(2)}) copy-start(f32[1,3,3072]{2,0,1:T(1,128)} %param.14) | copy-start | bytes 110596
  29.8 13.7 %copy-start.6 = (bf16[96,768]{1,0:T(8,128)(2,1)S(1)}, bf16[96,768]{1,0:T(8,128)(2,1)}, u32[]{:S(2)}) copy-start(bf16[96,768]{1,0:T(8,128)(2,1)} %get-tuple-element.28.refs_4_) | copy-start | bytes 442372
  29.8 22.2 %all-to-all-start.1 = ((bf16[8,2,384,128]{3,2,1,0:T(8,128)(2,1)}), bf16[8,2,384,128]{3,2,1,0:T(8,128)(2,1)S(1)}, u32[]{:S(2)}, u32[]{:S(2)}) async-start(bf16[8,2,384,128]{3,2,1,0:T(8,128)(2,1)} %attend.1), calls=%async_computation.1 | async-start | bytes 3145728 | tf_op jit(solution)/shard_map/all_to_all | solution.py:446
  34.3 7.9 %collective-permute-start.4 = (bf16[192,2048]{1,0:T(8,128)(2,1)S(1)}, bf16[192,2048]{1,0:T(8,128)(2,1)S(1)}, u32[]{:S(2)}, u32[]{:S(2)}) collective-permute-start(bf16[192,2048]{1,0:T(8,128)(2,1)S(1)} %bitcast.14), channel_id=1, source_target_pairs={{0,8},{8,0},{1,9},{9,1},{2,10},{10,2},{3,11},{11,3},{4,12},{12,4},... | collective-permute-start | bytes 2359304 | tf_op jit(solution)/shard_map/ppermute | solution.py:444
  39.4 4.2 %collective-permute-start.5 = (bf16[192,2048]{1,0:T(8,128)(2,1)S(1)}, bf16[192,2048]{1,0:T(8,128)(2,1)S(1)}, u32[]{:S(2)}, u32[]{:S(2)}) collective-permute-start(bf16[192,2048]{1,0:T(8,128)(2,1)S(1)} %collective-permute-done.refs_1_), channel_id=1, source_target_pairs={{0,8},{8,0},{1,9},{9,1},{2,10},{10,2},{3,11},{11,3},{4,12},{12,4},... | collective-permute-start | bytes 2359304 | tf_op jit(solution)/shard_map/ppermute | solution.py:444
  41.3 0.9 %copy-start.3 = (bf16[192,2048]{1,0:T(8,128)(2,1)}, bf16[192,2048]{1,0:T(8,128)(2,1)S(1)}, u32[]{:S(2)}) copy-start(bf16[192,2048]{1,0:T(8,128)(2,1)S(1)} %collective-permute-done.refs_1_) | copy-start | bytes 2359300
  43.5 1.1 %copy-start.4 = (bf16[192,2048]{1,0:T(8,128)(2,1)S(1)}, bf16[192,2048]{1,0:T(8,128)(2,1)}, u32[]{:S(2)}) copy-start(bf16[192,2048]{1,0:T(8,128)(2,1)} %copy-done.3) | copy-start | bytes 2359300
  44.7 1.0 %copy-start.5 = (bf16[3072,48]{0,1:T(8,128)(2,1)S(1)}, bf16[3072,48]{0,1:T(8,128)(2,1)}, u32[]{:S(2)}) copy-start(bf16[3072,48]{0,1:T(8,128)(2,1)} %param.15) | copy-start | bytes 884740
  47.4 1.6 %copy-start = (bf16[768,2048]{1,0:T(8,128)(2,1)}, bf16[768,2048]{1,0:T(8,128)(2,1)S(1)}, u32[]{:S(2)}) copy-start(bf16[768,2048]{1,0:T(8,128)(2,1)S(1)} %get-tuple-element.33.w_hbm) | copy-start | bytes 9437188
  52.0 17.2 %copy-start.1 = (f32[96,24]{0,1:T(8,128)S(1)}, f32[96,24]{0,1:T(8,128)}, u32[]{:S(2)}) copy-start(f32[96,24]{0,1:T(8,128)} %param.16) | copy-start | bytes 27652
  57.0 12.2 %all-to-all-start.2 = ((f32[8,32,128]{2,1,0:T(8,128)}), f32[8,32,128]{2,1,0:T(8,128)S(1)}, u32[]{:S(2)}, u32[]{:S(2)}) async-start(f32[8,32,128]{2,1,0:T(8,128)} %project.1), calls=%async_computation.2 | async-start | bytes 262144 | tf_op jit(solution)/shard_map/all_to_all | solution.py:450
